TPU v7x, 256 devices: a whole 4x4x8 slice. The times are simulated.
256 devices in a mesh: node: 16 (over x, y), local: 16 (over z, core).
Axes of the slice: x: 4, y: 4, z: 8, core: 2. Of those that a mesh axis runs over, the one named last changes fastest.
Arguments:
- pooled: bfloat16 [131072, 512], P(('node', 'local')), may hold values from -6 to 6
- lookups: int32 [131072, 4], P(('node', 'local')), may hold values from 0 to 16895, as said below
- converted: int32 [131072], P(('node', 'local')), may hold values 0 or 1
- w_hidden: bfloat16 [512, 2048], replicated, may hold values from -0.25 to 0.25
- w_out: bfloat16 [2048], replicated, may hold values from -0.125 to 0.125
- hot_accum: float32 [4, 512, 128], replicated, may hold values from 0.01 to 1
- cold_accum: float32 [4, 16384, 128], P(None, ('node', 'local')), may hold values from 1e-05 to 0.01
Outputs:
- w1_grad: bfloat16 [512, 2048], replicated
- hot_step: float32 [4, 512, 128], replicated
- cold_step: float32 [4, 16384, 128], P(None, ('node', 'local'))
Inputs may be any that keep to these rules, and one draw needn't show every extreme that they name: `lookups`: each entry below 512 names a hot row of its table; an entry 512 + c names cold row c of its table, held by device c // 64 (device index node * 16 + local). Among the 512 samples of one device, at most 8 entries over all tables name cold rows of one owner; in every draw some owner receives exactly 8 from every device.
All inputs are finite; a program needn't handle non-finite values. No bound on the sum of `converted` on one device may be relied on, other than what follows from the above.
Results may differ from a plain program's by a relative error of at most 0.0066.
Values may be sent and summed in bfloat16 or wider, within the bound.
No kernel may reach another device: no remote copies, remote signals or barrier semaphores. Data moves between devices by JAX's collectives and lax.ppermute only.
A program may use at most 64 MiB of HBM per device.

v0:
```python
import math

import jax
import jax.numpy as jnp
from jax import lax
from jax.sharding import PartitionSpec as P

CAP = 8


def silu_grad(values):
    sig = jax.nn.sigmoid(values)
    return sig * (1.0 + values * (1.0 - sig))


def adagrad_step(total, accum):
    return total / jnp.sqrt(accum + total * total)


def slot_ranks(owner_key, owners, block_len):
    block_count = owner_key.shape[0] // block_len
    keyed = owner_key.reshape(block_count, block_len)
    lower = (
        jnp.arange(block_len, dtype=jnp.int32)[:, None]
        > jnp.arange(block_len, dtype=jnp.int32)[None, :]
    ).astype(jnp.bfloat16)
    owner_range = jnp.arange(owners, dtype=jnp.int32)

    def slot_one_block(carry, block_keys):
        member = block_keys[:, None] == owner_range[None, :]
        member_b = member.astype(jnp.bfloat16)
        before = jnp.dot(lower, member_b, preferred_element_type=jnp.float32) + carry[None, :]
        rank = jnp.sum(jnp.where(member, before, 0.0), axis=1)
        return (carry + jnp.sum(member.astype(jnp.float32), axis=0), rank)

    start = jnp.zeros((owners,), jnp.float32)
    unused, ranks = lax.scan(slot_one_block, start, keyed)
    return ranks.reshape(-1).astype(jnp.int32)


def pack_slots(slot_index, values, slot_count, block_len, exact):
    block_count = slot_index.shape[0] // block_len
    slot_blocks = slot_index.reshape(block_count, block_len)
    value_blocks = values.reshape((block_count, block_len) + values.shape[1:])
    slot_range = jnp.arange(slot_count, dtype=jnp.int32)

    def pack_one_block(total, piece):
        slots, rows = piece
        member = slots[:, None] == slot_range[None, :]
        if exact:
            term = lax.dot_general(
                member.astype(jnp.float32),
                rows,
                (((0,), (0,)), ((), ())),
                precision=lax.Precision.HIGHEST,
                preferred_element_type=jnp.float32,
            )
        else:
            term = lax.dot_general(
                member.astype(jnp.bfloat16),
                rows,
                (((0,), (0,)), ((), ())),
                preferred_element_type=jnp.float32,
            )
        return (total + term, None)

    start = jnp.zeros((slot_count,) + values.shape[1:], jnp.float32)
    total, unused = lax.scan(pack_one_block, start, (slot_blocks, value_blocks))
    return total


def on_device(pooled, lookups, converted, w_hidden, w_out, hot_accum, cold_accum):
    tok_rows, tables = lookups.shape
    hot_rows = hot_accum.shape[1]
    cold_rows = cold_accum.shape[1]
    emb_width = hot_accum.shape[2]
    node_count = lax.axis_size("node")
    local_count = lax.axis_size("local")
    owners = node_count * local_count
    slot_count = owners * CAP
    flat_ids = lookups.reshape(-1)
    lookup_count = flat_ids.shape[0]
    block_len = math.gcd(lookup_count, 512)
    position = jnp.arange(lookup_count, dtype=jnp.int32)
    is_cold = flat_ids >= hot_rows
    offset = jnp.where(is_cold, flat_ids - hot_rows, 0)
    owner_ids = offset // cold_rows
    target = position % tables * cold_rows + offset % cold_rows
    owner_key = jnp.where(is_cold, owner_ids, owners)
    ranks = slot_ranks(owner_key, owners, block_len)
    slot_index = jnp.where(is_cold, owner_key * CAP + ranks, slot_count)
    slot_target = pack_slots(slot_index, target.astype(jnp.float32), slot_count, block_len, True)
    slot_rows = slot_target.astype(jnp.int32)
    arrived_rows = lax.all_to_all(
        lax.all_to_all(
            slot_rows.reshape(node_count, local_count, CAP),
            "node",
            split_axis=0,
            concat_axis=0,
            tiled=True,
        ),
        "local",
        split_axis=1,
        concat_axis=1,
        tiled=True,
    )
    pre_act = jnp.dot(pooled, w_hidden, preferred_element_type=jnp.float32)
    hidden = jax.nn.silu(pre_act).astype(jnp.bfloat16)
    logit = jnp.dot(hidden, w_out, preferred_element_type=jnp.float32)
    chance = jax.nn.sigmoid(logit)
    target_value = converted.astype(jnp.float32)
    loss_weight = target_value * (1.0 + chance) + (1.0 - target_value) * (1.0 - chance) * (
        1.0 + chance
    )
    logit_grad = loss_weight * (chance - target_value)
    pre_grad = (
        logit_grad[:, None] * w_out.astype(jnp.float32)[None, :] * silu_grad(pre_act)
    ).astype(jnp.bfloat16)
    input_grad = lax.dot_general(
        pre_grad, w_hidden, (((1,), (1,)), ((), ())), preferred_element_type=jnp.float32
    ).astype(jnp.bfloat16)
    grad_rows = input_grad.reshape(lookup_count, emb_width)
    buffer = pack_slots(slot_index, grad_rows, slot_count, block_len, False).astype(jnp.bfloat16)
    arrived = lax.all_to_all(
        lax.all_to_all(
            buffer.reshape(node_count, local_count, CAP, emb_width),
            "node",
            split_axis=0,
            concat_axis=0,
            tiled=True,
        ),
        "local",
        split_axis=1,
        concat_axis=1,
        tiled=True,
    )
    weight_term = lax.dot_general(
        pooled, pre_grad, (((0,), (0,)), ((), ())), preferred_element_type=jnp.float32
    )
    hot_onehot = (
        lookups[:, :, None] == jnp.arange(hot_rows, dtype=jnp.int32)[None, None, :]
    ).astype(jnp.bfloat16)
    grads3 = input_grad.reshape(tok_rows, tables, emb_width)
    hot_term = jnp.einsum("bth,bte->the", hot_onehot, grads3, preferred_element_type=jnp.float32)
    w1_sum, hot_sum = lax.psum((weight_term, hot_term), ("node", "local"))
    w1_grad = w1_sum.astype(jnp.bfloat16)
    hot_step = adagrad_step(hot_sum, hot_accum)
    cold_onehot = (
        arrived_rows.reshape(-1)[:, None]
        == jnp.arange(tables * cold_rows, dtype=jnp.int32)[None, :]
    ).astype(jnp.bfloat16)
    cold_flat = lax.dot_general(
        cold_onehot,
        arrived.reshape(-1, emb_width),
        (((0,), (0,)), ((), ())),
        preferred_element_type=jnp.float32,
    )
    cold_sum = cold_flat.reshape(tables, cold_rows, emb_width)
    cold_step = adagrad_step(cold_sum, cold_accum)
    return (w1_grad, hot_step, cold_step)


def solution(mesh):
    in_specs = (
        P(("node", "local"), None),
        P(("node", "local"), None),
        P(("node", "local")),
        P(),
        P(),
        P(),
        P(None, ("node", "local"), None),
    )
    out_specs = (P(), P(), P(None, ("node", "local"), None))
    return jax.shard_map(
        on_device, mesh=mesh, in_specs=in_specs, out_specs=out_specs, check_vma=False
    )
```

profile of v0, /device:TPU:1, one launch (start us, length us, event | category | flops | bytes accessed | tf_op | source)
XLA Modules:
  0.0 339.7 jit_solution(234674365716563491)
XLA Ops:
  7.2 0.9 broadcast_compare_fusion.1
  8.0 0.7 broadcast_add_fusion
  8.7 0.2 copy.29
  8.9 0.2 ge.10
  9.1 0.1 copy.30
  9.3 0.2 sub.28
  9.5 2.4 while.35
  9.5 0.1 fusion.63
  9.7 0.4 fusion.65
  10.1 0.1 dynamic_update_slice.6
  10.1 0.1 fusion.63
  10.3 0.4 fusion.65
  10.6 0.1 dynamic_update_slice.6
  10.7 0.1 fusion.63
  10.9 0.4 fusion.65
  11.2 0.1 dynamic_update_slice.6
  11.3 0.1 fusion.63
  11.5 0.4 fusion.65
  11.8 0.1 dynamic_update_slice.6
  11.9 6.0 %while.36 = (s32[]{:T(128)}, f32[2048]{0:T(1024)S(1)}, s32[4,512]{1,0:T(4,128)S(1)}, f32[4,512]{1,0:T(4,128)S(1)}, s32[]{:T(128)}, /*index=5*/s32[]{:T(128)}) while((s32[]{:T(128)}, f32[2048]{0:T(1024)S(1)}, s32[4,512]{1,0:T(4,128)S(1)}, f32[4,512]{1,0:T(4,128)S(1)}, s32[]{:T(128)}, /*index=5*/s32[]{:T(128)}) %tuple.74), condition=%wide.region_7.8_spmd.clone, body=%wide.region_6.7_spmd.clone.sunk | while | flops 13635587 | bytes 41055 | solution.py:68
  12.0 1.5 fusion.67
  13.5 1.5 fusion.67
  15.0 1.5 fusion.67
  16.4 1.5 fusion.67
  17.9 0.1 reshape.66
  18.0 0.1 copy.31
  18.1 0.7 reshape.74
  18.8 7.6 %all-to-all-start = ((s32[16,1,128]{2,1,0:T(1,128)}), s32[16,1,128]{2,1,0:T(1,128)S(1)}, u32[]{:S(2)}, u32[]{:S(2)}) async-start(s32[16,1,128]{2,1,0:T(1,128)} %reshape.74), calls=%async_computation | async-start | bytes 16384 | tf_op jit(solution)/shard_map/all_to_all | solution.py:95
  26.5 1.3 fusion.44
  27.8 1.2 fusion.31
  29.0 2.0 multiply_convert_fusion
  31.0 1.3 copy-done.1
  32.3 2.2 convolution_convert_fusion
  34.5 1.3 copy.34
  35.8 1.1 reshape_reshape.3
  36.9 14.2 %while.37 = (s32[]{:T(128)}, f32[2048,128]{1,0:T(8,128)}, s32[4,512]{1,0:T(4,128)S(1)}, bf16[4,512,128]{2,1,0:T(8,128)(2,1)}, s32[]{:T(128)}, /*index=5*/s32[]{:T(128)}) while((s32[]{:T(128)}, f32[2048,128]{1,0:T(8,128)}, s32[4,512]{1,0:T(4,128)S(1)}, bf16[4,512,128]{2,1,0:T(8,128)(2,1)}, s32[]{:T(128)}, ...), condition=%wide.region_9.10_spmd.clone, body=%wide.region_8.9_spmd.clone.sunk | while | flops 270008320 | bytes 2234463 | solution.py:68
  36.9 3.2 fusion.69
  40.1 3.6 %fusion.69 = f32[2048,128]{1,0:T(8,128)} fusion(s32[512]{0:T(512)S(1)} %bitcast.65, f32[2048,128]{1,0:T(8,128)} %get-tuple-element.289, pred[]{:T(512)S(6)} %compare.19, bf16[4,512,128]{2,1,0:T(8,128)(2,1)} %get-tuple-element.297, s32[]{:T(128)S(6)} %copy.53), kind=kOutput, calls=%fused_computation.26.clone.1 | convolution fusion | flops 270008320 | bytes 2230277 | tf_op jit(solution)/shard_map/while/body/eval_jaxpr/dot_general | solution.py:59
  43.8 3.6 %fusion.69 = f32[2048,128]{1,0:T(8,128)} fusion(s32[512]{0:T(512)S(1)} %bitcast.65, f32[2048,128]{1,0:T(8,128)} %get-tuple-element.289, pred[]{:T(512)S(6)} %compare.19, bf16[4,512,128]{2,1,0:T(8,128)(2,1)} %get-tuple-element.297, s32[]{:T(128)S(6)} %copy.53), kind=kOutput, calls=%fused_computation.26.clone.1 | convolution fusion | flops 270008320 | bytes 2230277 | tf_op jit(solution)/shard_map/while/body/eval_jaxpr/dot_general | solution.py:59
  47.4 3.6 %fusion.69 = f32[2048,128]{1,0:T(8,128)} fusion(s32[512]{0:T(512)S(1)} %bitcast.65, f32[2048,128]{1,0:T(8,128)} %get-tuple-element.289, pred[]{:T(512)S(6)} %compare.19, bf16[4,512,128]{2,1,0:T(8,128)(2,1)} %get-tuple-element.297, s32[]{:T(128)S(6)} %copy.53), kind=kOutput, calls=%fused_computation.26.clone.1 | convolution fusion | flops 270008320 | bytes 2230277 | tf_op jit(solution)/shard_map/while/body/eval_jaxpr/dot_general | solution.py:59
  51.0 2.1 convert_element_type.53
  53.1 6.7 %all-to-all-start.2 = ((bf16[16,16,8,128]{3,2,1,0:T(8,128)(2,1)}), bf16[16,16,8,128]{3,2,1,0:T(8,128)(2,1)S(1)}, u32[]{:S(2)}, u32[]{:S(2)}) async-start(bf16[16,16,8,128]{3,2,1,0:T(8,128)(2,1)} %bitcast.3), calls=%async_computation.2 | async-start | bytes 1048576 | tf_op jit(solution)/shard_map/all_to_all | solution.py:125
  59.8 2.8 fusion.27
  62.6 0.6 broadcast.124
  63.2 0.7 reduce
  64.0 0.1 reshape.75
  64.0 0.1 copy.32
  64.1 0.7 reshape.76
  64.8 3.9 %all-to-all-done.2 = bf16[16,16,8,128]{3,2,1,0:T(8,128)(2,1)S(1)} async-done(((bf16[16,16,8,128]{3,2,1,0:T(8,128)(2,1)}), bf16[16,16,8,128]{3,2,1,0:T(8,128)(2,1)S(1)}, u32[]{:S(2)}, u32[]{:S(2)}) %all-to-all-start.2) | async-done | bytes 524320 | tf_op jit(solution)/shard_map/all_to_all | solution.py:125
  68.7 12.0 %all-to-all-start.1 = ((s32[16,1,128]{2,1,0:T(1,128)}), s32[16,1,128]{2,1,0:T(1,128)S(1)}, u32[]{:S(2)}, u32[]{:S(2)}) async-start(s32[16,1,128]{2,1,0:T(1,128)} %reshape.76), calls=%async_computation.1 | async-start | bytes 16384 | tf_op jit(solution)/shard_map/all_to_all | solution.py:94
  80.7 4.9 %convolution_bitcast_fusion = f32[512,2048]{0,1:T(8,128)} fusion(bf16[512,2048]{1,0:T(8,128)(2,1)} %copy-done.1, bf16[512,512]{1,0:T(8,128)(2,1)S(1)} %copy-done.2), kind=kOutput, calls=%fused_computation.37 | convolution fusion | flops 1073741824 | bytes 6815744 | tf_op jit(solution)/shard_map/dot_general | solution.py:137
  85.6 0.9 copy.35
  86.5 1.2 all-to-all-done.1
  87.7 6.0 %all-to-all-start.3 = ((bf16[16,16,8,128]{3,2,0,1:T(8,128)(2,1)}), bf16[16,16,8,128]{3,2,0,1:T(8,128)(2,1)S(1)}, u32[]{:S(2)}, u32[]{:S(2)}) async-start(bf16[16,16,8,128]{3,2,0,1:T(8,128)(2,1)} %copy.35), calls=%async_computation.3 | async-start | bytes 1048576 | tf_op jit(solution)/shard_map/all_to_all | solution.py:124
  93.7 128.7 %all-reduce.4 = bf16[512,2048]{0,1:T(8,128)(2,1)} all-reduce(f32[512,2048]{0,1:T(8,128)} %convolution_bitcast_fusion), channel_id=1, replica_groups=mesh['node'=16,'local'=16] {'node','local'}, use_global_device_ids=true, to_apply=%region_0.1 | all-reduce | flops 1048576 | bytes 6291456 | tf_op jit(solution)/shard_map/psum | solution.py:145
  222.4 3.9 %copy.37 = bf16[512,2048]{1,0:T(8,128)(2,1)} copy(bf16[512,2048]{0,1:T(8,128)(2,1)} %all-reduce.4) | data formatting | bytes 4194304
  226.4 0.7 reduce.1
  227.1 0.1 reshape.77
  227.2 0.1 copy.33
  227.3 0.1 eq.95
  227.4 101.5 %all-reduce.3.cloned.1.call-done = f32[4,512,128]{2,1,0:T(8,128)} async-done(((f32[4,512,128]{2,1,0:T(8,128)}), f32[4,512,128]{2,1,0:T(8,128)}) %all-reduce.3.cloned.1.call-update) | async-done | bytes 1048592 | tf_op jit(solution)/shard_map/psum | solution.py:145
  328.9 2.7 rsqrt_multiply_fusion
  331.6 0.1 copy.36
  331.7 1.2 rsqrt_multiply_fusion.1
  (48 shorter events, 0.3 us)
Async XLA Ops:
  7.2 19.3 %copy-start = (bf16[512,2048]{1,0:T(8,128)(2,1)S(1)}, bf16[512,2048]{1,0:T(8,128)(2,1)}, u32[]{:S(2)}) copy-start(bf16[512,2048]{1,0:T(8,128)(2,1)} %param.16) | copy-start | bytes 6291460
  11.9 14.5 %copy-start.4 = (bf16[2048]{0:T(1024)(128)(2,1)S(1)}, bf16[2048]{0:T(1024)(128)(2,1)}, u32[]{:S(2)}) copy-start(bf16[2048]{0:T(1024)(128)(2,1)} %param.17) | copy-start | bytes 12292
  11.9 14.6 %copy-start.2 = (bf16[512,512]{1,0:T(8,128)(2,1)S(1)}, bf16[512,512]{1,0:T(8,128)(2,1)}, u32[]{:S(2)}) copy-start(bf16[512,512]{1,0:T(8,128)(2,1)} %param.13) | copy-start | bytes 1572868
  18.8 34.3 %all-to-all-start = ((s32[16,1,128]{2,1,0:T(1,128)}), s32[16,1,128]{2,1,0:T(1,128)S(1)}, u32[]{:S(2)}, u32[]{:S(2)}) async-start(s32[16,1,128]{2,1,0:T(1,128)} %reshape.74), calls=%async_computation | async-start | bytes 16384 | tf_op jit(solution)/shard_map/all_to_all | solution.py:95
  27.8 1.2 copy-start.5
  31.0 1.3 copy-start.1
  36.9 23.0 %copy-start.3 = (s32[512,4]{0,1:T(4,128)S(1)}, s32[512,4]{0,1:T(4,128)}, u32[]{:S(2)}) copy-start(s32[512,4]{0,1:T(4,128)} %param.14) | copy-start | bytes 24580
  53.1 15.6 %all-to-all-start.2 = ((bf16[16,16,8,128]{3,2,1,0:T(8,128)(2,1)}), bf16[16,16,8,128]{3,2,1,0:T(8,128)(2,1)S(1)}, u32[]{:S(2)}, u32[]{:S(2)}) async-start(bf16[16,16,8,128]{3,2,1,0:T(8,128)(2,1)} %bitcast.3), calls=%async_computation.2 | async-start | bytes 1048576 | tf_op jit(solution)/shard_map/all_to_all | solution.py:125
  59.8 269.1 %all-reduce.3.cloned.1.call-start = ((), (), s32[]{:S(2)}) async-start(), calls=%async_computation.4 | async-start | bytes 2097152 | tf_op jit(solution)/shard_map/psum | solution.py:145
  68.7 18.9 %all-to-all-start.1 = ((s32[16,1,128]{2,1,0:T(1,128)}), s32[16,1,128]{2,1,0:T(1,128)S(1)}, u32[]{:S(2)}, u32[]{:S(2)}) async-start(s32[16,1,128]{2,1,0:T(1,128)} %reshape.76), calls=%async_computation.1 | async-start | bytes 16384 | tf_op jit(solution)/shard_map/all_to_all | solution.py:94
  87.7 243.9 %all-to-all-start.3 = ((bf16[16,16,8,128]{3,2,0,1:T(8,128)(2,1)}), bf16[16,16,8,128]{3,2,0,1:T(8,128)(2,1)S(1)}, u32[]{:S(2)}, u32[]{:S(2)}) async-start(bf16[16,16,8,128]{3,2,0,1:T(8,128)(2,1)} %copy.35), calls=%async_computation.3 | async-start | bytes 1048576 | tf_op jit(solution)/shard_map/all_to_all | solution.py:124
  222.4 109.3 %copy-start.6 = (f32[4,64,128]{2,1,0:T(8,128)S(1)}, f32[4,64,128]{2,1,0:T(8,128)}, u32[]{:S(2)}) copy-start(f32[4,64,128]{2,1,0:T(8,128)} %param.19) | copy-start | bytes 393220
Sparse Core Ops, SparseCore 0:
  66.6 262.2 all-reduce.2
where the time goes:
time: 341 us; the launch traced here: 340 us
  blocking collectives  129 us (38%)
  waiting for transfers between devices  107 us (31%)
  matrix products  34.9 us (10%)
  starting transfers between devices  32.3 us (9%)
  between operations  14.3 us (4%)
  local copies, waits for them, and re-layouts  12.4 us (4%)
  other arithmetic  10.4 us (3%)
    psum x1, blocking collectives, on_device(): w1_sum, hot_sum = lax.psum((weight_term, hot_term), ('node', 'local'))  129 us
    psum x1, waiting for transfers between devices, on_device(): w1_sum, hot_sum = lax.psum((weight_term, hot_term), ('node', 'local'))  101 us
    dot_general x4, matrix products, pack_one_block(): lax.dot_general(member.astype(jnp.bfloat16), rows, (((0,), (0,)), ((), ()...  14.2 us
    all_to_all x1, starting transfers between devices, on_device(): lax.all_to_all(lax.all_to_all(slot_rows.reshape(node_count, local_count,...  12 us
    all_to_all x1, starting transfers between devices, on_device(): lax.all_to_all(slot_rows.reshape(node_count, local_count, CAP), 'node', s...  7.59 us
    unnamed x20, local copies, waits for them, and re-layouts  6.86 us
  transfers between devices with their start and end apart: 5, of which 3 were waited for; matrix products, arithmetic and copies ran while one was open for 13% of the time, Pallas kernels for 0%

commit v1 on v0

v1 whole, which is shorter than its diff:
```python
import functools

import jax
import jax.numpy as jnp
from jax import lax
from jax.experimental import pallas as pl
from jax.experimental.pallas import tpu as pltpu
from jax.sharding import PartitionSpec as P

CAP = 8
E = 128
HID = 2048
FEAT = 512
TOK = 512
TABLES = 4
HOT = 512
COLD_DEV = 64
NODES = 16
LOCALS = 16
ZS = 8
OWNERS = NODES * LOCALS
HALF = FEAT // 2
WIDE = HID + 512
CHUNK = HALF // NODES
ZCOL = HID // ZS
ZWIDE = ZCOL + E
SLOTS = LOCALS * CAP
SLAB = SLOTS + 16
BF = jnp.bfloat16
F32 = jnp.float32
LIMIT = pltpu.CompilerParams(vmem_limit_bytes=56 * 1024 * 1024)


def dot(a, b):
    return jnp.dot(a, b, preferred_element_type=F32)


def dot_nt(a, b):
    return lax.dot_general(a, b, (((1,), (1,)), ((), ())), preferred_element_type=F32)


def wide(tile, copies):
    return jnp.concatenate([tile] * copies, axis=1)


def backprop_kernel(core_ref, x_ref, ids_ref, y_ref, wh_ref, wo_ref, send_ref, own_ref, grad_ref, slope_ref, pre_ref, xt_ref):
    core = core_ref[0]
    step = 256
    x = x_ref[...]
    logit = jnp.zeros((TOK, E), F32)
    for j in range(HID // step):
        cols = slice(j * step, (j + 1) * step)
        v = dot(x, wh_ref[:, cols])
        s = jax.nn.sigmoid(v)
        h = v * s
        slope_ref[:, cols] = s + h * (1.0 - s)
        out_row = jnp.broadcast_to(wo_ref[:, cols], (E, step))
        logit = logit + dot_nt(h.astype(BF), out_row)
    xt_ref[...] = x.T
    chance = jax.nn.sigmoid(logit)
    y = jnp.broadcast_to(y_ref[...].astype(F32), (E, TOK)).T
    weight = y * (1.0 + chance) + (1.0 - y) * (1.0 - chance) * (1.0 + chance)
    lg = wide(weight * (chance - y), step // E)
    own_rows = pl.ds(pl.multiple_of(core * HALF, HALF), HALF)
    far_rows = pl.ds(pl.multiple_of((1 - core) * HALF, HALF), HALF)
    for j in range(HID // step):
        cols = slice(j * step, (j + 1) * step)
        out_row = wo_ref[:, cols].astype(F32)
        pre = (lg * out_row * slope_ref[:, cols]).astype(BF)
        pre_ref[:, cols] = pre
        send_ref[:, cols] = dot(xt_ref[far_rows, :], pre).astype(BF)
        own_ref[:, cols] = dot(xt_ref[own_rows, :], pre).astype(BF)
    grad_ref[...] = dot_nt(pre_ref[...], wh_ref[...]).astype(BF)
    hot_iota = lax.broadcasted_iota(jnp.int32, (HOT, TOK), 0)
    for side, out_ref in ((1 - core, send_ref), (core, own_ref)):
        for t in range(2):
            table = side * 2 + t
            hit = ids_ref[pl.ds(table, 1), :] == hot_iota
            onehot = jnp.where(hit, 1.0, 0.0).astype(BF)
            grads = grad_ref[:, pl.ds(pl.multiple_of(table * E, E), E)]
            total = dot(onehot, grads).astype(BF)
            at = HID + 2 * t * E
            out_ref[:, at:at + E] = total[:HALF]
            out_ref[:, at + E:at + 2 * E] = total[HALF:]


def backprop(core, x, ids, y, wh, wo):
    vmem = pl.BlockSpec(memory_space=pltpu.VMEM)
    half = jax.ShapeDtypeStruct((HALF, WIDE), BF)
    return pl.pallas_call(
        backprop_kernel,
        out_shape=(half, half, jax.ShapeDtypeStruct((TOK, FEAT), BF)),
        in_specs=[pl.BlockSpec(memory_space=pltpu.SMEM)] + [vmem] * 5,
        out_specs=(vmem, vmem, vmem),
        scratch_shapes=[
            pltpu.VMEM((TOK, HID), F32),
            pltpu.VMEM((TOK, HID), BF),
            pltpu.VMEM((FEAT, TOK), BF),
        ],
        compiler_params=LIMIT,
    )(core, x, ids, y, wh, wo)


def pack_kernel(ids_ref, grad_ref, out_ref, rows_ref):
    owner_iota = lax.broadcasted_iota(jnp.int32, (OWNERS, TOK), 0)
    earlier = lax.broadcasted_iota(jnp.int32, (TOK, TOK), 0) < lax.broadcasted_iota(jnp.int32, (TOK, TOK), 1)
    earlier = jnp.where(earlier, 1.0, 0.0).astype(BF)
    carry = jnp.zeros((OWNERS, 1), F32)
    slots, names = [], []
    for t in range(TABLES):
        ids = ids_ref[t:t + 1, :]
        cold = ids >= HOT
        offset = jnp.where(cold, ids - HOT, 0)
        owner = jnp.where(cold, offset >> 6, -1)
        member = jnp.where(owner == owner_iota, 1.0, 0.0)
        before = dot(member.astype(BF), earlier) + carry
        rank = jnp.sum(member * before, axis=0, keepdims=True).astype(jnp.int32)
        carry = carry + jnp.sum(member, axis=1, keepdims=True)
        slot = ((owner & (LOCALS - 1)) * NODES + (owner >> 4)) * CAP + rank
        slots.append(jnp.where(cold, slot, -1))
        names.append((offset & (COLD_DEV - 1)) + t * COLD_DEV)
        rows_ref[t * TOK:(t + 1) * TOK, :] = grad_ref[:, t * E:(t + 1) * E]
    slot_col = jnp.concatenate(slots + slots, axis=0).astype(F32).T.astype(jnp.int32)
    lane = lax.broadcasted_iota(jnp.int32, (TOK, SLOTS), 1)
    group = lax.broadcasted_iota(jnp.int32, (LOCALS, TOK), 0)
    labels = jnp.zeros((LOCALS, SLOTS), F32)
    for t in range(TABLES):
        low = jnp.where((slot_col[:, t:t + 1] & (SLOTS - 1)) == lane, 1.0, 0.0).astype(BF)
        high = jnp.where((slots[t] >> 7) == group, names[t].astype(F32), 0.0).astype(BF)
        labels = labels + dot(high, low)
    labels = labels.astype(BF)
    flat = jnp.concatenate(slots, axis=1)
    block = 512
    per = block // SLOTS
    iota = lax.broadcasted_iota(jnp.int32, (block, TABLES * TOK), 0)
    for b in range(LOCALS // per):
        member = jnp.where(flat - b * block == iota, 1.0, 0.0).astype(BF)
        packed = dot(member, rows_ref[...]).astype(BF)
        for q in range(per):
            out_ref[b * per + q, :SLOTS, :] = packed[q * SLOTS:(q + 1) * SLOTS]
            out_ref[b * per + q, SLOTS:, :] = labels


def pack(ids, grads):
    vmem = pl.BlockSpec(memory_space=pltpu.VMEM)
    return pl.pallas_call(
        pack_kernel,
        out_shape=jax.ShapeDtypeStruct((LOCALS, SLAB, E), BF),
        in_specs=[vmem] * 2,
        out_specs=vmem,
        scratch_shapes=[pltpu.VMEM((TABLES * TOK, E), BF)],
        compiler_params=LIMIT,
    )(ids, grads)


def add_kernel(a_ref, b_ref, out_ref):
    out_ref[...] = (a_ref[...].astype(F32) + b_ref[...].astype(F32)).astype(BF)


def add_halves(a, b):
    vmem = pl.BlockSpec(memory_space=pltpu.VMEM)
    return pl.pallas_call(
        add_kernel,
        out_shape=jax.ShapeDtypeStruct(a.shape, BF),
        in_specs=[vmem] * 2,
        out_specs=vmem,
        compiler_params=LIMIT,
    )(a, b)


def node_sum_kernel(in_ref, out_ref):
    total = in_ref[0].astype(F32)
    for n in range(1, NODES):
        total = total + in_ref[n].astype(F32)
    for z in range(ZS):
        out_ref[z, :, :ZCOL] = total[:, z * ZCOL:(z + 1) * ZCOL].astype(BF)
        at = HID + (z // 2) * E
        row = (z % 2) * 8
        hot = total[row:row + 8, at:at + E]
        hot = jnp.concatenate([hot, jnp.zeros_like(hot)], axis=0)
        out_ref[z, :, ZCOL:] = hot.astype(BF)


def node_sum(parts):
    vmem = pl.BlockSpec(memory_space=pltpu.VMEM)
    return pl.pallas_call(
        node_sum_kernel,
        out_shape=jax.ShapeDtypeStruct((ZS, CHUNK, ZWIDE), BF),
        in_specs=[vmem],
        out_specs=vmem,
        compiler_params=LIMIT,
    )(parts)


def z_sum_kernel(at_ref, in_ref, accum_ref, out_ref):
    total = in_ref[0].astype(F32)
    for z in range(1, ZS):
        total = total + in_ref[z].astype(F32)
    hot = total[:8, ZCOL:]
    stepped = hot / jnp.sqrt(accum_ref[...] + hot * hot)
    stepped = jnp.concatenate([stepped, jnp.zeros_like(stepped)], axis=0)
    done = jnp.concatenate([total[:, :ZCOL], stepped], axis=1).astype(BF)
    for z in range(ZS):
        out_ref[z] = done


def z_sum(block, parts, accum):
    return pl.pallas_call(
        z_sum_kernel,
        out_shape=jax.ShapeDtypeStruct((ZS, CHUNK, ZWIDE), BF),
        grid_spec=pltpu.PrefetchScalarGridSpec(
            num_scalar_prefetch=1,
            grid=(1,),
            in_specs=[
                pl.BlockSpec((ZS, CHUNK, ZWIDE), lambda i, at: (0, 0, 0)),
                pl.BlockSpec((8, E), lambda i, at: (at[0], 0)),
            ],
            out_specs=pl.BlockSpec((ZS, CHUNK, ZWIDE), lambda i, at: (0, 0, 0)),
        ),
        compiler_params=LIMIT,
    )(block, parts, accum)


def spread_kernel(in_ref, out_ref):
    parts = [in_ref[z] for z in range(ZS)]
    pieces = [part[:, :ZCOL] for part in parts]
    for k in range(4):
        pair = [parts[2 * k + q][:, ZCOL:].astype(F32)[:8] for q in range(2)]
        pieces.append(jnp.concatenate(pair, axis=0).astype(BF))
    row = jnp.concatenate(pieces, axis=1)
    for n in range(NODES):
        out_ref[n] = row


def spread(parts):
    vmem = pl.BlockSpec(memory_space=pltpu.VMEM)
    return pl.pallas_call(
        spread_kernel,
        out_shape=jax.ShapeDtypeStruct((NODES, CHUNK, WIDE), BF),
        in_specs=[vmem],
        out_specs=vmem,
        compiler_params=LIMIT,
    )(parts)


def finish_kernel(core_ref, own_ref, far_ref, w1_ref, hot_ref):
    core = core_ref[0]
    for side, in_ref in ((core, own_ref), (1 - core, far_ref)):
        w1_ref[pl.ds(pl.multiple_of(side * HALF, HALF), HALF), :] = in_ref[:, :HID]
        for k in range(4):
            row = pl.multiple_of(side * 1024 + k * HALF, HALF)
            hot_ref[pl.ds(row, HALF), :] = in_ref[:, HID + k * E:HID + (k + 1) * E].astype(F32)


def finish(core, own, far):
    vmem = pl.BlockSpec(memory_space=pltpu.VMEM)
    return pl.pallas_call(
        finish_kernel,
        out_shape=(
            jax.ShapeDtypeStruct((FEAT, HID), BF),
            jax.ShapeDtypeStruct((TABLES * HOT, E), F32),
        ),
        in_specs=[pl.BlockSpec(memory_space=pltpu.SMEM), vmem, vmem],
        out_specs=(vmem, vmem),
        compiler_params=LIMIT,
    )(core, own, far)


def cold_kernel(node_ref, in_ref, accum_ref, out_ref):
    node = node_ref[0]
    labels = jnp.concatenate([in_ref[n, SLOTS:, :] for n in range(NODES)], axis=0)
    lane = lax.broadcasted_iota(jnp.int32, (SLOTS, SLOTS), 0)
    place = lax.broadcasted_iota(jnp.int32, (SLOTS, SLOTS), 1)
    pick = jnp.where(lane == node * CAP + (place & (CAP - 1)), 1.0, 0.0).astype(BF)
    moved = dot(labels, pick)
    keep = lax.broadcasted_iota(jnp.int32, (LOCALS, SLOTS), 0) == lax.broadcasted_iota(jnp.int32, (LOCALS, SLOTS), 1) >> 3
    rows = lax.broadcasted_iota(jnp.int32, (TABLES * COLD_DEV, SLOTS), 0).astype(F32)
    total = jnp.zeros((TABLES * COLD_DEV, E), F32)
    for n in range(NODES):
        named = jnp.where(keep, moved[n * LOCALS:(n + 1) * LOCALS], 0.0)
        named = jnp.sum(named, axis=0, keepdims=True)
        onehot = jnp.where(named == rows, 1.0, 0.0).astype(BF)
        total = total + dot(onehot, in_ref[n, :SLOTS, :])
    accum = accum_ref[...]
    out_ref[...] = total / jnp.sqrt(accum + total * total)


def cold_update(node, arrived, accum):
    vmem = pl.BlockSpec(memory_space=pltpu.VMEM)
    return pl.pallas_call(
        cold_kernel,
        out_shape=jax.ShapeDtypeStruct((TABLES * COLD_DEV, E), F32),
        in_specs=[pl.BlockSpec(memory_space=pltpu.SMEM), vmem, vmem],
        out_specs=vmem,
        compiler_params=LIMIT,
    )(node, arrived, accum)


def on_device(pooled, lookups, converted, w_hidden, w_out, hot_accum, cold_accum):
    node = lax.axis_index("node")
    local = lax.axis_index("local")
    zed, core = local // 2, local % 2
    ids = lookups.T
    core_arg = core.reshape(1)
    swap = [(i, i ^ 1) for i in range(LOCALS)]
    same_core = [[2 * z + c for z in range(ZS)] for c in range(2)]
    send, own, grads = backprop(
        core_arg, pooled, ids, converted.reshape(1, TOK), w_hidden, w_out.reshape(1, HID)
    )
    other = lax.ppermute(send, "local", swap)
    slab = pack(ids, grads)
    chip = add_halves(own, other)
    parts = lax.all_to_all(chip.reshape(NODES, CHUNK, WIDE), "node", 0, 0, tiled=True)
    slab = lax.all_to_all(slab, "local", 0, 0, tiled=True)
    rows = slab[:, :SLOTS].reshape(LOCALS, NODES, CAP, E).transpose(1, 0, 2, 3)
    labels = lax.dynamic_index_in_dim(slab, SLOTS + local, 1, keepdims=False)
    slab = jnp.concatenate(
        [
            rows.reshape(NODES, SLOTS, E),
            jnp.broadcast_to(labels[None], (NODES, LOCALS, E)),
        ],
        axis=1,
    )
    parts = lax.all_to_all(node_sum(parts), "local", 0, 0, axis_index_groups=same_core, tiled=True)
    block = (core * 1024 + (zed // 2) * HALF + node * CHUNK + (zed % 2) * 8) // 8
    parts = z_sum(block.reshape(1), parts, hot_accum.reshape(TABLES * HOT, E))
    slab = lax.all_to_all(slab, "node", 0, 0, tiled=True)
    parts = lax.all_to_all(parts, "local", 0, 0, axis_index_groups=same_core, tiled=True)
    parts = lax.all_to_all(spread(parts), "node", 0, 0, tiled=True)
    half = parts.reshape(HALF, WIDE)
    far = lax.ppermute(half, "local", swap)
    w1_grad, hot_step = finish(core_arg, half, far)
    cold_step = cold_update(node.reshape(1), slab, cold_accum.reshape(TABLES * COLD_DEV, E))
    return (w1_grad, hot_step.reshape(TABLES, HOT, E), cold_step.reshape(TABLES, COLD_DEV, E))


def solution(mesh):
    both = ("node", "local")
    in_specs = (P(both, None), P(both, None), P(both), P(), P(), P(), P(None, both, None))
    out_specs = (P(), P(), P(None, both, None))
    return jax.shard_map(on_device, mesh=mesh, in_specs=in_specs, out_specs=out_specs, check_vma=False)
```

time: 341 us -> 149 us (0.44)
  blocking collectives: 129 us -> 50.6 us
  waiting for transfers between devices: 107 us -> 39 us
  matrix products: 34.9 us -> 0 us
  Pallas kernels: 0 us -> 28.4 us
  between operations: 14.3 us -> 0.7 us
  other arithmetic: 10.4 us -> 0.04 us
  local copies, waits for them, and re-layouts: 12.4 us -> 4.21 us
  starting transfers between devices: 32.3 us -> 24.7 us
    psum x1 -> x0, blocking collectives: 129 us -> none  [on_device(): w1_sum, hot_sum = lax.psum((weight_term, hot_term), ('node', 'local'))]
    psum x1 -> x0, waiting for transfers between devices: 101 us -> none  [on_device(): w1_sum, hot_sum = lax.psum((weight_term, hot_term), ('node', 'local'))]
    all_to_all x0 -> x3, blocking collectives: none -> 50.6 us  [the longest x1 24 us: on_device(): lax.all_to_all(chip.reshape(NODES, CHUNK, WIDE), 'node', 0, 0, tiled=True)]
    dot_general x18 -> x0, matrix products: 34.9 us -> none  [the longest x4 14.2 us: pack_one_block(): lax.dot_general(member.astype(jnp.bfloat16), rows, (((0,), (0,)), ((), ()...]
    all_to_all x4 -> x3, waiting for transfers between devices: 5.04 us -> 36.2 us  [the longest x1 18.3 us: on_device(): slab = lax.all_to_all(slab, 'local', 0, 0, tiled=True)]
    pallas_call x0 -> x8, Pallas kernels: none -> 28.4 us  [the longest x1 8.07 us: backprop(): pl.pallas_call(backprop_kernel, out_shape=(half, half, jax.ShapeDtypeStru...]
    all_to_all x4 -> x3, starting transfers between devices: 32.3 us -> 21.2 us  [the longest x1 9.27 us: on_device(): slab = lax.all_to_all(slab, 'local', 0, 0, tiled=True)]
    convert_element_type x5 -> x0, other arithmetic: 4.11 us -> none  [the longest x1 2.07 us: on_device(): pack_slots(slot_index, grad_rows, slot_count, block_len, False)]
  transfers between devices with their start and end apart: 5 -> 5, of which waited for: 3 -> 4; matrix products, arithmetic and copies ran while one was open for 13% -> 0% of each run, Pallas kernels for 0% -> 5%
where the time goes in v1:
time: 149 us; the launch traced here: 148 us
  blocking collectives  50.6 us (34%)
  waiting for transfers between devices  39 us (26%)
  Pallas kernels  28.4 us (19%)
  starting transfers between devices  24.7 us (17%)
  local copies, waits for them, and re-layouts  4.21 us (3%)
    all_to_all x1, blocking collectives, on_device(): lax.all_to_all(chip.reshape(NODES, CHUNK, WIDE), 'node', 0, 0, tiled=True)  24 us
    all_to_all x1, waiting for transfers between devices, on_device(): slab = lax.all_to_all(slab, 'local', 0, 0, tiled=True)  18.3 us
    all_to_all x1, blocking collectives, on_device(): slab = lax.all_to_all(slab, 'node', 0, 0, tiled=True)  14.9 us
    all_to_all x1, blocking collectives, on_device(): lax.all_to_all(parts, 'local', 0, 0, axis_index_groups=same_core, tiled=T...  11.6 us
    all_to_all x1, waiting for transfers between devices, on_device(): parts = lax.all_to_all(spread(parts), 'node', 0, 0, tiled=True)  10.2 us
    all_to_all x1, starting transfers between devices, on_device(): slab = lax.all_to_all(slab, 'local', 0, 0, tiled=True)  9.27 us
    all_to_all x1, starting transfers between devices, on_device(): lax.all_to_all(node_sum(parts), 'local', 0, 0, axis_index_groups=same_cor...  8.19 us
    pallas_call x1, Pallas kernels, backprop(): pl.pallas_call(backprop_kernel, out_shape=(half, half, jax.ShapeDtypeStru...  8.07 us
  transfers between devices with their start and end apart: 5, of which 4 were waited for; matrix products, arithmetic and copies ran while one was open for 0% of the time, Pallas kernels for 5%

profile of v1, /device:TPU:1, one launch (start us, length us, event | category | flops | bytes accessed | tf_op | source)
XLA Modules:
  0.0 147.7 jit_solution(3743845123063457259)
XLA Ops:
  0.6 1.3 reshape.50.wo_ref
  1.9 8.1 %shard_map.94 = (bf16[256,2560]{1,0:T(8,128)(2,1)}, bf16[256,2560]{1,0:T(8,128)(2,1)}, bf16[512,512]{1,0:T(8,128)(2,1)}) custom-call(s32[1]{0:T(128)} %bitcast.core_ref, bf16[512,512]{1,0:T(8,128)(2,1)} %x_ref.1, s32[4,512]{1,0:T(4,128)} %bitcast.27, s32[1,512]{1,0:T(1,128)} %bitcast.30, bf16[512,2048]{1,0:T(8,128)(2,1)} %wh_ref.1, ...), custom_call_target="tpu_custom_call" | custom-call | tf_op jit(solution)/shard_map/pallas_call | solution.py:90
  10.0 3.2 %collective-permute-start = (bf16[256,2560]{1,0:T(8,128)(2,1)}, bf16[256,2560]{1,0:T(8,128)(2,1)S(1)}, u32[]{:S(2)}, u32[]{:S(2)}) collective-permute-start(bf16[256,2560]{1,0:T(8,128)(2,1)} %get-tuple-element.9), channel_id=1, source_target_pairs={{0,1},{1,0},{2,3},{3,2},{4,5},{5,4},{6,7},{7,6},{8,9},{9,8},{10,11... | collective-permute-start | bytes 3932168 | tf_op jit(solution)/shard_map/ppermute | solution.py:310
  13.2 2.9 %collective-permute-done.b_ref = bf16[256,2560]{1,0:T(8,128)(2,1)S(1)} collective-permute-done((bf16[256,2560]{1,0:T(8,128)(2,1)}, bf16[256,2560]{1,0:T(8,128)(2,1)S(1)}, u32[]{:S(2)}, u32[]{:S(2)}) %collective-permute-start) | collective-permute-done | bytes 1310752 | tf_op jit(solution)/shard_map/ppermute | solution.py:310
  16.1 0.0 copy-start.2
  16.1 1.1 copy-done.2
  17.2 3.1 %shard_map.95 = bf16[256,2560]{1,0:T(8,128)(2,1)} custom-call(bf16[256,2560]{1,0:T(8,128)(2,1)} %get-tuple-element.8.a_ref, bf16[256,2560]{1,0:T(8,128)(2,1)} %copy-done.2), custom_call_target="tpu_custom_call" | custom-call | tf_op jit(solution)/shard_map/pallas_call | solution.py:162
  20.2 24.0 %all_to_all.30.in_ref = bf16[16,16,2560]{2,1,0:T(8,128)(2,1)} all-to-all(bf16[16,16,2560]{2,1,0:T(8,128)(2,1)} %bitcast.23), channel_id=1, replica_groups=mesh['node'=16,'local'=16] {'node'}, dimensions={0} | all-to-all | bytes 2621440 | tf_op jit(solution)/shard_map/all_to_all | solution.py:313
  44.3 2.1 %shard_map.96 = bf16[8,16,384]{2,1,0:T(8,128)(2,1)} custom-call(bf16[16,16,2560]{2,1,0:T(8,128)(2,1)} %all_to_all.30.in_ref), custom_call_target="tpu_custom_call" | custom-call | tf_op jit(solution)/shard_map/pallas_call | solution.py:186
  46.4 8.2 %all-to-all-start.1 = ((bf16[8,16,384]{2,1,0:T(8,128)(2,1)}), bf16[8,16,384]{2,1,0:T(8,128)(2,1)S(1)}, u32[]{:S(2)}, u32[]{:S(2)}) async-start(bf16[8,16,384]{2,1,0:T(8,128)(2,1)} %shard_map.96), calls=%async_computation.1 | async-start | bytes 196608 | tf_op jit(solution)/shard_map/all_to_all | solution.py:324
  54.6 7.7 %all-to-all-done.1.in_ref = bf16[8,16,384]{2,1,0:T(8,128)(2,1)S(1)} async-done(((bf16[8,16,384]{2,1,0:T(8,128)(2,1)}), bf16[8,16,384]{2,1,0:T(8,128)(2,1)S(1)}, u32[]{:S(2)}, u32[]{:S(2)}) %all-to-all-start.1) | async-done | bytes 98336 | tf_op jit(solution)/shard_map/all_to_all | solution.py:324
  62.3 0.0 copy-start.3
  62.3 0.6 copy-done.3
  62.9 1.6 %shard_map.97 = bf16[8,16,384]{2,1,0:T(8,128)(2,1)} custom-call(s32[1]{0:T(128)} %bitcast.1.at_ref, bf16[8,16,384]{2,1,0:T(8,128)(2,1)} %copy-done.3, f32[2048,128]{1,0:T(8,128)} %bitcast.24), custom_call_target="tpu_custom_call" | custom-call | tf_op jit(solution)/shard_map/pallas_call | solution.py:208
  64.5 11.6 %all_to_all.31.in_ref = bf16[8,16,384]{2,1,0:T(8,128)(2,1)} all-to-all(bf16[8,16,384]{2,1,0:T(8,128)(2,1)} %shard_map.97), channel_id=1, replica_groups={{0,2,4,6,8,10,12,14},{1,3,5,7,9,11,13,15},{16,18,20,22,24,26,28,30},{17..., dimensions={0} | all-to-all | bytes 196608 | tf_op jit(solution)/shard_map/all_to_all | solution.py:328
  76.1 2.1 %shard_map.98 = bf16[16,16,2560]{2,1,0:T(8,128)(2,1)} custom-call(bf16[8,16,384]{2,1,0:T(8,128)(2,1)} %all_to_all.31.in_ref), custom_call_target="tpu_custom_call" | custom-call | tf_op jit(solution)/shard_map/pallas_call | solution.py:237
  78.2 3.7 %all-to-all-start.3 = ((bf16[16,16,2560]{2,1,0:T(8,128)(2,1)}), bf16[16,16,2560]{2,1,0:T(8,128)(2,1)S(1)}, u32[]{:S(2)}, u32[]{:S(2)}) async-start(bf16[16,16,2560]{2,1,0:T(8,128)(2,1)} %shard_map.98), calls=%async_computation.3 | async-start | bytes 2621440 | tf_op jit(solution)/shard_map/all_to_all | solution.py:329
  81.9 5.6 %shard_map.100 = bf16[16,144,128]{2,1,0:T(8,128)(2,1)} custom-call(s32[4,512]{1,0:T(4,128)} %bitcast.28, bf16[512,512]{1,0:T(8,128)(2,1)} %get-tuple-element.12.grad_ref), custom_call_target="tpu_custom_call" | custom-call | tf_op jit(solution)/shard_map/pallas_call | solution.py:146
  87.5 10.2 %all-to-all-done.3 = bf16[16,16,2560]{2,1,0:T(8,128)(2,1)S(1)} async-done(((bf16[16,16,2560]{2,1,0:T(8,128)(2,1)}), bf16[16,16,2560]{2,1,0:T(8,128)(2,1)S(1)}, u32[]{:S(2)}, u32[]{:S(2)}) %all-to-all-start.3) | async-done | bytes 1310752 | tf_op jit(solution)/shard_map/all_to_all | solution.py:329
  97.7 0.0 copy-start
  97.7 9.3 %all-to-all-start.4 = ((bf16[16,144,128]{2,1,0:T(8,128)(2,1)}), bf16[16,144,128]{2,1,0:T(8,128)(2,1)S(1)}, u32[]{:S(2)}, u32[]{:S(2)}) async-start(bf16[16,144,128]{2,1,0:T(8,128)(2,1)} %shard_map.100), calls=%async_computation.4 | async-start | bytes 1179648 | tf_op jit(solution)/shard_map/all_to_all | solution.py:314
  107.0 0.3 collective-permute-start.1
  107.3 18.3 %all-to-all-done.4 = bf16[16,144,128]{2,1,0:T(8,128)(2,1)S(1)} async-done(((bf16[16,144,128]{2,1,0:T(8,128)(2,1)}), bf16[16,144,128]{2,1,0:T(8,128)(2,1)S(1)}, u32[]{:S(2)}, u32[]{:S(2)}) %all-to-all-start.4) | async-done | bytes 589856 | tf_op jit(solution)/shard_map/all_to_all | solution.py:314
  125.6 0.1 copy_bitcast_fusion
  125.8 0.0 copy-done
  125.8 14.9 %all_to_all.32.in_ref = bf16[16,144,128]{2,1,0:T(8,128)(2,1)} all-to-all(bf16[16,144,128]{2,1,0:T(8,128)(2,1)S(1)} %pad_maximum_fusion), channel_id=1, replica_groups=mesh['node'=16,'local'=16] {'node'}, dimensions={0} | all-to-all | bytes 1179648 | tf_op jit(solution)/shard_map/all_to_all | solution.py:327
  140.8 2.3 %shard_map.101 = f32[256,128]{1,0:T(8,128)} custom-call(s32[1]{0:T(128)} %bitcast.8.node_ref, bf16[16,144,128]{2,1,0:T(8,128)(2,1)} %all_to_all.32.in_ref, f32[256,128]{1,0:T(8,128)} %bitcast.25), custom_call_target="tpu_custom_call" | custom-call | tf_op jit(solution)/shard_map/pallas_call | solution.py:290
  143.1 0.0 collective-permute-done.1.far_ref
  143.1 0.0 copy-start.1
  143.1 1.1 copy-done.1
  144.2 3.5 %shard_map.99 = (bf16[512,2048]{1,0:T(8,128)(2,1)}, f32[2048,128]{1,0:T(8,128)}) custom-call(s32[1]{0:T(128)} %bitcast.core_ref, bf16[256,2560]{1,0:T(8,128)(2,1)} %bitcast.22, bf16[256,2560]{1,0:T(8,128)(2,1)} %copy-done.1), custom_call_target="tpu_custom_call" | custom-call | tf_op jit(solution)/shard_map/pallas_call | solution.py:257
  (4 shorter events, 0.1 us)
Async XLA Ops:
  10.0 6.1 %collective-permute-start = (bf16[256,2560]{1,0:T(8,128)(2,1)}, bf16[256,2560]{1,0:T(8,128)(2,1)S(1)}, u32[]{:S(2)}, u32[]{:S(2)}) collective-permute-start(bf16[256,2560]{1,0:T(8,128)(2,1)} %get-tuple-element.9), channel_id=1, source_target_pairs={{0,1},{1,0},{2,3},{3,2},{4,5},{5,4},{6,7},{7,6},{8,9},{9,8},{10,11... | collective-permute-start | bytes 3932168 | tf_op jit(solution)/shard_map/ppermute | solution.py:310
  16.1 1.1 copy-start.2
  46.4 15.9 %all-to-all-start.1 = ((bf16[8,16,384]{2,1,0:T(8,128)(2,1)}), bf16[8,16,384]{2,1,0:T(8,128)(2,1)S(1)}, u32[]{:S(2)}, u32[]{:S(2)}) async-start(bf16[8,16,384]{2,1,0:T(8,128)(2,1)} %shard_map.96), calls=%async_computation.1 | async-start | bytes 196608 | tf_op jit(solution)/shard_map/all_to_all | solution.py:324
  62.3 0.6 copy-start.3
  78.2 19.5 %all-to-all-start.3 = ((bf16[16,16,2560]{2,1,0:T(8,128)(2,1)}), bf16[16,16,2560]{2,1,0:T(8,128)(2,1)S(1)}, u32[]{:S(2)}, u32[]{:S(2)}) async-start(bf16[16,16,2560]{2,1,0:T(8,128)(2,1)} %shard_map.98), calls=%async_computation.3 | async-start | bytes 2621440 | tf_op jit(solution)/shard_map/all_to_all | solution.py:329
  97.7 28.2 %copy-start = (bf16[16,16,2560]{2,1,0:T(8,128)(2,1)}, bf16[16,16,2560]{2,1,0:T(8,128)(2,1)S(1)}, u32[]{:S(2)}) copy-start(bf16[16,16,2560]{2,1,0:T(8,128)(2,1)S(1)} %all-to-all-done.3) | copy-start | bytes 3932164
  97.7 27.9 %all-to-all-start.4 = ((bf16[16,144,128]{2,1,0:T(8,128)(2,1)}), bf16[16,144,128]{2,1,0:T(8,128)(2,1)S(1)}, u32[]{:S(2)}, u32[]{:S(2)}) async-start(bf16[16,144,128]{2,1,0:T(8,128)(2,1)} %shard_map.100), calls=%async_computation.4 | async-start | bytes 1179648 | tf_op jit(solution)/shard_map/all_to_all | solution.py:314
  107.0 36.1 %collective-permute-start.1 = (bf16[256,2560]{1,0:T(8,128)(2,1)S(1)}, bf16[256,2560]{1,0:T(8,128)(2,1)S(1)}, u32[]{:S(2)}, u32[]{:S(2)}) collective-permute-start(bf16[256,2560]{1,0:T(8,128)(2,1)S(1)} %bitcast.21), channel_id=1, source_target_pairs={{0,1},{1,0},{2,3},{3,2},{4,5},{5,4},{6,7},{7,6},{8,9},{9,8},{10,11... | collective-permute-start | bytes 3932168 | tf_op jit(solution)/shard_map/ppermute | solution.py:331
  143.1 1.1 copy-start.1

commit v2 on v1

v2 whole, which is shorter than its diff:
```python
import jax
import jax.numpy as jnp
from jax import lax
from jax.experimental import pallas as pl
from jax.experimental.pallas import tpu as pltpu
from jax.sharding import Mesh
from jax.sharding import PartitionSpec as P

CAP = 8
E = 128
HID = 2048
FEAT = 512
TOK = 512
TABLES = 4
HOT = 512
COLD_DEV = 64
NODES = 16
LOCALS = 16
ZQ = 4
ZP = 2
GROUP = NODES * ZP
OWNERS = NODES * LOCALS
HALF = FEAT // 2
CHUNK = HALF // NODES
PCOL = HID // ZP
WIDE = PCOL + 2 * E
HOT_HALF = TABLES * HOT // 2
SLOT_HALF = OWNERS * CAP // 2
NODE_SLOTS = SLOT_HALF // NODES
PAIR = 2 * CAP
SLAB = ZQ + 1
BF = jnp.bfloat16
F32 = jnp.float32
MIB = 1024 * 1024
AXES = ("node", "zq", "zp", "core")
VMEM = pl.BlockSpec(memory_space=pltpu.VMEM)
HBM = pl.BlockSpec(memory_space=pltpu.HBM)
SMEM = pl.BlockSpec(memory_space=pltpu.SMEM)


def dot(a, b):
    return jnp.dot(a, b, preferred_element_type=F32)


def dot_nt(a, b):
    return lax.dot_general(a, b, (((1,), (1,)), ((), ())), preferred_element_type=F32)


def shape(*dims, dtype=BF):
    return jax.ShapeDtypeStruct(dims, dtype)


def call(kernel, out_shape, args, scalars=0, scratch=(), limit=16, flops=0, size=0, spec=VMEM, out_specs=None):
    many = isinstance(out_shape, (tuple, list))
    return pl.pallas_call(
        kernel,
        out_shape=out_shape,
        in_specs=[SMEM] * scalars + [spec] * (len(args) - scalars),
        out_specs=out_specs or (tuple(VMEM for _ in out_shape) if many else VMEM),
        scratch_shapes=scratch,
        compiler_params=pltpu.CompilerParams(vmem_limit_bytes=limit * MIB),
        cost_estimate=pl.CostEstimate(flops=flops, bytes_accessed=size, transcendentals=0),
    )(*args)


def backprop_kernel(
    core_ref, x_hbm, ids_hbm, y_hbm, wh_hbm, wo_hbm, send_hbm, own_ref, grad_hbm,
    slope_ref, pre_ref, xt_ref, x_ref, ids_ref, y_ref, wh_ref, wo_ref, send_ref, grad_ref, hit_ref, sems, out_sems,
):
    core = core_ref[0]
    step = 256
    blocks = HID // step
    loads = [
        pltpu.make_async_copy(wh_hbm.at[:, pl.ds(j * step, step)], wh_ref.at[:, pl.ds(j * step, step)], sems.at[j])
        for j in range(blocks)
    ]
    small = [
        pltpu.make_async_copy(src, dst, sems.at[blocks + i])
        for i, (src, dst) in enumerate(((x_hbm, x_ref), (wo_hbm, wo_ref), (ids_hbm, ids_ref), (y_hbm, y_ref)))
    ]
    stores = []

    def store(src, dst):
        copy = pltpu.make_async_copy(src, dst, out_sems.at[len(stores)])
        copy.start()
        stores.append(copy)

    for copy in (*small[1:], small[0], *loads):
        copy.start()
    for copy in small[1:]:
        copy.wait()
    hot_iota = lax.broadcasted_iota(jnp.int32, (HOT, TOK), 0)
    for t in range(TABLES):
        hit = ids_ref[t:t + 1, :] == hot_iota
        hit_ref[t] = jnp.where(hit, 1.0, 0.0).astype(BF)
    small[0].wait()
    x = x_ref[...]
    xt_ref[...] = x.T
    wo = wo_ref[...].astype(F32)
    logit = jnp.zeros((TOK, E), F32)
    for j in range(blocks):
        if j % 4 == 0:
            for copy in loads[j:j + 4]:
                copy.wait()
        cols = slice(j * step, (j + 1) * step)
        v = dot(x, wh_ref[:, cols])
        s = jax.nn.sigmoid(v)
        h = v * s
        slope_ref[:, cols] = s + h * (1.0 - s)
        out_row = jnp.concatenate([wo[2 * j:2 * j + 1], wo[2 * j + 1:2 * j + 2]], axis=1)
        out_row = jnp.broadcast_to(out_row, (E, step)).astype(BF)
        logit = logit + dot_nt(h.astype(BF), out_row)
    chance = jax.nn.sigmoid(logit)
    y = jnp.broadcast_to(y_ref[...].astype(F32), (E, TOK)).T
    weight = y * (1.0 + chance) + (1.0 - y) * (1.0 - chance) * (1.0 + chance)
    lg = weight * (chance - y)
    lg = jnp.concatenate([lg] * (step // E), axis=1)
    own_rows = pl.ds(pl.multiple_of(core * HALF, HALF), HALF)
    far_rows = pl.ds(pl.multiple_of((1 - core) * HALF, HALF), HALF)
    for j in range(HID // step):
        cols = slice(j * step, (j + 1) * step)
        out_row = jnp.concatenate([wo[2 * j:2 * j + 1], wo[2 * j + 1:2 * j + 2]], axis=1)
        pre = (lg * out_row * slope_ref[:, cols]).astype(BF)
        pre_ref[:, cols] = pre
        part, at = divmod(j * step, PCOL)
        for rows, out_ref in ((far_rows, send_ref), (own_rows, own_ref)):
            term = dot(xt_ref[rows, :], pre).astype(BF)
            out_ref[:, part, :, at:at + step] = term.reshape(NODES, CHUNK, step)
        if at + step == PCOL:
            store(send_ref.at[:, part, :, pl.ds(0, PCOL)], send_hbm.at[:, part, :, pl.ds(0, PCOL)])
    grad_ref[...] = dot_nt(pre_ref[...], wh_ref[...]).astype(BF)
    store(grad_ref, grad_hbm)
    for side, out_ref in ((1 - core, send_ref), (core, own_ref)):
        for t in range(ZP):
            table = side * 2 + t
            onehot = hit_ref[table]
            grads = grad_ref[:, pl.ds(pl.multiple_of(table * E, E), E)]
            total = dot(onehot, grads).astype(BF)
            for b in range(2):
                at = PCOL + b * E
                out_ref[:, t, :, at:at + E] = total[b * HALF:(b + 1) * HALF].reshape(NODES, CHUNK, E)
        if out_ref is send_ref:
            store(send_ref.at[:, :, :, pl.ds(PCOL, 2 * E)], send_hbm.at[:, :, :, pl.ds(PCOL, 2 * E)])
    for copy in stores:
        copy.wait()


def pack_kernel(core_ref, ids_ref, grad_ref, send_ref, own_ref, rows_ref):
    core = core_ref[0]
    owner_iota = lax.broadcasted_iota(jnp.int32, (OWNERS, TOK), 0)
    earlier = lax.broadcasted_iota(jnp.int32, (TOK, TOK), 0) < lax.broadcasted_iota(jnp.int32, (TOK, TOK), 1)
    earlier = jnp.where(earlier, 1.0, 0.0).astype(BF)
    carry = jnp.zeros((OWNERS, 1), F32)
    slots, names = [], []
    for t in range(TABLES):
        ids = ids_ref[t:t + 1, :]
        cold = ids >= HOT
        offset = jnp.where(cold, ids - HOT, 0)
        owner = jnp.where(cold, offset >> 6, -1)
        member = jnp.where(owner == owner_iota, 1.0, 0.0)
        before = dot(member.astype(BF), earlier) + carry
        rank = jnp.sum(member * before, axis=0, keepdims=True).astype(jnp.int32)
        carry = carry + jnp.sum(member, axis=1, keepdims=True)
        core_at, zp_at, zq_at, node_at = owner & 1, (owner >> 1) & 1, (owner >> 2) & 3, owner >> 4
        slot = (((core_at * NODES + node_at) * ZP + zp_at) * ZQ + zq_at) * CAP + rank
        slots.append(jnp.where(cold, slot, -1))
        names.append(((offset & (COLD_DEV - 1)) + t * COLD_DEV).astype(F32))
        rows_ref[t * TOK:(t + 1) * TOK, :] = grad_ref[:, t * E:(t + 1) * E]
    slot_col = jnp.concatenate(slots + slots, axis=0).astype(F32).T.astype(jnp.int32)
    lane = lax.broadcasted_iota(jnp.int32, (TOK, E), 1) - core * NODE_SLOTS
    group = lax.broadcasted_iota(jnp.int32, (NODES, TOK), 0)
    flat = jnp.concatenate(slots, axis=1)
    block = 512
    iota = lax.broadcasted_iota(jnp.int32, (block, TABLES * TOK), 0)
    low = [jnp.where((slot_col[:, t:t + 1] & (NODE_SLOTS - 1)) == lane, 1.0, 0.0).astype(BF) for t in range(TABLES)]
    for side, out_ref in ((1 - core, send_ref), (core, own_ref)):
        labels = jnp.zeros((NODES, E), F32)
        for t in range(TABLES):
            high = jnp.where((slots[t] >> 6) - side * NODES == group, names[t], 0.0).astype(BF)
            labels = labels + dot(high, low[t])
        out_ref[SLOT_HALF:, :] = labels.astype(BF)
        for b in range(SLOT_HALF // block):
            member = jnp.where(flat - (side * SLOT_HALF + b * block) == iota, 1.0, 0.0).astype(BF)
            out_ref[b * block:(b + 1) * block, :] = dot(member, rows_ref[...]).astype(BF)


def add_kernel(a_ref, b_ref, out_ref):
    out_ref[...] = a_ref[...] + b_ref[...]


def merge_kernel(core_ref, cold_ref, far_cold_ref, out_ref):
    first = core_ref[0] == 0
    own, far = cold_ref[...].astype(F32), far_cold_ref[...].astype(F32)
    labels = (own[SLOT_HALF:] + far[SLOT_HALF:]).astype(BF)
    own = own[:SLOT_HALF].reshape(GROUP * ZQ, CAP, E)
    far = far[:SLOT_HALF].reshape(GROUP * ZQ, CAP, E)
    pair = [jnp.where(first, own, far), jnp.where(first, far, own)]
    out_ref[:, :ZQ] = jnp.concatenate(pair, axis=1).astype(BF).reshape(GROUP, ZQ, PAIR, E)
    for g in range(GROUP):
        out_ref[g, ZQ] = labels


def group_sum_kernel(in_ref, out_ref):
    total = in_ref[0].astype(F32)
    for g in range(1, GROUP):
        total = total + in_ref[g].astype(F32)
    out_ref[...] = total.astype(BF)


def step_kernel(block_ref, a_ref, b_ref, c_ref, d_ref, accum0_ref, accum1_ref, out_ref):
    total = (a_ref[...].astype(F32) + b_ref[...].astype(F32)) + (c_ref[...].astype(F32) + d_ref[...].astype(F32))
    hot = total[:, PCOL:]
    accum = jnp.concatenate([accum0_ref[...], accum1_ref[...]], axis=1)
    stepped = hot / jnp.sqrt(accum + hot * hot)
    out_ref[...] = jnp.concatenate([total[:, :PCOL], stepped], axis=1).astype(BF)


def spread_kernel(place_ref, own_ref, far_ref, out_ref):
    zp = place_ref[2]
    own, far = own_ref[...], far_ref[...]
    for n in range(NODES):
        out_ref[n, zp] = own
        out_ref[n, 1 - zp] = far


def step(blocks, parts, accum):
    return pl.pallas_call(
        step_kernel,
        out_shape=shape(CHUNK, WIDE),
        grid_spec=pltpu.PrefetchScalarGridSpec(
            num_scalar_prefetch=1,
            grid=(1,),
            in_specs=[VMEM] * ZQ + [
                pl.BlockSpec((CHUNK, E), lambda i, at: (at[0], 0)),
                pl.BlockSpec((CHUNK, E), lambda i, at: (at[1], 0)),
            ],
            out_specs=VMEM,
        ),
        compiler_params=pltpu.CompilerParams(vmem_limit_bytes=16 * MIB),
        cost_estimate=pl.CostEstimate(flops=0, bytes_accessed=2 * MIB, transcendentals=0),
    )(blocks, *parts, accum, accum)


def cold_dense_kernel(place_ref, in_ref, *out_refs):
    node, zq, zp = place_ref[0], place_ref[1], place_ref[2]
    mine = lax.broadcasted_iota(jnp.int32, (NODES, E), 0) == node
    labels = []
    for g in range(GROUP):
        named = jnp.where(mine, in_ref[g, ZQ].astype(F32), 0.0)
        labels.append(jnp.sum(named, axis=0, keepdims=True))
    labels = jnp.concatenate(labels, axis=0).astype(BF)
    entries = GROUP * PAIR
    lane = lax.broadcasted_iota(jnp.int32, (E, entries), 0)
    place = lax.broadcasted_iota(jnp.int32, (E, entries), 1)
    wanted = ((place >> 3) & 1) * NODE_SLOTS + zp * (ZQ * CAP) + (place & 7)
    keep = lax.broadcasted_iota(jnp.int32, (GROUP, entries), 0) == lax.broadcasted_iota(jnp.int32, (GROUP, entries), 1) >> 4
    rows = lax.broadcasted_iota(jnp.int32, (TABLES * COLD_DEV, entries), 0).astype(F32)
    for d, out_ref in enumerate(out_refs):
        target = zq ^ d
        moved = dot(labels, jnp.where(lane == wanted + target * CAP, 1.0, 0.0).astype(BF))
        named = jnp.sum(jnp.where(keep, moved, 0.0), axis=0, keepdims=True)
        onehot = jnp.where(named == rows, 1.0, 0.0).astype(BF)
        out_ref[...] = dot(onehot, in_ref[:, target].reshape(entries, E)).astype(BF)


def cold_step_kernel(accum_ref, a_ref, b_ref, c_ref, d_ref, out_ref):
    total = (a_ref[...].astype(F32) + b_ref[...].astype(F32)) + (c_ref[...].astype(F32) + d_ref[...].astype(F32))
    out_ref[...] = total / jnp.sqrt(accum_ref[...] + total * total)


def finish_kernel(core_ref, in_ref, *refs):
    w1_ref, hot_ref = refs[-2:]
    for part in range(ZP):
        w1_ref[:, part * PCOL:(part + 1) * PCOL] = in_ref[:, part, :, :PCOL].reshape(HALF, PCOL)
        for b in range(2):
            at = PCOL + b * E
            hot = in_ref[:, part, :, at:at + E].reshape(HALF, E)
            hot_ref[(2 * part + b) * HALF:(2 * part + b + 1) * HALF, :] = hot.astype(F32)


def finish(side, half, held=()):
    return pl.pallas_call(
        finish_kernel,
        out_shape=(shape(FEAT, HID), shape(TABLES * HOT, E, dtype=F32)),
        grid_spec=pltpu.PrefetchScalarGridSpec(
            num_scalar_prefetch=1,
            grid=(1,),
            in_specs=[VMEM] + [pl.BlockSpec(memory_space=pl.ANY)] * len(held),
            out_specs=(
                pl.BlockSpec((HALF, HID), lambda i, at: (at[0], 0)),
                pl.BlockSpec((HOT_HALF, E), lambda i, at: (at[0], 0)),
            ),
        ),
        input_output_aliases={2: 0, 3: 1} if held else {},
        compiler_params=pltpu.CompilerParams(vmem_limit_bytes=16 * MIB),
        cost_estimate=pl.CostEstimate(flops=0, bytes_accessed=4 * MIB, transcendentals=0),
    )(side, half, *held)


def on_device(pooled, lookups, converted, w_hidden, w_out, hot_accum, cold_accum):
    node, zq, zp, core = (lax.axis_index(name) for name in AXES)
    ids = lookups.T
    core_arg = core.reshape(1)
    place = jnp.stack([node, zq, zp])

    def in_hbm(array):
        return pltpu.with_memory_space_constraint(array, pltpu.HBM)

    def flip(array, axis, mask):
        return lax.ppermute(array, axis, [(i, i ^ mask) for i in range(lax.axis_size(axis))])

    def exchange(array):
        return lax.all_to_all(array, ("node", "zp"), 0, 0, tiled=True)

    halves = shape(NODES, ZP, CHUNK, WIDE)
    send, own, grads = call(
        backprop_kernel,
        (pltpu.HBM(halves.shape, BF), pltpu.VMEM(halves.shape, BF), pltpu.HBM((TOK, FEAT), BF)),
        (core_arg, *map(in_hbm, (pooled, ids, converted.reshape(1, TOK), w_hidden, w_out.reshape(HID // E, E)))),
        scalars=1,
        scratch=[
            pltpu.VMEM((TOK, HID), F32),
            pltpu.VMEM((TOK, HID), BF),
            pltpu.VMEM((FEAT, TOK), BF),
            pltpu.VMEM((TOK, FEAT), BF),
            pltpu.VMEM((TABLES, TOK), jnp.int32),
            pltpu.VMEM((1, TOK), jnp.int32),
            pltpu.VMEM((FEAT, HID), BF),
            pltpu.VMEM((HID // E, E), BF),
            pltpu.VMEM((NODES, ZP, CHUNK, WIDE), BF),
            pltpu.VMEM((TOK, FEAT), BF),
            pltpu.VMEM((TABLES, HOT, TOK), BF),
            pltpu.SemaphoreType.DMA((HID // 256 + 4,)),
            pltpu.SemaphoreType.DMA((4,)),
        ],
        spec=HBM,
        out_specs=(HBM, VMEM, HBM),
        limit=24,
        flops=4 * 10**9,
        size=8 * MIB,
    )
    chip = call(add_kernel, halves, (own, flip(send, "core", 1)), size=3 * MIB)
    parts = exchange(chip.reshape(GROUP, CHUNK, WIDE))
    cold_send, cold_own = call(
        pack_kernel,
        (shape(SLOT_HALF + NODES, E), shape(SLOT_HALF + NODES, E)),
        (core_arg, ids, grads),
        scalars=1,
        scratch=[pltpu.VMEM((TABLES * TOK, E), BF)],
        flops=6 * 10**9,
        size=8 * MIB,
    )
    slab = call(
        merge_kernel,
        shape(GROUP, SLAB, PAIR, E),
        (core_arg, cold_own, flip(cold_send, "core", 1)),
        scalars=1,
        size=3 * MIB,
    )
    part = call(group_sum_kernel, shape(CHUNK, WIDE), (parts,), size=2 * MIB)
    slab = exchange(slab)
    quad = [part] + [flip(part, "zq", d) for d in range(1, ZQ)]
    block = ((core * ZP + zp) * 2 * HALF + node * CHUNK) // CHUNK
    done = step(jnp.stack([block, block + HALF // CHUNK]), quad, hot_accum.reshape(TABLES * HOT, E))
    whole = call(spread_kernel, halves, (place, done, flip(done, "zp", 1)), scalars=1, size=2 * MIB)
    half = lax.all_to_all(whole, "node", 0, 0, tiled=True)
    cold = call(
        cold_dense_kernel,
        tuple(shape(TABLES * COLD_DEV, E) for _ in range(ZQ)),
        (place, slab),
        scalars=1,
        flops=10**9,
        size=2 * MIB,
    )
    cold = [cold[0]] + [flip(cold[d], "zq", d) for d in range(1, ZQ)]
    half, cold = lax.optimization_barrier((half, cold))
    cold_step = call(
        cold_step_kernel,
        shape(TABLES * COLD_DEV, E, dtype=F32),
        (cold_accum.reshape(TABLES * COLD_DEV, E), *cold),
        size=MIB,
    )
    far = flip(half, "core", 1)
    held = finish(core_arg, half)
    w1_grad, hot_step = finish(1 - core_arg, far, held)
    return (w1_grad, hot_step.reshape(TABLES, HOT, E), cold_step.reshape(TABLES, COLD_DEV, E))


def solution(mesh):
    mesh = Mesh(mesh.devices.reshape(NODES, ZQ, ZP, 2), AXES)
    in_specs = (P(AXES, None), P(AXES, None), P(AXES), P(), P(), P(), P(None, AXES, None))
    out_specs = (P(), P(), P(None, AXES, None))
    return jax.shard_map(on_device, mesh=mesh, in_specs=in_specs, out_specs=out_specs, check_vma=False)
```

time: 149 us -> 97.4 us (0.65)
  blocking collectives: 50.6 us -> 0 us
  starting transfers between devices: 24.7 us -> 43.5 us
  Pallas kernels: 28.4 us -> 20.8 us
  waiting for transfers between devices: 39 us -> 31.8 us
  local copies, waits for them, and re-layouts: 4.21 us -> 0.02 us
    all_to_all x3 -> x0, blocking collectives: 50.6 us -> none  [the longest x1 24 us: on_device(): lax.all_to_all(chip.reshape(NODES, CHUNK, WIDE), 'node', 0, 0, tiled=True)]
    ppermute x2 -> x10, starting transfers between devices: 3.55 us -> 26.3 us  [flip(): lax.ppermute(array, axis, [(i, i ^ mask) for i in range(lax.axis_size(axi...]
    all_to_all x3, waiting for transfers between devices: 36.2 us -> 16.4 us  [the longest x2 13.8 us: exchange(): return lax.all_to_all(array, ('node', 'zp'), 0, 0, tiled=True)]
    ppermute x2 -> x10, waiting for transfers between devices: 2.87 us -> 15.4 us  [flip(): lax.ppermute(array, axis, [(i, i ^ mask) for i in range(lax.axis_size(axi...]
    pallas_call x8 -> x11, Pallas kernels: 28.4 us -> 20.8 us  [the longest x8 17.7 us: call(): pl.pallas_call(kernel, out_shape=out_shape, in_specs=[SMEM] * scalars + [...]
    all_to_all x3, starting transfers between devices: 21.2 us -> 17.2 us  [the longest x2 10.7 us: exchange(): return lax.all_to_all(array, ('node', 'zp'), 0, 0, tiled=True)]
    unnamed x9 -> x8, local copies, waits for them, and re-layouts: 2.76 us -> 0.02 us
  transfers between devices with their start and end apart: 5 -> 13, of which waited for: 4 -> 10; matrix products, arithmetic and copies ran while one was open for 0% -> 0% of each run, Pallas kernels for 5% -> 11%
where the time goes in v2:
time: 97.4 us; the launch traced here: 97 us
  starting transfers between devices  43.5 us (45%)
  waiting for transfers between devices  31.8 us (33%)
  Pallas kernels  20.8 us (21%)
    ppermute x10, starting transfers between devices, flip(): lax.ppermute(array, axis, [(i, i ^ mask) for i in range(lax.axis_size(axi...  26.3 us
    pallas_call x8, Pallas kernels, call(): pl.pallas_call(kernel, out_shape=out_shape, in_specs=[SMEM] * scalars + [...  17.7 us
    ppermute x10, waiting for transfers between devices, flip(): lax.ppermute(array, axis, [(i, i ^ mask) for i in range(lax.axis_size(axi...  15.4 us
    all_to_all x2, waiting for transfers between devices, exchange(): return lax.all_to_all(array, ('node', 'zp'), 0, 0, tiled=True)  13.8 us
    all_to_all x2, starting transfers between devices, exchange(): return lax.all_to_all(array, ('node', 'zp'), 0, 0, tiled=True)  10.7 us
    all_to_all x1, starting transfers between devices, on_device(): half = lax.all_to_all(whole, 'node', 0, 0, tiled=True)  6.52 us
    all_to_all x1, waiting for transfers between devices, on_device(): half = lax.all_to_all(whole, 'node', 0, 0, tiled=True)  2.56 us
    pallas_call x2, Pallas kernels, finish(): pl.pallas_call(finish_kernel, out_shape=(shape(FEAT, HID), shape(TABLES *...  2.46 us
  transfers between devices with their start and end apart: 13, of which 10 were waited for; matrix products, arithmetic and copies ran while one was open for 0% of the time, Pallas kernels for 11%

profile of v2, /device:TPU:1, one launch (start us, length us, event | category | flops | bytes accessed | tf_op | source)
XLA Modules:
  0.0 97.0 jit_solution(8301305173580060175)
XLA Ops:
  0.6 7.5 %shard_map.94 = (bf16[16,2,16,1280]{3,2,1,0:T(8,128)(2,1)}, bf16[16,2,16,1280]{3,2,1,0:T(8,128)(2,1)S(1)}, bf16[512,512]{1,0:T(8,128)(2,1)}) custom-call(s32[1]{0:T(128)} %bitcast.core_ref, bf16[512,512]{1,0:T(8,128)(2,1)} %x_hbm.1, s32[4,512]{1,0:T(4,128)} %bitcast.17, s32[1,512]{1,0:T(1,128)} %bitcast.22, bf16[512,2048]{1,0:T(8,128)(2,1)} %wh_hbm.1, ...), custom_call_target="tpu_custom_call" | custom-call | flops 4000000000 | bytes 8388608 | tf_op jit(solution)/shard_map/pallas_call | solution.py:55
  8.2 3.3 %collective-permute-start = (bf16[16,2,16,1280]{3,2,1,0:T(8,128)(2,1)}, bf16[16,2,16,1280]{3,2,1,0:T(8,128)(2,1)S(1)}, u32[]{:S(2)}, u32[]{:S(2)}) collective-permute-start(bf16[16,2,16,1280]{3,2,1,0:T(8,128)(2,1)} %get-tuple-element.22), channel_id=1, source_target_pairs={{0,1},{1,0},{2,3},{3,2},{4,5},{5,4},{6,7},{7,6},{8,9},{9,8},{10,11... | collective-permute-start | bytes 3932168 | tf_op jit(solution)/shard_map/ppermute | solution.py:310
  11.5 2.9 %collective-permute-done.b_ref = bf16[16,2,16,1280]{3,2,1,0:T(8,128)(2,1)S(1)} collective-permute-done((bf16[16,2,16,1280]{3,2,1,0:T(8,128)(2,1)}, bf16[16,2,16,1280]{3,2,1,0:T(8,128)(2,1)S(1)}, u32[]{:S(2)}, u32[]{:S(2)}) %collective-permute-start) | collective-permute-done | bytes 1310752 | tf_op jit(solution)/shard_map/ppermute | solution.py:310
  14.4 1.2 %shard_map.95 = bf16[16,2,16,1280]{3,2,1,0:T(8,128)(2,1)} custom-call(bf16[16,2,16,1280]{3,2,1,0:T(8,128)(2,1)S(1)} %get-tuple-element.21.a_ref, bf16[16,2,16,1280]{3,2,1,0:T(8,128)(2,1)S(1)} %collective-permute-done.b_ref), custom_call_target="tpu_custom_call" | custom-call | bytes 3145728 | tf_op jit(solution)/shard_map/pallas_call | solution.py:55
  15.5 0.0 copy-start.2
  15.5 0.0 copy-start.3
  15.5 6.8 %all-to-all-start = ((bf16[32,16,1280]{2,1,0:T(8,128)(2,1)}), bf16[32,16,1280]{2,1,0:T(8,128)(2,1)S(1)}, u32[]{:S(2)}, u32[]{:S(2)}) async-start(bf16[32,16,1280]{2,1,0:T(8,128)(2,1)} %bitcast.9), calls=%async_computation | async-start | bytes 2621440 | tf_op jit(solution)/shard_map/all_to_all | solution.py:313
  22.3 0.0 copy-done.2
  22.4 0.0 copy-done.3
  22.4 3.9 %shard_map.99 = (bf16[1040,128]{1,0:T(8,128)(2,1)S(1)}, bf16[1040,128]{1,0:T(8,128)(2,1)S(1)}) custom-call(s32[1]{0:T(128)} %bitcast.core_ref, s32[4,512]{1,0:T(4,128)S(1)} %bitcast.18, bf16[512,512]{1,0:T(8,128)(2,1)S(1)} %copy-done.3), custom_call_target="tpu_custom_call" | custom-call | flops 6000000000 | bytes 8388608 | tf_op jit(solution)/shard_map/pallas_call | solution.py:55
  26.2 0.7 collective-permute-start.5
  27.0 1.2 %collective-permute-done.5.far_cold_ref = bf16[1040,128]{1,0:T(8,128)(2,1)S(1)} collective-permute-done((bf16[1040,128]{1,0:T(8,128)(2,1)S(1)}, bf16[1040,128]{1,0:T(8,128)(2,1)S(1)}, u32[]{:S(2)}, u32[]{:S(2)}) %collective-permute-start.5) | collective-permute-done | bytes 266272 | tf_op jit(solution)/shard_map/ppermute | solution.py:310
  28.1 0.9 shard_map.100
  29.1 0.0 copy-start
  29.1 13.8 %all-to-all-done.in_ref = bf16[32,16,1280]{2,1,0:T(8,128)(2,1)S(1)} async-done(((bf16[32,16,1280]{2,1,0:T(8,128)(2,1)}), bf16[32,16,1280]{2,1,0:T(8,128)(2,1)S(1)}, u32[]{:S(2)}, u32[]{:S(2)}) %all-to-all-start) | async-done | bytes 1310752 | tf_op jit(solution)/shard_map/all_to_all | solution.py:313
  42.9 3.9 %all-to-all-start.2 = ((bf16[32,5,16,128]{3,2,1,0:T(8,128)(2,1)}), bf16[32,5,16,128]{3,2,1,0:T(8,128)(2,1)S(1)}, u32[]{:S(2)}, u32[]{:S(2)}) async-start(bf16[32,5,16,128]{3,2,1,0:T(8,128)(2,1)} %shard_map.100), calls=%async_computation.2 | async-start | bytes 1310720 | tf_op jit(solution)/shard_map/all_to_all | solution.py:313
  46.8 0.2 shard_map.96.a_ref
  47.0 5.2 %collective-permute-start.3 = (bf16[16,1280]{1,0:T(8,128)(2,1)S(1)}, bf16[16,1280]{1,0:T(8,128)(2,1)S(1)}, u32[]{:S(2)}, u32[]{:S(2)}) collective-permute-start(bf16[16,1280]{1,0:T(8,128)(2,1)S(1)} %shard_map.96.a_ref), channel_id=1, source_target_pairs={{0,12},{4,8},{8,4},{12,0},{1,13},{5,9},{9,5},{13,1},{2,14},{6,10},... | collective-permute-start | bytes 122888 | tf_op jit(solution)/shard_map/ppermute | solution.py:310
  52.2 1.2 %collective-permute-start.2 = (bf16[16,1280]{1,0:T(8,128)(2,1)S(1)}, bf16[16,1280]{1,0:T(8,128)(2,1)S(1)}, u32[]{:S(2)}, u32[]{:S(2)}) collective-permute-start(bf16[16,1280]{1,0:T(8,128)(2,1)S(1)} %shard_map.96.a_ref), channel_id=1, source_target_pairs={{0,8},{4,12},{8,0},{12,4},{1,9},{5,13},{9,1},{13,5},{2,10},{6,14},... | collective-permute-start | bytes 122888 | tf_op jit(solution)/shard_map/ppermute | solution.py:310
  53.4 1.2 %collective-permute-start.1 = (bf16[16,1280]{1,0:T(8,128)(2,1)S(1)}, bf16[16,1280]{1,0:T(8,128)(2,1)S(1)}, u32[]{:S(2)}, u32[]{:S(2)}) collective-permute-start(bf16[16,1280]{1,0:T(8,128)(2,1)S(1)} %shard_map.96.a_ref), channel_id=1, source_target_pairs={{0,4},{4,0},{8,12},{12,8},{1,5},{5,1},{9,13},{13,9},{2,6},{6,2},{1... | collective-permute-start | bytes 122888 | tf_op jit(solution)/shard_map/ppermute | solution.py:310
  54.6 0.1 pad_add_fusion.1.block_ref
  54.7 4.0 %collective-permute-done.3.d_ref = bf16[16,1280]{1,0:T(8,128)(2,1)S(1)} collective-permute-done((bf16[16,1280]{1,0:T(8,128)(2,1)S(1)}, bf16[16,1280]{1,0:T(8,128)(2,1)S(1)}, u32[]{:S(2)}, u32[]{:S(2)}) %collective-permute-start.3) | collective-permute-done | bytes 40992 | tf_op jit(solution)/shard_map/ppermute | solution.py:310
  58.7 1.5 %collective-permute-done.2.c_ref = bf16[16,1280]{1,0:T(8,128)(2,1)S(1)} collective-permute-done((bf16[16,1280]{1,0:T(8,128)(2,1)S(1)}, bf16[16,1280]{1,0:T(8,128)(2,1)S(1)}, u32[]{:S(2)}, u32[]{:S(2)}) %collective-permute-start.2) | collective-permute-done | bytes 40992 | tf_op jit(solution)/shard_map/ppermute | solution.py:310
  60.1 0.0 collective-permute-done.1.b_ref
  60.1 0.0 copy-done
  60.2 0.6 shard_map.97.own_ref
  60.7 1.7 %collective-permute-start.4 = (bf16[16,1280]{1,0:T(8,128)(2,1)S(1)}, bf16[16,1280]{1,0:T(8,128)(2,1)S(1)}, u32[]{:S(2)}, u32[]{:S(2)}) collective-permute-start(bf16[16,1280]{1,0:T(8,128)(2,1)S(1)} %shard_map.97.own_ref), channel_id=1, source_target_pairs={{0,2},{2,0},{1,3},{3,1},{4,6},{6,4},{5,7},{7,5},{8,10},{10,8},{9,1... | collective-permute-start | bytes 122888 | tf_op jit(solution)/shard_map/ppermute | solution.py:310
  62.5 0.1 pad_add_fusion.place_ref
  62.5 1.3 %collective-permute-done.4.far_ref = bf16[16,1280]{1,0:T(8,128)(2,1)S(1)} collective-permute-done((bf16[16,1280]{1,0:T(8,128)(2,1)S(1)}, bf16[16,1280]{1,0:T(8,128)(2,1)S(1)}, u32[]{:S(2)}, u32[]{:S(2)}) %collective-permute-start.4) | collective-permute-done | bytes 40992 | tf_op jit(solution)/shard_map/ppermute | solution.py:310
  63.8 1.7 %shard_map.98 = bf16[16,2,16,1280]{3,2,1,0:T(8,128)(2,1)} custom-call(s32[3]{0:T(128)S(1)} %pad_add_fusion.place_ref, bf16[16,1280]{1,0:T(8,128)(2,1)S(1)} %shard_map.97.own_ref, bf16[16,1280]{1,0:T(8,128)(2,1)S(1)} %collective-permute-done.4.far_ref), custom_call_target="tpu_custom_call" | custom-call | bytes 2097152 | tf_op jit(solution)/shard_map/pallas_call | solution.py:55
  65.5 0.0 all-to-all-done.2.in_ref
  65.5 6.5 %all-to-all-start.1 = ((bf16[16,2,16,1280]{3,2,1,0:T(8,128)(2,1)}), bf16[16,2,16,1280]{3,2,1,0:T(8,128)(2,1)S(1)}, u32[]{:S(2)}, u32[]{:S(2)}) async-start(bf16[16,2,16,1280]{3,2,1,0:T(8,128)(2,1)} %shard_map.98), calls=%async_computation.1 | async-start | bytes 2621440 | tf_op jit(solution)/shard_map/all_to_all | solution.py:366
  72.1 1.6 %shard_map.101 = (bf16[256,128]{1,0:T(8,128)(2,1)S(1)}, bf16[256,128]{1,0:T(8,128)(2,1)S(1)}, bf16[256,128]{1,0:T(8,128)(2,1)S(1)}, bf16[256,128]{1,0:T(8,128)(2,1)S(1)}) custom-call(s32[3]{0:T(128)S(1)} %pad_add_fusion.place_ref, bf16[32,5,16,128]{3,2,1,0:T(8,128)(2,1)S(1)} %all-to-all-done.2.in_ref), custom_call_target="tpu_custom_call" | custom-call | flops 1000000000 | bytes 2097152 | tf_op jit(solution)/shard_map/pallas_call | solution.py:55
  73.7 0.0 copy-start.1
  73.7 1.6 %collective-permute-start.6 = (bf16[256,128]{1,0:T(8,128)(2,1)S(1)}, bf16[256,128]{1,0:T(8,128)(2,1)S(1)}, u32[]{:S(2)}, u32[]{:S(2)}) collective-permute-start(bf16[256,128]{1,0:T(8,128)(2,1)S(1)} %get-tuple-element.27), channel_id=1, source_target_pairs={{0,4},{4,0},{8,12},{12,8},{1,5},{5,1},{9,13},{13,9},{2,6},{6,2},{1... | collective-permute-start | bytes 196616 | tf_op jit(solution)/shard_map/ppermute | solution.py:310
  75.3 2.2 %collective-permute-start.7 = (bf16[256,128]{1,0:T(8,128)(2,1)S(1)}, bf16[256,128]{1,0:T(8,128)(2,1)S(1)}, u32[]{:S(2)}, u32[]{:S(2)}) collective-permute-start(bf16[256,128]{1,0:T(8,128)(2,1)S(1)} %get-tuple-element.28), channel_id=1, source_target_pairs={{0,8},{4,12},{8,0},{12,4},{1,9},{5,13},{9,1},{13,5},{2,10},{6,14},... | collective-permute-start | bytes 196616 | tf_op jit(solution)/shard_map/ppermute | solution.py:310
  77.5 2.0 %collective-permute-start.8 = (bf16[256,128]{1,0:T(8,128)(2,1)S(1)}, bf16[256,128]{1,0:T(8,128)(2,1)S(1)}, u32[]{:S(2)}, u32[]{:S(2)}) collective-permute-start(bf16[256,128]{1,0:T(8,128)(2,1)S(1)} %get-tuple-element.29), channel_id=1, source_target_pairs={{0,12},{4,8},{8,4},{12,0},{1,13},{5,9},{9,5},{13,1},{2,14},{6,10},... | collective-permute-start | bytes 196616 | tf_op jit(solution)/shard_map/ppermute | solution.py:310
  79.4 0.0 collective-permute-done.6.b_ref
  79.4 3.0 %collective-permute-done.7.c_ref = bf16[256,128]{1,0:T(8,128)(2,1)S(1)} collective-permute-done((bf16[256,128]{1,0:T(8,128)(2,1)S(1)}, bf16[256,128]{1,0:T(8,128)(2,1)S(1)}, u32[]{:S(2)}, u32[]{:S(2)}) %collective-permute-start.7) | collective-permute-done | bytes 65568 | tf_op jit(solution)/shard_map/ppermute | solution.py:310
  82.5 0.9 collective-permute-done.8.d_ref
  83.4 2.6 %all-to-all-done.1.in_ref = bf16[16,2,16,1280]{3,2,1,0:T(8,128)(2,1)S(1)} async-done(((bf16[16,2,16,1280]{3,2,1,0:T(8,128)(2,1)}), bf16[16,2,16,1280]{3,2,1,0:T(8,128)(2,1)S(1)}, u32[]{:S(2)}, u32[]{:S(2)}) %all-to-all-start.1) | async-done | bytes 1310752 | tf_op jit(solution)/shard_map/all_to_all | solution.py:366
  85.9 7.2 %collective-permute-start.9 = (bf16[16,2,16,1280]{3,2,1,0:T(8,128)(2,1)S(1)}, bf16[16,2,16,1280]{3,2,1,0:T(8,128)(2,1)S(1)}, u32[]{:S(2)}, u32[]{:S(2)}) collective-permute-start(bf16[16,2,16,1280]{3,2,1,0:T(8,128)(2,1)S(1)} %all-to-all-done.1.in_ref), channel_id=1, source_target_pairs={{0,1},{1,0},{2,3},{3,2},{4,5},{5,4},{6,7},{7,6},{8,9},{9,8},{10,11... | collective-permute-start | bytes 3932168 | tf_op jit(solution)/shard_map/ppermute | solution.py:310
  93.1 1.2 %shard_map.102 = (bf16[512,2048]{1,0:T(8,128)(2,1)}, f32[2048,128]{1,0:T(8,128)}) custom-call(s32[1]{0:T(128)} %bitcast.core_ref, bf16[16,2,16,1280]{3,2,1,0:T(8,128)(2,1)S(1)} %all-to-all-done.1.in_ref), custom_call_target="tpu_custom_call" | custom-call | bytes 4194304 | tf_op jit(solution)/shard_map/pallas_call | solution.py:282
  94.4 0.0 copy-done.1
  94.4 0.7 shard_map.104
  95.1 0.7 collective-permute-done.9.in_ref
  95.8 1.2 %shard_map.103 = (bf16[512,2048]{1,0:T(8,128)(2,1)}, f32[2048,128]{1,0:T(8,128)}) custom-call(s32[1]{0:T(128)S(6)} %sub.7.core_ref, bf16[16,2,16,1280]{3,2,1,0:T(8,128)(2,1)S(1)} %collective-permute-done.9.in_ref, bf16[512,2048]{1,0:T(8,128)(2,1)} %get-tuple-element.31.refs_0_, ...), custom_call_target="tpu_custom_call", output_to_operand_aliasing={{0}: (2, {}), {1}: (3, {})} | custom-call | bytes 4194304 | tf_op jit(solution)/shard_map/pallas_call | solution.py:282
Async XLA Ops:
  8.2 6.2 %collective-permute-start = (bf16[16,2,16,1280]{3,2,1,0:T(8,128)(2,1)}, bf16[16,2,16,1280]{3,2,1,0:T(8,128)(2,1)S(1)}, u32[]{:S(2)}, u32[]{:S(2)}) collective-permute-start(bf16[16,2,16,1280]{3,2,1,0:T(8,128)(2,1)} %get-tuple-element.22), channel_id=1, source_target_pairs={{0,1},{1,0},{2,3},{3,2},{4,5},{5,4},{6,7},{7,6},{8,9},{9,8},{10,11... | collective-permute-start | bytes 3932168 | tf_op jit(solution)/shard_map/ppermute | solution.py:310
  15.5 6.8 %copy-start.2 = (s32[512,4]{0,1:T(4,128)S(1)}, s32[512,4]{0,1:T(4,128)}, u32[]{:S(2)}) copy-start(s32[512,4]{0,1:T(4,128)} %param.8) | copy-start | bytes 24580
  15.5 6.8 %copy-start.3 = (bf16[512,512]{1,0:T(8,128)(2,1)S(1)}, bf16[512,512]{1,0:T(8,128)(2,1)}, u32[]{:S(2)}) copy-start(bf16[512,512]{1,0:T(8,128)(2,1)} %get-tuple-element.23.grad_ref) | copy-start | bytes 1572868
  15.5 27.3 %all-to-all-start = ((bf16[32,16,1280]{2,1,0:T(8,128)(2,1)}), bf16[32,16,1280]{2,1,0:T(8,128)(2,1)S(1)}, u32[]{:S(2)}, u32[]{:S(2)}) async-start(bf16[32,16,1280]{2,1,0:T(8,128)(2,1)} %bitcast.9), calls=%async_computation | async-start | bytes 2621440 | tf_op jit(solution)/shard_map/all_to_all | solution.py:313
  26.2 1.9 %collective-permute-start.5 = (bf16[1040,128]{1,0:T(8,128)(2,1)S(1)}, bf16[1040,128]{1,0:T(8,128)(2,1)S(1)}, u32[]{:S(2)}, u32[]{:S(2)}) collective-permute-start(bf16[1040,128]{1,0:T(8,128)(2,1)S(1)} %get-tuple-element.25), channel_id=1, source_target_pairs={{0,1},{1,0},{2,3},{3,2},{4,5},{5,4},{6,7},{7,6},{8,9},{9,8},{10,11... | collective-permute-start | bytes 798728 | tf_op jit(solution)/shard_map/ppermute | solution.py:310
  29.1 31.1 %copy-start = (f32[4,512,128]{2,1,0:T(8,128)S(1)}, f32[4,512,128]{2,1,0:T(8,128)}, u32[]{:S(2)}) copy-start(f32[4,512,128]{2,1,0:T(8,128)} %param.12) | copy-start | bytes 3145732
  42.9 22.6 %all-to-all-start.2 = ((bf16[32,5,16,128]{3,2,1,0:T(8,128)(2,1)}), bf16[32,5,16,128]{3,2,1,0:T(8,128)(2,1)S(1)}, u32[]{:S(2)}, u32[]{:S(2)}) async-start(bf16[32,5,16,128]{3,2,1,0:T(8,128)(2,1)} %shard_map.100), calls=%async_computation.2 | async-start | bytes 1310720 | tf_op jit(solution)/shard_map/all_to_all | solution.py:313
  47.0 11.7 %collective-permute-start.3 = (bf16[16,1280]{1,0:T(8,128)(2,1)S(1)}, bf16[16,1280]{1,0:T(8,128)(2,1)S(1)}, u32[]{:S(2)}, u32[]{:S(2)}) collective-permute-start(bf16[16,1280]{1,0:T(8,128)(2,1)S(1)} %shard_map.96.a_ref), channel_id=1, source_target_pairs={{0,12},{4,8},{8,4},{12,0},{1,13},{5,9},{9,5},{13,1},{2,14},{6,10},... | collective-permute-start | bytes 122888 | tf_op jit(solution)/shard_map/ppermute | solution.py:310
  52.2 7.9 %collective-permute-start.2 = (bf16[16,1280]{1,0:T(8,128)(2,1)S(1)}, bf16[16,1280]{1,0:T(8,128)(2,1)S(1)}, u32[]{:S(2)}, u32[]{:S(2)}) collective-permute-start(bf16[16,1280]{1,0:T(8,128)(2,1)S(1)} %shard_map.96.a_ref), channel_id=1, source_target_pairs={{0,8},{4,12},{8,0},{12,4},{1,9},{5,13},{9,1},{13,5},{2,10},{6,14},... | collective-permute-start | bytes 122888 | tf_op jit(solution)/shard_map/ppermute | solution.py:310
  53.4 6.8 %collective-permute-start.1 = (bf16[16,1280]{1,0:T(8,128)(2,1)S(1)}, bf16[16,1280]{1,0:T(8,128)(2,1)S(1)}, u32[]{:S(2)}, u32[]{:S(2)}) collective-permute-start(bf16[16,1280]{1,0:T(8,128)(2,1)S(1)} %shard_map.96.a_ref), channel_id=1, source_target_pairs={{0,4},{4,0},{8,12},{12,8},{1,5},{5,1},{9,13},{13,9},{2,6},{6,2},{1... | collective-permute-start | bytes 122888 | tf_op jit(solution)/shard_map/ppermute | solution.py:310
  60.7 3.1 %collective-permute-start.4 = (bf16[16,1280]{1,0:T(8,128)(2,1)S(1)}, bf16[16,1280]{1,0:T(8,128)(2,1)S(1)}, u32[]{:S(2)}, u32[]{:S(2)}) collective-permute-start(bf16[16,1280]{1,0:T(8,128)(2,1)S(1)} %shard_map.97.own_ref), channel_id=1, source_target_pairs={{0,2},{2,0},{1,3},{3,1},{4,6},{6,4},{5,7},{7,5},{8,10},{10,8},{9,1... | collective-permute-start | bytes 122888 | tf_op jit(solution)/shard_map/ppermute | solution.py:310
  65.5 20.4 %all-to-all-start.1 = ((bf16[16,2,16,1280]{3,2,1,0:T(8,128)(2,1)}), bf16[16,2,16,1280]{3,2,1,0:T(8,128)(2,1)S(1)}, u32[]{:S(2)}, u32[]{:S(2)}) async-start(bf16[16,2,16,1280]{3,2,1,0:T(8,128)(2,1)} %shard_map.98), calls=%async_computation.1 | async-start | bytes 2621440 | tf_op jit(solution)/shard_map/all_to_all | solution.py:366
  73.7 20.7 %copy-start.1 = (f32[4,64,128]{2,1,0:T(8,128)S(1)}, f32[4,64,128]{2,1,0:T(8,128)}, u32[]{:S(2)}) copy-start(f32[4,64,128]{2,1,0:T(8,128)} %param.13) | copy-start | bytes 393220
  73.7 5.7 %collective-permute-start.6 = (bf16[256,128]{1,0:T(8,128)(2,1)S(1)}, bf16[256,128]{1,0:T(8,128)(2,1)S(1)}, u32[]{:S(2)}, u32[]{:S(2)}) collective-permute-start(bf16[256,128]{1,0:T(8,128)(2,1)S(1)} %get-tuple-element.27), channel_id=1, source_target_pairs={{0,4},{4,0},{8,12},{12,8},{1,5},{5,1},{9,13},{13,9},{2,6},{6,2},{1... | collective-permute-start | bytes 196616 | tf_op jit(solution)/shard_map/ppermute | solution.py:310
  75.3 7.2 %collective-permute-start.7 = (bf16[256,128]{1,0:T(8,128)(2,1)S(1)}, bf16[256,128]{1,0:T(8,128)(2,1)S(1)}, u32[]{:S(2)}, u32[]{:S(2)}) collective-permute-start(bf16[256,128]{1,0:T(8,128)(2,1)S(1)} %get-tuple-element.28), channel_id=1, source_target_pairs={{0,8},{4,12},{8,0},{12,4},{1,9},{5,13},{9,1},{13,5},{2,10},{6,14},... | collective-permute-start | bytes 196616 | tf_op jit(solution)/shard_map/ppermute | solution.py:310
  77.5 5.9 %collective-permute-start.8 = (bf16[256,128]{1,0:T(8,128)(2,1)S(1)}, bf16[256,128]{1,0:T(8,128)(2,1)S(1)}, u32[]{:S(2)}, u32[]{:S(2)}) collective-permute-start(bf16[256,128]{1,0:T(8,128)(2,1)S(1)} %get-tuple-element.29), channel_id=1, source_target_pairs={{0,12},{4,8},{8,4},{12,0},{1,13},{5,9},{9,5},{13,1},{2,14},{6,10},... | collective-permute-start | bytes 196616 | tf_op jit(solution)/shard_map/ppermute | solution.py:310
  85.9 9.9 %collective-permute-start.9 = (bf16[16,2,16,1280]{3,2,1,0:T(8,128)(2,1)S(1)}, bf16[16,2,16,1280]{3,2,1,0:T(8,128)(2,1)S(1)}, u32[]{:S(2)}, u32[]{:S(2)}) collective-permute-start(bf16[16,2,16,1280]{3,2,1,0:T(8,128)(2,1)S(1)} %all-to-all-done.1.in_ref), channel_id=1, source_target_pairs={{0,1},{1,0},{2,3},{3,2},{4,5},{5,4},{6,7},{7,6},{8,9},{9,8},{10,11... | collective-permute-start | bytes 3932168 | tf_op jit(solution)/shard_map/ppermute | solution.py:310

commit v3 on v2

--- a/solution.py
+++ b/solution.py
@@ -32,7 +32,6 @@
 BF = jnp.bfloat16
 F32 = jnp.float32
 MIB = 1024 * 1024
-AXES = ("node", "zq", "zp", "core")
 VMEM = pl.BlockSpec(memory_space=pltpu.VMEM)
 HBM = pl.BlockSpec(memory_space=pltpu.HBM)
 SMEM = pl.BlockSpec(memory_space=pltpu.SMEM)
@@ -64,8 +63,8 @@
 
 
 def backprop_kernel(
-    core_ref, x_hbm, ids_hbm, y_hbm, wh_hbm, wo_hbm, send_hbm, own_ref, grad_hbm,
-    slope_ref, pre_ref, xt_ref, x_ref, ids_ref, y_ref, wh_ref, wo_ref, send_ref, grad_ref, hit_ref, sems, out_sems,
+    core_ref, x_hbm, ids_hbm, y_hbm, wh_hbm, wo_hbm, send_hbm, own_ref, pre_ref, wh_ref, hit_ref,
+    slope_ref, xt_ref, x_ref, ids_ref, y_ref, wo_ref, send_ref, sems, out_sems,
 ):
     core = core_ref[0]
     step = 256
@@ -79,12 +78,6 @@
         for i, (src, dst) in enumerate(((x_hbm, x_ref), (wo_hbm, wo_ref), (ids_hbm, ids_ref), (y_hbm, y_ref)))
     ]
     stores = []
-
-    def store(src, dst):
-        copy = pltpu.make_async_copy(src, dst, out_sems.at[len(stores)])
-        copy.start()
-        stores.append(copy)
-
     for copy in (*small[1:], small[0], *loads):
         copy.start()
     for copy in small[1:]:
@@ -127,22 +120,23 @@
             term = dot(xt_ref[rows, :], pre).astype(BF)
             out_ref[:, part, :, at:at + step] = term.reshape(NODES, CHUNK, step)
         if at + step == PCOL:
-            store(send_ref.at[:, part, :, pl.ds(0, PCOL)], send_hbm.at[:, part, :, pl.ds(0, PCOL)])
+            copy = pltpu.make_async_copy(send_ref.at[:, part], send_hbm.at[:, part], out_sems.at[part])
+            copy.start()
+            stores.append(copy)
+    for copy in stores:
+        copy.wait()
+
+
+def hot_kernel(core_ref, pre_ref, wh_ref, hit_ref, send_ref, own_ref, grad_ref):
+    core = core_ref[0]
     grad_ref[...] = dot_nt(pre_ref[...], wh_ref[...]).astype(BF)
-    store(grad_ref, grad_hbm)
     for side, out_ref in ((1 - core, send_ref), (core, own_ref)):
         for t in range(ZP):
             table = side * 2 + t
-            onehot = hit_ref[table]
             grads = grad_ref[:, pl.ds(pl.multiple_of(table * E, E), E)]
-            total = dot(onehot, grads).astype(BF)
+            total = dot(hit_ref[table], grads).astype(BF)
             for b in range(2):
-                at = PCOL + b * E
-                out_ref[:, t, :, at:at + E] = total[b * HALF:(b + 1) * HALF].reshape(NODES, CHUNK, E)
-        if out_ref is send_ref:
-            store(send_ref.at[:, :, :, pl.ds(PCOL, 2 * E)], send_hbm.at[:, :, :, pl.ds(PCOL, 2 * E)])
-    for copy in stores:
-        copy.wait()
+                out_ref[:, t, :, b * E:(b + 1) * E] = total[b * HALF:(b + 1) * HALF].reshape(NODES, CHUNK, E)
 
 
 def pack_kernel(core_ref, ids_ref, grad_ref, send_ref, own_ref, rows_ref):
@@ -184,8 +178,27 @@
             out_ref[b * block:(b + 1) * block, :] = dot(member, rows_ref[...]).astype(BF)
 
 
-def add_kernel(a_ref, b_ref, out_ref):
-    out_ref[...] = a_ref[...] + b_ref[...]
+def add_part(a, b, at, held=None):
+    width = a.shape[-1]
+    rest = () if held is None else (held,)
+
+    def kernel(a_ref, b_ref, *refs):
+        out_hbm, sum_ref, sem = refs[-3:]
+        sum_ref[...] = a_ref[...] + b_ref[...]
+        copy = pltpu.make_async_copy(sum_ref, out_hbm.at[:, :, :, pl.ds(at, width)], sem)
+        copy.start()
+        copy.wait()
+
+    return pl.pallas_call(
+        kernel,
+        out_shape=pltpu.HBM((NODES, ZP, CHUNK, WIDE), BF),
+        in_specs=[VMEM] * 2 + [HBM] * len(rest),
+        out_specs=HBM,
+        scratch_shapes=[pltpu.VMEM(a.shape, BF), pltpu.SemaphoreType.DMA],
+        input_output_aliases={2: 0} if rest else {},
+        compiler_params=pltpu.CompilerParams(vmem_limit_bytes=8 * MIB),
+        cost_estimate=pl.CostEstimate(flops=0, bytes_accessed=2 * MIB, transcendentals=0),
+    )(a, b, *rest)
 
 
 def merge_kernel(core_ref, cold_ref, far_cold_ref, out_ref):
@@ -270,12 +283,14 @@
 
 def finish_kernel(core_ref, in_ref, *refs):
     w1_ref, hot_ref = refs[-2:]
-    for part in range(ZP):
-        w1_ref[:, part * PCOL:(part + 1) * PCOL] = in_ref[:, part, :, :PCOL].reshape(HALF, PCOL)
-        for b in range(2):
-            at = PCOL + b * E
-            hot = in_ref[:, part, :, at:at + E].reshape(HALF, E)
-            hot_ref[(2 * part + b) * HALF:(2 * part + b + 1) * HALF, :] = hot.astype(F32)
+    for n in range(NODES):
+        rows = slice(n * CHUNK, (n + 1) * CHUNK)
+        for part in range(ZP):
+            piece = in_ref[NODES - 1 - n, part]
+            w1_ref[rows, part * PCOL:(part + 1) * PCOL] = piece[:, :PCOL]
+            for b in range(2):
+                at = (2 * part + b) * HALF + n * CHUNK
+                hot_ref[at:at + CHUNK, :] = piece[:, PCOL + b * E:PCOL + (b + 1) * E].astype(F32)
 
 
 def finish(side, half, held=()):
@@ -298,7 +313,8 @@
 
 
 def on_device(pooled, lookups, converted, w_hidden, w_out, hot_accum, cold_accum):
-    node, zq, zp, core = (lax.axis_index(name) for name in AXES)
+    me = lax.axis_index("all")
+    node, zq, zp, core = me >> 4, (me >> 2) & 3, (me >> 1) & 1, me & 1
     ids = lookups.T
     core_arg = core.reshape(1)
     place = jnp.stack([node, zq, zp])
@@ -306,41 +322,61 @@
     def in_hbm(array):
         return pltpu.with_memory_space_constraint(array, pltpu.HBM)
 
-    def flip(array, axis, mask):
-        return lax.ppermute(array, axis, [(i, i ^ mask) for i in range(lax.axis_size(axis))])
-
-    def exchange(array):
-        return lax.all_to_all(array, ("node", "zp"), 0, 0, tiled=True)
-
+    def flip(array, mask):
+        return lax.ppermute(array, "all", [(i, i ^ mask) for i in range(OWNERS)])
+
+    def exchange(array, groups):
+        return lax.all_to_all(array, "all", 0, 0, axis_index_groups=groups, tiled=True)
+
+    with_pair = [
+        [n * LOCALS + q * 4 + p * 2 + c for n in range(NODES) for p in range(ZP)] for q in range(ZQ) for c in range(2)
+    ]
+    alone = [
+        [n * LOCALS + low for n in reversed(range(NODES))] for low in range(LOCALS)
+    ]
     halves = shape(NODES, ZP, CHUNK, WIDE)
-    send, own, grads = call(
+    half_w1, half_hot = (NODES, ZP, CHUNK, PCOL), (NODES, ZP, CHUNK, 2 * E)
+    w1_send, w1_own, pre, weights, hits = call(
         backprop_kernel,
-        (pltpu.HBM(halves.shape, BF), pltpu.VMEM(halves.shape, BF), pltpu.HBM((TOK, FEAT), BF)),
+        (
+            pltpu.HBM(half_w1, BF),
+            pltpu.VMEM(half_w1, BF),
+            pltpu.VMEM((TOK, HID), BF),
+            pltpu.VMEM((FEAT, HID), BF),
+            pltpu.VMEM((TABLES, HOT, TOK), BF),
+        ),
         (core_arg, *map(in_hbm, (pooled, ids, converted.reshape(1, TOK), w_hidden, w_out.reshape(HID // E, E)))),
         scalars=1,
         scratch=[
             pltpu.VMEM((TOK, HID), F32),
-            pltpu.VMEM((TOK, HID), BF),
             pltpu.VMEM((FEAT, TOK), BF),
             pltpu.VMEM((TOK, FEAT), BF),
             pltpu.VMEM((TABLES, TOK), jnp.int32),
             pltpu.VMEM((1, TOK), jnp.int32),
-            pltpu.VMEM((FEAT, HID), BF),
             pltpu.VMEM((HID // E, E), BF),
-            pltpu.VMEM((NODES, ZP, CHUNK, WIDE), BF),
-            pltpu.VMEM((TOK, FEAT), BF),
-            pltpu.VMEM((TABLES, HOT, TOK), BF),
+            pltpu.VMEM(half_w1, BF),
             pltpu.SemaphoreType.DMA((HID // 256 + 4,)),
-            pltpu.SemaphoreType.DMA((4,)),
+            pltpu.SemaphoreType.DMA((ZP,)),
         ],
         spec=HBM,
-        out_specs=(HBM, VMEM, HBM),
+        out_specs=(HBM, VMEM, VMEM, VMEM, VMEM),
         limit=24,
-        flops=4 * 10**9,
+        flops=3 * 10**9,
         size=8 * MIB,
     )
-    chip = call(add_kernel, halves, (own, flip(send, "core", 1)), size=3 * MIB)
-    parts = exchange(chip.reshape(GROUP, CHUNK, WIDE))
+    w1_far = flip(w1_send, 1)
+    hot_send, hot_own, grads = call(
+        hot_kernel,
+        (pltpu.VMEM(half_hot, BF), pltpu.VMEM(half_hot, BF), shape(TOK, FEAT)),
+        (core_arg, pre, weights, hits),
+        scalars=1,
+        flops=2 * 10**9,
+        size=6 * MIB,
+    )
+    hot_far = flip(hot_send, 1)
+    chip = add_part(w1_own, w1_far, 0)
+    chip = add_part(hot_own, hot_far, PCOL, chip)
+    parts = exchange(chip.reshape(GROUP, CHUNK, WIDE), with_pair)
     cold_send, cold_own = call(
         pack_kernel,
         (shape(SLOT_HALF + NODES, E), shape(SLOT_HALF + NODES, E)),
@@ -353,17 +389,17 @@
     slab = call(
         merge_kernel,
         shape(GROUP, SLAB, PAIR, E),
-        (core_arg, cold_own, flip(cold_send, "core", 1)),
+        (core_arg, cold_own, flip(cold_send, 1)),
         scalars=1,
         size=3 * MIB,
     )
     part = call(group_sum_kernel, shape(CHUNK, WIDE), (parts,), size=2 * MIB)
-    slab = exchange(slab)
-    quad = [part] + [flip(part, "zq", d) for d in range(1, ZQ)]
+    slab = exchange(slab, with_pair)
+    quad = [part] + [flip(part, 4 * d) for d in range(1, ZQ)]
     block = ((core * ZP + zp) * 2 * HALF + node * CHUNK) // CHUNK
     done = step(jnp.stack([block, block + HALF // CHUNK]), quad, hot_accum.reshape(TABLES * HOT, E))
-    whole = call(spread_kernel, halves, (place, done, flip(done, "zp", 1)), scalars=1, size=2 * MIB)
-    half = lax.all_to_all(whole, "node", 0, 0, tiled=True)
+    whole = call(spread_kernel, halves, (place, done, flip(done, 2)), scalars=1, size=2 * MIB)
+    half = exchange(whole, alone)
     cold = call(
         cold_dense_kernel,
         tuple(shape(TABLES * COLD_DEV, E) for _ in range(ZQ)),
@@ -372,7 +408,7 @@
         flops=10**9,
         size=2 * MIB,
     )
-    cold = [cold[0]] + [flip(cold[d], "zq", d) for d in range(1, ZQ)]
+    cold = [cold[0]] + [flip(cold[d], 4 * d) for d in range(1, ZQ)]
     half, cold = lax.optimization_barrier((half, cold))
     cold_step = call(
         cold_step_kernel,
@@ -380,14 +416,15 @@
         (cold_accum.reshape(TABLES * COLD_DEV, E), *cold),
         size=MIB,
     )
-    far = flip(half, "core", 1)
+    far = flip(half, 1)
     held = finish(core_arg, half)
     w1_grad, hot_step = finish(1 - core_arg, far, held)
     return (w1_grad, hot_step.reshape(TABLES, HOT, E), cold_step.reshape(TABLES, COLD_DEV, E))
 
 
 def solution(mesh):
-    mesh = Mesh(mesh.devices.reshape(NODES, ZQ, ZP, 2), AXES)
-    in_specs = (P(AXES, None), P(AXES, None), P(AXES), P(), P(), P(), P(None, AXES, None))
-    out_specs = (P(), P(), P(None, AXES, None))
+    mesh = Mesh(mesh.devices.reshape(OWNERS), ("all",))
+    rows = P("all")
+    in_specs = (rows, rows, rows, P(), P(), P(), P(None, "all"))
+    out_specs = (P(), P(), P(None, "all"))
     return jax.shard_map(on_device, mesh=mesh, in_specs=in_specs, out_specs=out_specs, check_vma=False)

time: 97.4 us -> 94.5 us (0.970)
  waiting for transfers between devices: 31.8 us -> 28.5 us
  Pallas kernels: 20.8 us -> 21.8 us
    all_to_all x3, waiting for transfers between devices: 16.4 us -> 14.1 us  [exchange(): lax.all_to_all(array, 'all', 0, 0, axis_index_groups=groups, tiled=True)]
    ppermute x10 -> x11, starting transfers between devices: 26.3 us -> 24.2 us  [flip(): return lax.ppermute(array, 'all', [(i, i ^ mask) for i in range(OWNERS)])]
    pallas_call x0 -> x2, Pallas kernels: none -> 1.82 us  [add_part(): pl.pallas_call(kernel, out_shape=pltpu.HBM((NODES, ZP, CHUNK, WIDE), BF),...]
    all_to_all x3, starting transfers between devices: 17.2 us -> 18.6 us  [exchange(): lax.all_to_all(array, 'all', 0, 0, axis_index_groups=groups, tiled=True)]
    ppermute x10 -> x11, waiting for transfers between devices: 15.4 us -> 14.4 us  [flip(): return lax.ppermute(array, 'all', [(i, i ^ mask) for i in range(OWNERS)])]
  transfers between devices with their start and end apart: 13 -> 14, of which waited for: 10 -> 9; matrix products, arithmetic and copies ran while one was open for 0% -> 0% of each run, Pallas kernels for 11% -> 15%
where the time goes in v3:
time: 94.5 us; the launch traced here: 94.1 us
  starting transfers between devices  42.8 us (45%)
  waiting for transfers between devices  28.5 us (30%)
  Pallas kernels  21.8 us (23%)
    ppermute x11, starting transfers between devices, flip(): return lax.ppermute(array, 'all', [(i, i ^ mask) for i in range(OWNERS)])  24.2 us
    all_to_all x3, starting transfers between devices, exchange(): lax.all_to_all(array, 'all', 0, 0, axis_index_groups=groups, tiled=True)  18.6 us
    pallas_call x8, Pallas kernels, call(): pl.pallas_call(kernel, out_shape=out_shape, in_specs=[SMEM] * scalars + [...  16.9 us
    ppermute x11, waiting for transfers between devices, flip(): return lax.ppermute(array, 'all', [(i, i ^ mask) for i in range(OWNERS)])  14.4 us
    all_to_all x3, waiting for transfers between devices, exchange(): lax.all_to_all(array, 'all', 0, 0, axis_index_groups=groups, tiled=True)  14.1 us
    pallas_call x2, Pallas kernels, finish(): pl.pallas_call(finish_kernel, out_shape=(shape(FEAT, HID), shape(TABLES *...  2.48 us
  transfers between devices with their start and end apart: 14, of which 9 were waited for; matrix products, arithmetic and copies ran while one was open for 0% of the time, Pallas kernels for 15%

profile of v3, /device:TPU:1, one launch (start us, length us, event | category | flops | bytes accessed | tf_op | source)
XLA Modules:
  0.0 94.1 jit_solution(15640761318111040857)
XLA Ops:
  0.6 5.9 %shard_map.94 = (bf16[16,2,16,1024]{3,2,1,0:T(8,128)(2,1)}, bf16[16,2,16,1024]{3,2,1,0:T(8,128)(2,1)S(1)}, bf16[512,2048]{1,0:T(8,128)(2,1)S(1)}, bf16[512,2048]{1,0:T(8,128)(2,1)S(1)}, bf16[4,512,512]{2,1,0:T(8,128)(2,1)S(1)}) custom-call(s32[1]{0:T(128)} %bitcast.core_ref, bf16[512,512]{1,0:T(8,128)(2,1)} %x_hbm.1, s32[4,512]{1,0:T(4,128)} %bitcast.17, ...), custom_call_target="tpu_custom_call" | custom-call | flops 3000000000 | bytes 8388608 | tf_op jit(solution)/shard_map/pallas_call | solution.py:54
  6.5 3.3 %collective-permute-start.1 = (bf16[16,2,16,1024]{3,2,1,0:T(8,128)(2,1)}, bf16[16,2,16,1024]{3,2,1,0:T(8,128)(2,1)S(1)}, u32[]{:S(2)}, u32[]{:S(2)}) collective-permute-start(bf16[16,2,16,1024]{3,2,1,0:T(8,128)(2,1)} %get-tuple-element.32), channel_id=1, source_target_pairs={{0,1},{1,0},{2,3},{3,2},{4,5},{5,4},{6,7},{7,6},{8,9},{9,8},{10,11... | collective-permute-start | bytes 3145736 | tf_op jit(solution)/shard_map/ppermute | solution.py:326
  9.9 2.0 %shard_map.95 = (bf16[16,2,16,256]{3,2,1,0:T(8,128)(2,1)S(1)}, bf16[16,2,16,256]{3,2,1,0:T(8,128)(2,1)S(1)}, bf16[512,512]{1,0:T(8,128)(2,1)S(1)}) custom-call(s32[1]{0:T(128)} %bitcast.core_ref, bf16[512,2048]{1,0:T(8,128)(2,1)S(1)} %get-tuple-element.26.pre_ref, bf16[512,2048]{1,0:T(8,128)(2,1)S(1)} %get-tuple-element.27.wh_ref, ...), custom_call_target="tpu_custom_call" | custom-call | flops 2000000000 | bytes 6291456 | tf_op jit(solution)/shard_map/pallas_call | solution.py:54
  11.9 0.1 collective-permute-start
  12.0 0.4 collective-permute-done.1.b_ref
  12.4 1.1 %shard_map.96.refs_0_ = bf16[16,2,16,1280]{3,2,1,0:T(8,128)(2,1)} custom-call(bf16[16,2,16,1024]{3,2,1,0:T(8,128)(2,1)S(1)} %get-tuple-element.31.a_ref, bf16[16,2,16,1024]{3,2,1,0:T(8,128)(2,1)S(1)} %collective-permute-done.1.b_ref), custom_call_target="tpu_custom_call" | custom-call | bytes 2097152 | tf_op jit(solution)/shard_map/pallas_call | solution.py:192
  13.4 0.0 collective-permute-done.b_ref
  13.5 0.7 shard_map.97
  14.2 0.0 copy-start.2
  14.2 6.7 %all-to-all-start = ((bf16[32,16,1280]{2,1,0:T(8,128)(2,1)}), bf16[32,16,1280]{2,1,0:T(8,128)(2,1)S(1)}, u32[]{:S(2)}, u32[]{:S(2)}) async-start(bf16[32,16,1280]{2,1,0:T(8,128)(2,1)} %bitcast.19), calls=%async_computation | async-start | bytes 2621440 | tf_op jit(solution)/shard_map/all_to_all | solution.py:329
  20.9 0.0 copy-done.2
  20.9 3.9 %shard_map.101 = (bf16[1040,128]{1,0:T(8,128)(2,1)S(1)}, bf16[1040,128]{1,0:T(8,128)(2,1)S(1)}) custom-call(s32[1]{0:T(128)} %bitcast.core_ref, s32[4,512]{1,0:T(4,128)S(1)} %bitcast.18, bf16[512,512]{1,0:T(8,128)(2,1)S(1)} %get-tuple-element.33.grad_ref), custom_call_target="tpu_custom_call" | custom-call | flops 6000000000 | bytes 8388608 | tf_op jit(solution)/shard_map/pallas_call | solution.py:54
  24.8 0.0 copy-start
  24.8 0.7 collective-permute-start.6
  25.5 1.2 %collective-permute-done.6.far_cold_ref = bf16[1040,128]{1,0:T(8,128)(2,1)S(1)} collective-permute-done((bf16[1040,128]{1,0:T(8,128)(2,1)S(1)}, bf16[1040,128]{1,0:T(8,128)(2,1)S(1)}, u32[]{:S(2)}, u32[]{:S(2)}) %collective-permute-start.6) | collective-permute-done | bytes 266272 | tf_op jit(solution)/shard_map/ppermute | solution.py:326
  26.7 0.9 shard_map.102
  27.6 13.8 %all-to-all-done.in_ref = bf16[32,16,1280]{2,1,0:T(8,128)(2,1)S(1)} async-done(((bf16[32,16,1280]{2,1,0:T(8,128)(2,1)}), bf16[32,16,1280]{2,1,0:T(8,128)(2,1)S(1)}, u32[]{:S(2)}, u32[]{:S(2)}) %all-to-all-start) | async-done | bytes 1310752 | tf_op jit(solution)/shard_map/all_to_all | solution.py:329
  41.5 3.9 %all-to-all-start.2 = ((bf16[32,5,16,128]{3,2,1,0:T(8,128)(2,1)}), bf16[32,5,16,128]{3,2,1,0:T(8,128)(2,1)S(1)}, u32[]{:S(2)}, u32[]{:S(2)}) async-start(bf16[32,5,16,128]{3,2,1,0:T(8,128)(2,1)} %shard_map.102), calls=%async_computation.2 | async-start | bytes 1310720 | tf_op jit(solution)/shard_map/all_to_all | solution.py:329
  45.4 0.2 shard_map.98.a_ref
  45.6 3.3 %collective-permute-start.2 = (bf16[16,1280]{1,0:T(8,128)(2,1)S(1)}, bf16[16,1280]{1,0:T(8,128)(2,1)S(1)}, u32[]{:S(2)}, u32[]{:S(2)}) collective-permute-start(bf16[16,1280]{1,0:T(8,128)(2,1)S(1)} %shard_map.98.a_ref), channel_id=1, source_target_pairs={{0,4},{1,5},{2,6},{3,7},{4,0},{5,1},{6,2},{7,3},{8,12},{9,13},{10,... | collective-permute-start | bytes 122888 | tf_op jit(solution)/shard_map/ppermute | solution.py:326
  48.9 4.2 %collective-permute-start.3 = (bf16[16,1280]{1,0:T(8,128)(2,1)S(1)}, bf16[16,1280]{1,0:T(8,128)(2,1)S(1)}, u32[]{:S(2)}, u32[]{:S(2)}) collective-permute-start(bf16[16,1280]{1,0:T(8,128)(2,1)S(1)} %shard_map.98.a_ref), channel_id=1, source_target_pairs={{0,8},{1,9},{2,10},{3,11},{4,12},{5,13},{6,14},{7,15},{8,0},{9,1},... | collective-permute-start | bytes 122888 | tf_op jit(solution)/shard_map/ppermute | solution.py:326
  53.1 0.0 collective-permute-start.4
  53.1 0.1 pad_add_fusion.1.block_ref
  53.2 0.0 collective-permute-done.2.b_ref
  53.2 6.5 %collective-permute-done.3.c_ref = bf16[16,1280]{1,0:T(8,128)(2,1)S(1)} collective-permute-done((bf16[16,1280]{1,0:T(8,128)(2,1)S(1)}, bf16[16,1280]{1,0:T(8,128)(2,1)S(1)}, u32[]{:S(2)}, u32[]{:S(2)}) %collective-permute-start.3) | collective-permute-done | bytes 40992 | tf_op jit(solution)/shard_map/ppermute | solution.py:326
  59.6 0.0 collective-permute-done.4.d_ref
  59.6 0.0 copy-done
  59.6 0.6 shard_map.99.own_ref
  60.2 0.6 collective-permute-start.5
  60.8 0.1 pad_add_fusion.place_ref
  60.9 2.2 %collective-permute-done.5.far_ref = bf16[16,1280]{1,0:T(8,128)(2,1)S(1)} collective-permute-done((bf16[16,1280]{1,0:T(8,128)(2,1)S(1)}, bf16[16,1280]{1,0:T(8,128)(2,1)S(1)}, u32[]{:S(2)}, u32[]{:S(2)}) %collective-permute-start.5) | collective-permute-done | bytes 40992 | tf_op jit(solution)/shard_map/ppermute | solution.py:326
  63.2 1.7 %shard_map.100 = bf16[16,2,16,1280]{3,2,1,0:T(8,128)(2,1)} custom-call(s32[3]{0:T(128)S(1)} %pad_add_fusion.place_ref, bf16[16,1280]{1,0:T(8,128)(2,1)S(1)} %shard_map.99.own_ref, bf16[16,1280]{1,0:T(8,128)(2,1)S(1)} %collective-permute-done.5.far_ref), custom_call_target="tpu_custom_call" | custom-call | bytes 2097152 | tf_op jit(solution)/shard_map/pallas_call | solution.py:54
  64.8 0.0 all-to-all-done.2.in_ref
  64.9 8.1 %all-to-all-start.1 = ((bf16[16,2,16,1280]{3,2,1,0:T(8,128)(2,1)}), bf16[16,2,16,1280]{3,2,1,0:T(8,128)(2,1)S(1)}, u32[]{:S(2)}, u32[]{:S(2)}) async-start(bf16[16,2,16,1280]{3,2,1,0:T(8,128)(2,1)} %shard_map.100), calls=%async_computation.1 | async-start | bytes 2621440 | tf_op jit(solution)/shard_map/all_to_all | solution.py:329
  72.9 0.0 copy-start.1
  72.9 1.6 %shard_map.103 = (bf16[256,128]{1,0:T(8,128)(2,1)S(1)}, bf16[256,128]{1,0:T(8,128)(2,1)S(1)}, bf16[256,128]{1,0:T(8,128)(2,1)S(1)}, bf16[256,128]{1,0:T(8,128)(2,1)S(1)}) custom-call(s32[3]{0:T(128)S(1)} %pad_add_fusion.place_ref, bf16[32,5,16,128]{3,2,1,0:T(8,128)(2,1)S(1)} %all-to-all-done.2.in_ref), custom_call_target="tpu_custom_call" | custom-call | flops 1000000000 | bytes 2097152 | tf_op jit(solution)/shard_map/pallas_call | solution.py:54
  74.6 1.0 %collective-permute-start.7 = (bf16[256,128]{1,0:T(8,128)(2,1)S(1)}, bf16[256,128]{1,0:T(8,128)(2,1)S(1)}, u32[]{:S(2)}, u32[]{:S(2)}) collective-permute-start(bf16[256,128]{1,0:T(8,128)(2,1)S(1)} %get-tuple-element.37), channel_id=1, source_target_pairs={{0,4},{1,5},{2,6},{3,7},{4,0},{5,1},{6,2},{7,3},{8,12},{9,13},{10,... | collective-permute-start | bytes 196616 | tf_op jit(solution)/shard_map/ppermute | solution.py:326
  75.6 1.9 %collective-permute-start.8 = (bf16[256,128]{1,0:T(8,128)(2,1)S(1)}, bf16[256,128]{1,0:T(8,128)(2,1)S(1)}, u32[]{:S(2)}, u32[]{:S(2)}) collective-permute-start(bf16[256,128]{1,0:T(8,128)(2,1)S(1)} %get-tuple-element.38), channel_id=1, source_target_pairs={{0,8},{1,9},{2,10},{3,11},{4,12},{5,13},{6,14},{7,15},{8,0},{9,1},... | collective-permute-start | bytes 196616 | tf_op jit(solution)/shard_map/ppermute | solution.py:326
  77.4 2.9 %collective-permute-start.9 = (bf16[256,128]{1,0:T(8,128)(2,1)S(1)}, bf16[256,128]{1,0:T(8,128)(2,1)S(1)}, u32[]{:S(2)}, u32[]{:S(2)}) collective-permute-start(bf16[256,128]{1,0:T(8,128)(2,1)S(1)} %get-tuple-element.39), channel_id=1, source_target_pairs={{0,12},{1,13},{2,14},{3,15},{4,8},{5,9},{6,10},{7,11},{8,4},{9,5},... | collective-permute-start | bytes 196616 | tf_op jit(solution)/shard_map/ppermute | solution.py:326
  80.3 0.0 collective-permute-done.7.b_ref
  80.3 2.5 %collective-permute-done.8.c_ref = bf16[256,128]{1,0:T(8,128)(2,1)S(1)} collective-permute-done((bf16[256,128]{1,0:T(8,128)(2,1)S(1)}, bf16[256,128]{1,0:T(8,128)(2,1)S(1)}, u32[]{:S(2)}, u32[]{:S(2)}) %collective-permute-start.8) | collective-permute-done | bytes 65568 | tf_op jit(solution)/shard_map/ppermute | solution.py:326
  82.8 0.9 collective-permute-done.9.d_ref
  83.7 0.3 all-to-all-done.1.in_ref
  84.0 6.2 %collective-permute-start.10 = (bf16[16,2,16,1280]{3,2,1,0:T(8,128)(2,1)S(1)}, bf16[16,2,16,1280]{3,2,1,0:T(8,128)(2,1)S(1)}, u32[]{:S(2)}, u32[]{:S(2)}) collective-permute-start(bf16[16,2,16,1280]{3,2,1,0:T(8,128)(2,1)S(1)} %all-to-all-done.1.in_ref), channel_id=1, source_target_pairs={{0,1},{1,0},{2,3},{3,2},{4,5},{5,4},{6,7},{7,6},{8,9},{9,8},{10,11... | collective-permute-start | bytes 3932168 | tf_op jit(solution)/shard_map/ppermute | solution.py:326
  90.2 1.2 %shard_map.104 = (bf16[512,2048]{1,0:T(8,128)(2,1)}, f32[2048,128]{1,0:T(8,128)}) custom-call(s32[1]{0:T(128)} %bitcast.core_ref, bf16[16,2,16,1280]{3,2,1,0:T(8,128)(2,1)S(1)} %all-to-all-done.1.in_ref), custom_call_target="tpu_custom_call" | custom-call | bytes 4194304 | tf_op jit(solution)/shard_map/pallas_call | solution.py:297
  91.4 0.0 copy-done.1
  91.4 0.7 shard_map.106
  92.1 0.7 collective-permute-done.10.in_ref
  92.8 1.2 %shard_map.105 = (bf16[512,2048]{1,0:T(8,128)(2,1)}, f32[2048,128]{1,0:T(8,128)}) custom-call(s32[1]{0:T(128)S(6)} %sub.7.core_ref, bf16[16,2,16,1280]{3,2,1,0:T(8,128)(2,1)S(1)} %collective-permute-done.10.in_ref, bf16[512,2048]{1,0:T(8,128)(2,1)} %get-tuple-element.41.refs_0_, ...), custom_call_target="tpu_custom_call", output_to_operand_aliasing={{0}: (2, {}), {1}: (3, {})} | custom-call | bytes 4194304 | tf_op jit(solution)/shard_map/pallas_call | solution.py:297
Async XLA Ops:
  6.5 5.8 %collective-permute-start.1 = (bf16[16,2,16,1024]{3,2,1,0:T(8,128)(2,1)}, bf16[16,2,16,1024]{3,2,1,0:T(8,128)(2,1)S(1)}, u32[]{:S(2)}, u32[]{:S(2)}) collective-permute-start(bf16[16,2,16,1024]{3,2,1,0:T(8,128)(2,1)} %get-tuple-element.32), channel_id=1, source_target_pairs={{0,1},{1,0},{2,3},{3,2},{4,5},{5,4},{6,7},{7,6},{8,9},{9,8},{10,11... | collective-permute-start | bytes 3145736 | tf_op jit(solution)/shard_map/ppermute | solution.py:326
  11.9 1.6 %collective-permute-start = (bf16[16,2,16,256]{3,2,1,0:T(8,128)(2,1)S(1)}, bf16[16,2,16,256]{3,2,1,0:T(8,128)(2,1)S(1)}, u32[]{:S(2)}, u32[]{:S(2)}) collective-permute-start(bf16[16,2,16,256]{3,2,1,0:T(8,128)(2,1)S(1)} %get-tuple-element.30), channel_id=1, source_target_pairs={{0,1},{1,0},{2,3},{3,2},{4,5},{5,4},{6,7},{7,6},{8,9},{9,8},{10,11... | collective-permute-start | bytes 786440 | tf_op jit(solution)/shard_map/ppermute | solution.py:326
  14.2 6.7 %copy-start.2 = (s32[512,4]{0,1:T(4,128)S(1)}, s32[512,4]{0,1:T(4,128)}, u32[]{:S(2)}) copy-start(s32[512,4]{0,1:T(4,128)} %param.8) | copy-start | bytes 24580
  14.2 27.2 %all-to-all-start = ((bf16[32,16,1280]{2,1,0:T(8,128)(2,1)}), bf16[32,16,1280]{2,1,0:T(8,128)(2,1)S(1)}, u32[]{:S(2)}, u32[]{:S(2)}) async-start(bf16[32,16,1280]{2,1,0:T(8,128)(2,1)} %bitcast.19), calls=%async_computation | async-start | bytes 2621440 | tf_op jit(solution)/shard_map/all_to_all | solution.py:329
  24.8 34.9 %copy-start = (f32[4,512,128]{2,1,0:T(8,128)S(1)}, f32[4,512,128]{2,1,0:T(8,128)}, u32[]{:S(2)}) copy-start(f32[4,512,128]{2,1,0:T(8,128)} %param.12) | copy-start | bytes 3145732
  24.8 1.9 %collective-permute-start.6 = (bf16[1040,128]{1,0:T(8,128)(2,1)S(1)}, bf16[1040,128]{1,0:T(8,128)(2,1)S(1)}, u32[]{:S(2)}, u32[]{:S(2)}) collective-permute-start(bf16[1040,128]{1,0:T(8,128)(2,1)S(1)} %get-tuple-element.35), channel_id=1, source_target_pairs={{0,1},{1,0},{2,3},{3,2},{4,5},{5,4},{6,7},{7,6},{8,9},{9,8},{10,11... | collective-permute-start | bytes 798728 | tf_op jit(solution)/shard_map/ppermute | solution.py:326
  41.5 23.4 %all-to-all-start.2 = ((bf16[32,5,16,128]{3,2,1,0:T(8,128)(2,1)}), bf16[32,5,16,128]{3,2,1,0:T(8,128)(2,1)S(1)}, u32[]{:S(2)}, u32[]{:S(2)}) async-start(bf16[32,5,16,128]{3,2,1,0:T(8,128)(2,1)} %shard_map.102), calls=%async_computation.2 | async-start | bytes 1310720 | tf_op jit(solution)/shard_map/all_to_all | solution.py:329
  45.6 7.6 %collective-permute-start.2 = (bf16[16,1280]{1,0:T(8,128)(2,1)S(1)}, bf16[16,1280]{1,0:T(8,128)(2,1)S(1)}, u32[]{:S(2)}, u32[]{:S(2)}) collective-permute-start(bf16[16,1280]{1,0:T(8,128)(2,1)S(1)} %shard_map.98.a_ref), channel_id=1, source_target_pairs={{0,4},{1,5},{2,6},{3,7},{4,0},{5,1},{6,2},{7,3},{8,12},{9,13},{10,... | collective-permute-start | bytes 122888 | tf_op jit(solution)/shard_map/ppermute | solution.py:326
  48.9 10.8 %collective-permute-start.3 = (bf16[16,1280]{1,0:T(8,128)(2,1)S(1)}, bf16[16,1280]{1,0:T(8,128)(2,1)S(1)}, u32[]{:S(2)}, u32[]{:S(2)}) collective-permute-start(bf16[16,1280]{1,0:T(8,128)(2,1)S(1)} %shard_map.98.a_ref), channel_id=1, source_target_pairs={{0,8},{1,9},{2,10},{3,11},{4,12},{5,13},{6,14},{7,15},{8,0},{9,1},... | collective-permute-start | bytes 122888 | tf_op jit(solution)/shard_map/ppermute | solution.py:326
  53.1 6.6 %collective-permute-start.4 = (bf16[16,1280]{1,0:T(8,128)(2,1)S(1)}, bf16[16,1280]{1,0:T(8,128)(2,1)S(1)}, u32[]{:S(2)}, u32[]{:S(2)}) collective-permute-start(bf16[16,1280]{1,0:T(8,128)(2,1)S(1)} %shard_map.98.a_ref), channel_id=1, source_target_pairs={{0,12},{1,13},{2,14},{3,15},{4,8},{5,9},{6,10},{7,11},{8,4},{9,5},... | collective-permute-start | bytes 122888 | tf_op jit(solution)/shard_map/ppermute | solution.py:326
  60.2 2.9 %collective-permute-start.5 = (bf16[16,1280]{1,0:T(8,128)(2,1)S(1)}, bf16[16,1280]{1,0:T(8,128)(2,1)S(1)}, u32[]{:S(2)}, u32[]{:S(2)}) collective-permute-start(bf16[16,1280]{1,0:T(8,128)(2,1)S(1)} %shard_map.99.own_ref), channel_id=1, source_target_pairs={{0,2},{1,3},{2,0},{3,1},{4,6},{5,7},{6,4},{7,5},{8,10},{9,11},{10,... | collective-permute-start | bytes 122888 | tf_op jit(solution)/shard_map/ppermute | solution.py:326
  64.9 19.1 %all-to-all-start.1 = ((bf16[16,2,16,1280]{3,2,1,0:T(8,128)(2,1)}), bf16[16,2,16,1280]{3,2,1,0:T(8,128)(2,1)S(1)}, u32[]{:S(2)}, u32[]{:S(2)}) async-start(bf16[16,2,16,1280]{3,2,1,0:T(8,128)(2,1)} %shard_map.100), calls=%async_computation.1 | async-start | bytes 2621440 | tf_op jit(solution)/shard_map/all_to_all | solution.py:329
  72.9 18.5 %copy-start.1 = (f32[4,64,128]{2,1,0:T(8,128)S(1)}, f32[4,64,128]{2,1,0:T(8,128)}, u32[]{:S(2)}) copy-start(f32[4,64,128]{2,1,0:T(8,128)} %param.13) | copy-start | bytes 393220
  74.6 5.7 %collective-permute-start.7 = (bf16[256,128]{1,0:T(8,128)(2,1)S(1)}, bf16[256,128]{1,0:T(8,128)(2,1)S(1)}, u32[]{:S(2)}, u32[]{:S(2)}) collective-permute-start(bf16[256,128]{1,0:T(8,128)(2,1)S(1)} %get-tuple-element.37), channel_id=1, source_target_pairs={{0,4},{1,5},{2,6},{3,7},{4,0},{5,1},{6,2},{7,3},{8,12},{9,13},{10,... | collective-permute-start | bytes 196616 | tf_op jit(solution)/shard_map/ppermute | solution.py:326
  75.6 7.2 %collective-permute-start.8 = (bf16[256,128]{1,0:T(8,128)(2,1)S(1)}, bf16[256,128]{1,0:T(8,128)(2,1)S(1)}, u32[]{:S(2)}, u32[]{:S(2)}) collective-permute-start(bf16[256,128]{1,0:T(8,128)(2,1)S(1)} %get-tuple-element.38), channel_id=1, source_target_pairs={{0,8},{1,9},{2,10},{3,11},{4,12},{5,13},{6,14},{7,15},{8,0},{9,1},... | collective-permute-start | bytes 196616 | tf_op jit(solution)/shard_map/ppermute | solution.py:326
  77.4 6.2 %collective-permute-start.9 = (bf16[256,128]{1,0:T(8,128)(2,1)S(1)}, bf16[256,128]{1,0:T(8,128)(2,1)S(1)}, u32[]{:S(2)}, u32[]{:S(2)}) collective-permute-start(bf16[256,128]{1,0:T(8,128)(2,1)S(1)} %get-tuple-element.39), channel_id=1, source_target_pairs={{0,12},{1,13},{2,14},{3,15},{4,8},{5,9},{6,10},{7,11},{8,4},{9,5},... | collective-permute-start | bytes 196616 | tf_op jit(solution)/shard_map/ppermute | solution.py:326
  84.0 8.9 %collective-permute-start.10 = (bf16[16,2,16,1280]{3,2,1,0:T(8,128)(2,1)S(1)}, bf16[16,2,16,1280]{3,2,1,0:T(8,128)(2,1)S(1)}, u32[]{:S(2)}, u32[]{:S(2)}) collective-permute-start(bf16[16,2,16,1280]{3,2,1,0:T(8,128)(2,1)S(1)} %all-to-all-done.1.in_ref), channel_id=1, source_target_pairs={{0,1},{1,0},{2,3},{3,2},{4,5},{5,4},{6,7},{7,6},{8,9},{9,8},{10,11... | collective-permute-start | bytes 3932168 | tf_op jit(solution)/shard_map/ppermute | solution.py:326

commit v4 on v3

--- a/solution.py
+++ b/solution.py
@@ -220,38 +220,55 @@
     out_ref[...] = total.astype(BF)
 
 
-def step_kernel(block_ref, a_ref, b_ref, c_ref, d_ref, accum0_ref, accum1_ref, out_ref):
-    total = (a_ref[...].astype(F32) + b_ref[...].astype(F32)) + (c_ref[...].astype(F32) + d_ref[...].astype(F32))
-    hot = total[:, PCOL:]
-    accum = jnp.concatenate([accum0_ref[...], accum1_ref[...]], axis=1)
-    stepped = hot / jnp.sqrt(accum + hot * hot)
-    out_ref[...] = jnp.concatenate([total[:, :PCOL], stepped], axis=1).astype(BF)
-
-
-def spread_kernel(place_ref, own_ref, far_ref, out_ref):
-    zp = place_ref[2]
-    own, far = own_ref[...], far_ref[...]
-    for n in range(NODES):
-        out_ref[n, zp] = own
-        out_ref[n, 1 - zp] = far
-
-
-def step(blocks, parts, accum):
+def pick_kernel(at_ref, low_ref, high_ref, out_ref):
+    out_ref[:, :E] = low_ref[...]
+    out_ref[:, E:] = high_ref[...]
+
+
+def pick(blocks, accum):
     return pl.pallas_call(
-        step_kernel,
-        out_shape=shape(CHUNK, WIDE),
+        pick_kernel,
+        out_shape=pltpu.VMEM((CHUNK, 2 * E), F32),
         grid_spec=pltpu.PrefetchScalarGridSpec(
             num_scalar_prefetch=1,
             grid=(1,),
-            in_specs=[VMEM] * ZQ + [
+            in_specs=[
                 pl.BlockSpec((CHUNK, E), lambda i, at: (at[0], 0)),
                 pl.BlockSpec((CHUNK, E), lambda i, at: (at[1], 0)),
             ],
             out_specs=VMEM,
         ),
-        compiler_params=pltpu.CompilerParams(vmem_limit_bytes=16 * MIB),
+    )(blocks, accum, accum)
+
+
+def step_kernel(a_ref, b_ref, c_ref, d_ref, accum_ref, out_ref):
+    total = (a_ref[...].astype(F32) + b_ref[...].astype(F32)) + (c_ref[...].astype(F32) + d_ref[...].astype(F32))
+    hot = total[:, PCOL:]
+    out_ref[:, :PCOL] = total[:, :PCOL].astype(BF)
+    out_ref[:, PCOL:] = (hot / jnp.sqrt(accum_ref[...] + hot * hot)).astype(BF)
+
+
+def spread_kernel(part_ref, in_ref, *refs):
+    out_hbm, sems = refs[-2:]
+    part = part_ref[0]
+    copies = [pltpu.make_async_copy(in_ref, out_hbm.at[n, part], sems.at[n]) for n in range(NODES)]
+    for copy in copies:
+        copy.start()
+    for copy in copies:
+        copy.wait()
+
+
+def spread(part, chunk, held=()):
+    return pl.pallas_call(
+        spread_kernel,
+        out_shape=pltpu.HBM((NODES, ZP, CHUNK, WIDE), BF),
+        in_specs=[SMEM, VMEM] + [HBM] * len(held),
+        out_specs=HBM,
+        scratch_shapes=[pltpu.SemaphoreType.DMA((NODES,))],
+        input_output_aliases={2: 0} if held else {},
+        compiler_params=pltpu.CompilerParams(vmem_limit_bytes=4 * MIB),
         cost_estimate=pl.CostEstimate(flops=0, bytes_accessed=2 * MIB, transcendentals=0),
-    )(blocks, *parts, accum, accum)
+    )(part, chunk, *held)
 
 
 def cold_dense_kernel(place_ref, in_ref, *out_refs):
@@ -393,12 +410,16 @@
         scalars=1,
         size=3 * MIB,
     )
+    block = ((core * ZP + zp) * 2 * HALF + node * CHUNK) // CHUNK
+    accum = pick(jnp.stack([block, block + HALF // CHUNK]), in_hbm(hot_accum.reshape(TABLES * HOT, E)))
+    slab, accum = lax.optimization_barrier((slab, accum))
     part = call(group_sum_kernel, shape(CHUNK, WIDE), (parts,), size=2 * MIB)
     slab = exchange(slab, with_pair)
-    quad = [part] + [flip(part, 4 * d) for d in range(1, ZQ)]
-    block = ((core * ZP + zp) * 2 * HALF + node * CHUNK) // CHUNK
-    done = step(jnp.stack([block, block + HALF // CHUNK]), quad, hot_accum.reshape(TABLES * HOT, E))
-    whole = call(spread_kernel, halves, (place, done, flip(done, 2)), scalars=1, size=2 * MIB)
+    quad = [part] + [flip(part, 4 * d) for d in (2, 1, 3)]
+    done = call(step_kernel, pltpu.VMEM((CHUNK, WIDE), BF), (*quad, accum))
+    beside = flip(done, 2)
+    whole = spread(zp.reshape(1), done)
+    whole = spread(1 - zp.reshape(1), beside, (whole,))
     half = exchange(whole, alone)
     cold = call(
         cold_dense_kernel,
@@ -408,7 +429,7 @@
         flops=10**9,
         size=2 * MIB,
     )
-    cold = [cold[0]] + [flip(cold[d], 4 * d) for d in range(1, ZQ)]
+    cold = [cold[0]] + [flip(cold[d], 4 * d) for d in (2, 1, 3)]
     half, cold = lax.optimization_barrier((half, cold))
     cold_step = call(
         cold_step_kernel,

time: 94.5 us -> 93.1 us (0.985)
  waiting for transfers between devices: 28.5 us -> 25 us
  Pallas kernels: 21.8 us -> 22.9 us
    ppermute x11, waiting for transfers between devices: 14.4 us -> 11.5 us  [flip(): return lax.ppermute(array, 'all', [(i, i ^ mask) for i in range(OWNERS)])]
    pallas_call x1 -> x3, Pallas kernels: 0.58 us -> 3.29 us  [the longest x2 1.91 us: spread(): pl.pallas_call(spread_kernel, out_shape=pltpu.HBM((NODES, ZP, CHUNK, WIDE...]
    pallas_call x8, Pallas kernels: 16.9 us -> 15.3 us  [call(): pl.pallas_call(kernel, out_shape=out_shape, in_specs=[SMEM] * scalars + [...]
  transfers between devices with their start and end apart: 14 -> 14, of which waited for: 9 -> 9; matrix products, arithmetic and copies ran while one was open for 0% -> 1% of each run, Pallas kernels for 15% -> 16%
where the time goes in v4:
time: 93.1 us; the launch traced here: 92.7 us
  starting transfers between devices  43.3 us (47%)
  waiting for transfers between devices  25 us (27%)
  Pallas kernels  22.9 us (25%)
    ppermute x11, starting transfers between devices, flip(): return lax.ppermute(array, 'all', [(i, i ^ mask) for i in range(OWNERS)])  24.5 us
    all_to_all x3, starting transfers between devices, exchange(): lax.all_to_all(array, 'all', 0, 0, axis_index_groups=groups, tiled=True)  18.8 us
    pallas_call x8, Pallas kernels, call(): pl.pallas_call(kernel, out_shape=out_shape, in_specs=[SMEM] * scalars + [...  15.3 us
    all_to_all x3, waiting for transfers between devices, exchange(): lax.all_to_all(array, 'all', 0, 0, axis_index_groups=groups, tiled=True)  13.5 us
    ppermute x11, waiting for transfers between devices, flip(): return lax.ppermute(array, 'all', [(i, i ^ mask) for i in range(OWNERS)])  11.5 us
    pallas_call x2, Pallas kernels, finish(): pl.pallas_call(finish_kernel, out_shape=(shape(FEAT, HID), shape(TABLES *...  2.48 us
    pallas_call x2, Pallas kernels, spread(): pl.pallas_call(spread_kernel, out_shape=pltpu.HBM((NODES, ZP, CHUNK, WIDE...  1.91 us
  transfers between devices with their start and end apart: 14, of which 9 were waited for; matrix products, arithmetic and copies ran while one was open for 1% of the time, Pallas kernels for 16%

profile of v4, /device:TPU:1, one launch (start us, length us, event | category | flops | bytes accessed | tf_op | source)
XLA Modules:
  0.0 92.7 jit_solution(14578154514655017070)
XLA Ops:
  0.6 5.9 %shard_map.94 = (bf16[16,2,16,1024]{3,2,1,0:T(8,128)(2,1)}, bf16[16,2,16,1024]{3,2,1,0:T(8,128)(2,1)S(1)}, bf16[512,2048]{1,0:T(8,128)(2,1)S(1)}, bf16[512,2048]{1,0:T(8,128)(2,1)S(1)}, bf16[4,512,512]{2,1,0:T(8,128)(2,1)S(1)}) custom-call(s32[1]{0:T(128)} %bitcast.core_ref, bf16[512,512]{1,0:T(8,128)(2,1)} %x_hbm.1, s32[4,512]{1,0:T(4,128)} %bitcast.15, ...), custom_call_target="tpu_custom_call" | custom-call | flops 3000000000 | bytes 8388608 | tf_op jit(solution)/shard_map/pallas_call | solution.py:54
  6.5 3.3 %collective-permute-start.1 = (bf16[16,2,16,1024]{3,2,1,0:T(8,128)(2,1)}, bf16[16,2,16,1024]{3,2,1,0:T(8,128)(2,1)S(1)}, u32[]{:S(2)}, u32[]{:S(2)}) collective-permute-start(bf16[16,2,16,1024]{3,2,1,0:T(8,128)(2,1)} %get-tuple-element.34), channel_id=1, source_target_pairs={{0,1},{1,0},{2,3},{3,2},{4,5},{5,4},{6,7},{7,6},{8,9},{9,8},{10,11... | collective-permute-start | bytes 3145736 | tf_op jit(solution)/shard_map/ppermute | solution.py:343
  9.9 2.0 %shard_map.95 = (bf16[16,2,16,256]{3,2,1,0:T(8,128)(2,1)S(1)}, bf16[16,2,16,256]{3,2,1,0:T(8,128)(2,1)S(1)}, bf16[512,512]{1,0:T(8,128)(2,1)S(1)}) custom-call(s32[1]{0:T(128)} %bitcast.core_ref, bf16[512,2048]{1,0:T(8,128)(2,1)S(1)} %get-tuple-element.28.pre_ref, bf16[512,2048]{1,0:T(8,128)(2,1)S(1)} %get-tuple-element.29.wh_ref, ...), custom_call_target="tpu_custom_call" | custom-call | flops 2000000000 | bytes 6291456 | tf_op jit(solution)/shard_map/pallas_call | solution.py:54
  11.9 0.1 collective-permute-start
  12.0 0.4 collective-permute-done.1.b_ref
  12.4 1.1 %shard_map.96.refs_0_ = bf16[16,2,16,1280]{3,2,1,0:T(8,128)(2,1)} custom-call(bf16[16,2,16,1024]{3,2,1,0:T(8,128)(2,1)S(1)} %get-tuple-element.33.a_ref, bf16[16,2,16,1024]{3,2,1,0:T(8,128)(2,1)S(1)} %collective-permute-done.1.b_ref), custom_call_target="tpu_custom_call" | custom-call | bytes 2097152 | tf_op jit(solution)/shard_map/pallas_call | solution.py:192
  13.4 0.0 collective-permute-done.b_ref
  13.5 0.7 shard_map.97
  14.2 0.0 copy-start.1
  14.2 6.7 %all-to-all-start = ((bf16[32,16,1280]{2,1,0:T(8,128)(2,1)}), bf16[32,16,1280]{2,1,0:T(8,128)(2,1)S(1)}, u32[]{:S(2)}, u32[]{:S(2)}) async-start(bf16[32,16,1280]{2,1,0:T(8,128)(2,1)} %bitcast.17), calls=%async_computation | async-start | bytes 2621440 | tf_op jit(solution)/shard_map/all_to_all | solution.py:346
  20.9 0.0 copy-done.1
  20.9 3.9 %shard_map.99 = (bf16[1040,128]{1,0:T(8,128)(2,1)S(1)}, bf16[1040,128]{1,0:T(8,128)(2,1)S(1)}) custom-call(s32[1]{0:T(128)} %bitcast.core_ref, s32[4,512]{1,0:T(4,128)S(1)} %bitcast.16, bf16[512,512]{1,0:T(8,128)(2,1)S(1)} %get-tuple-element.35.grad_ref), custom_call_target="tpu_custom_call" | custom-call | flops 6000000000 | bytes 8388608 | tf_op jit(solution)/shard_map/pallas_call | solution.py:54
  24.8 0.7 collective-permute-start.5
  25.5 0.6 pad_add_fusion.at_ref
  26.2 1.4 %shard_map.101.accum_ref = f32[16,256]{1,0:T(8,128)S(1)} custom-call(s32[2]{0:T(128)} %pad_add_fusion.at_ref, f32[2048,128]{1,0:T(8,128)} %bitcast.18, f32[2048,128]{1,0:T(8,128)} %bitcast.19), custom_call_target="tpu_custom_call" | custom-call | tf_op jit(solution)/shard_map/pallas_call | solution.py:229
  27.5 0.0 collective-permute-done.5.far_cold_ref
  27.5 0.9 %shard_map.100 = bf16[32,5,16,128]{3,2,1,0:T(8,128)(2,1)} custom-call(s32[1]{0:T(128)} %bitcast.core_ref, bf16[1040,128]{1,0:T(8,128)(2,1)S(1)} %get-tuple-element.36.cold_ref, bf16[1040,128]{1,0:T(8,128)(2,1)S(1)} %collective-permute-done.5.far_cold_ref), custom_call_target="tpu_custom_call" | custom-call | bytes 3145728 | tf_op jit(solution)/shard_map/pallas_call | solution.py:54
  28.5 13.0 %all-to-all-done.in_ref = bf16[32,16,1280]{2,1,0:T(8,128)(2,1)S(1)} async-done(((bf16[32,16,1280]{2,1,0:T(8,128)(2,1)}), bf16[32,16,1280]{2,1,0:T(8,128)(2,1)S(1)}, u32[]{:S(2)}, u32[]{:S(2)}) %all-to-all-start) | async-done | bytes 1310752 | tf_op jit(solution)/shard_map/all_to_all | solution.py:346
  41.5 3.9 %all-to-all-start.2 = ((bf16[32,5,16,128]{3,2,1,0:T(8,128)(2,1)}), bf16[32,5,16,128]{3,2,1,0:T(8,128)(2,1)S(1)}, u32[]{:S(2)}, u32[]{:S(2)}) async-start(bf16[32,5,16,128]{3,2,1,0:T(8,128)(2,1)} %shard_map.100), calls=%async_computation.2 | async-start | bytes 1310720 | tf_op jit(solution)/shard_map/all_to_all | solution.py:346
  45.4 0.2 shard_map.98.a_ref
  45.6 6.3 %collective-permute-start.2 = (bf16[16,1280]{1,0:T(8,128)(2,1)S(1)}, bf16[16,1280]{1,0:T(8,128)(2,1)S(1)}, u32[]{:S(2)}, u32[]{:S(2)}) collective-permute-start(bf16[16,1280]{1,0:T(8,128)(2,1)S(1)} %shard_map.98.a_ref), channel_id=1, source_target_pairs={{0,8},{1,9},{2,10},{3,11},{4,12},{5,13},{6,14},{7,15},{8,0},{9,1},... | collective-permute-start | bytes 122888 | tf_op jit(solution)/shard_map/ppermute | solution.py:343
  51.9 1.2 %collective-permute-start.3 = (bf16[16,1280]{1,0:T(8,128)(2,1)S(1)}, bf16[16,1280]{1,0:T(8,128)(2,1)S(1)}, u32[]{:S(2)}, u32[]{:S(2)}) collective-permute-start(bf16[16,1280]{1,0:T(8,128)(2,1)S(1)} %shard_map.98.a_ref), channel_id=1, source_target_pairs={{0,4},{1,5},{2,6},{3,7},{4,0},{5,1},{6,2},{7,3},{8,12},{9,13},{10,... | collective-permute-start | bytes 122888 | tf_op jit(solution)/shard_map/ppermute | solution.py:343
  53.1 0.0 collective-permute-start.4
  53.1 5.4 %collective-permute-done.2.b_ref = bf16[16,1280]{1,0:T(8,128)(2,1)S(1)} collective-permute-done((bf16[16,1280]{1,0:T(8,128)(2,1)S(1)}, bf16[16,1280]{1,0:T(8,128)(2,1)S(1)}, u32[]{:S(2)}, u32[]{:S(2)}) %collective-permute-start.2) | collective-permute-done | bytes 40992 | tf_op jit(solution)/shard_map/ppermute | solution.py:343
  58.4 0.0 collective-permute-done.3.c_ref
  58.4 1.0 %collective-permute-done.4.d_ref = bf16[16,1280]{1,0:T(8,128)(2,1)S(1)} collective-permute-done((bf16[16,1280]{1,0:T(8,128)(2,1)S(1)}, bf16[16,1280]{1,0:T(8,128)(2,1)S(1)}, u32[]{:S(2)}, u32[]{:S(2)}) %collective-permute-start.4) | collective-permute-done | bytes 40992 | tf_op jit(solution)/shard_map/ppermute | solution.py:343
  59.5 1.2 %collective-permute-start.6 = (bf16[16,1280]{1,0:T(8,128)(2,1)S(1)}, bf16[16,1280]{1,0:T(8,128)(2,1)S(1)}, u32[]{:S(2)}, u32[]{:S(2)}) collective-permute-start(bf16[16,1280]{1,0:T(8,128)(2,1)S(1)} %shard_map.102.in_ref), channel_id=1, source_target_pairs={{0,2},{1,3},{2,0},{3,1},{4,6},{5,7},{6,4},{7,5},{8,10},{9,11},{10,... | collective-permute-start | bytes 122888 | tf_op jit(solution)/shard_map/ppermute | solution.py:343
  60.7 1.0 %shard_map.103.refs_0_ = bf16[16,2,16,1280]{3,2,1,0:T(8,128)(2,1)} custom-call(s32[1]{0:T(128)} %bitcast.1.part_ref, bf16[16,1280]{1,0:T(8,128)(2,1)S(1)} %shard_map.102.in_ref), custom_call_target="tpu_custom_call" | custom-call | bytes 2097152 | tf_op jit(solution)/shard_map/pallas_call | solution.py:262
  61.7 0.8 collective-permute-done.6.in_ref
  62.5 1.0 %shard_map.104 = bf16[16,2,16,1280]{3,2,1,0:T(8,128)(2,1)} custom-call(s32[1]{0:T(128)S(6)} %sub.11.part_ref, bf16[16,1280]{1,0:T(8,128)(2,1)S(1)} %collective-permute-done.6.in_ref, bf16[16,2,16,1280]{3,2,1,0:T(8,128)(2,1)} %shard_map.103.refs_0_), custom_call_target="tpu_custom_call", output_to_operand_aliasing={{}: (2, {})} | custom-call | bytes 2097152 | tf_op jit(solution)/shard_map/pallas_call | solution.py:262
  63.5 0.0 all-to-all-done.2.in_ref
  63.5 8.2 %all-to-all-start.1 = ((bf16[16,2,16,1280]{3,2,1,0:T(8,128)(2,1)}), bf16[16,2,16,1280]{3,2,1,0:T(8,128)(2,1)S(1)}, u32[]{:S(2)}, u32[]{:S(2)}) async-start(bf16[16,2,16,1280]{3,2,1,0:T(8,128)(2,1)} %shard_map.104), calls=%async_computation.1 | async-start | bytes 2621440 | tf_op jit(solution)/shard_map/all_to_all | solution.py:346
  71.7 0.1 pad_add_fusion.1.place_ref
  71.8 1.6 %shard_map.105 = (bf16[256,128]{1,0:T(8,128)(2,1)S(1)}, bf16[256,128]{1,0:T(8,128)(2,1)S(1)}, bf16[256,128]{1,0:T(8,128)(2,1)S(1)}, bf16[256,128]{1,0:T(8,128)(2,1)S(1)}) custom-call(s32[3]{0:T(128)S(1)} %pad_add_fusion.1.place_ref, bf16[32,5,16,128]{3,2,1,0:T(8,128)(2,1)S(1)} %all-to-all-done.2.in_ref), custom_call_target="tpu_custom_call" | custom-call | flops 1000000000 | bytes 2097152 | tf_op jit(solution)/shard_map/pallas_call | solution.py:54
  73.4 0.0 copy-start
  73.4 1.8 %collective-permute-start.7 = (bf16[256,128]{1,0:T(8,128)(2,1)S(1)}, bf16[256,128]{1,0:T(8,128)(2,1)S(1)}, u32[]{:S(2)}, u32[]{:S(2)}) collective-permute-start(bf16[256,128]{1,0:T(8,128)(2,1)S(1)} %get-tuple-element.41), channel_id=1, source_target_pairs={{0,8},{1,9},{2,10},{3,11},{4,12},{5,13},{6,14},{7,15},{8,0},{9,1},... | collective-permute-start | bytes 196616 | tf_op jit(solution)/shard_map/ppermute | solution.py:343
  75.2 1.5 %collective-permute-start.8 = (bf16[256,128]{1,0:T(8,128)(2,1)S(1)}, bf16[256,128]{1,0:T(8,128)(2,1)S(1)}, u32[]{:S(2)}, u32[]{:S(2)}) collective-permute-start(bf16[256,128]{1,0:T(8,128)(2,1)S(1)} %get-tuple-element.42), channel_id=1, source_target_pairs={{0,4},{1,5},{2,6},{3,7},{4,0},{5,1},{6,2},{7,3},{8,12},{9,13},{10,... | collective-permute-start | bytes 196616 | tf_op jit(solution)/shard_map/ppermute | solution.py:343
  76.7 2.5 %collective-permute-start.9 = (bf16[256,128]{1,0:T(8,128)(2,1)S(1)}, bf16[256,128]{1,0:T(8,128)(2,1)S(1)}, u32[]{:S(2)}, u32[]{:S(2)}) collective-permute-start(bf16[256,128]{1,0:T(8,128)(2,1)S(1)} %get-tuple-element.43), channel_id=1, source_target_pairs={{0,12},{1,13},{2,14},{3,15},{4,8},{5,9},{6,10},{7,11},{8,4},{9,5},... | collective-permute-start | bytes 196616 | tf_op jit(solution)/shard_map/ppermute | solution.py:343
  79.1 1.4 %collective-permute-done.7.b_ref = bf16[256,128]{1,0:T(8,128)(2,1)S(1)} collective-permute-done((bf16[256,128]{1,0:T(8,128)(2,1)S(1)}, bf16[256,128]{1,0:T(8,128)(2,1)S(1)}, u32[]{:S(2)}, u32[]{:S(2)}) %collective-permute-start.7) | collective-permute-done | bytes 65568 | tf_op jit(solution)/shard_map/ppermute | solution.py:343
  80.5 0.0 collective-permute-done.8.c_ref
  80.5 1.7 %collective-permute-done.9.d_ref = bf16[256,128]{1,0:T(8,128)(2,1)S(1)} collective-permute-done((bf16[256,128]{1,0:T(8,128)(2,1)S(1)}, bf16[256,128]{1,0:T(8,128)(2,1)S(1)}, u32[]{:S(2)}, u32[]{:S(2)}) %collective-permute-start.9) | collective-permute-done | bytes 65568 | tf_op jit(solution)/shard_map/ppermute | solution.py:343
  82.3 0.5 all-to-all-done.1.in_ref
  82.8 6.0 %collective-permute-start.10 = (bf16[16,2,16,1280]{3,2,1,0:T(8,128)(2,1)S(1)}, bf16[16,2,16,1280]{3,2,1,0:T(8,128)(2,1)S(1)}, u32[]{:S(2)}, u32[]{:S(2)}) collective-permute-start(bf16[16,2,16,1280]{3,2,1,0:T(8,128)(2,1)S(1)} %all-to-all-done.1.in_ref), channel_id=1, source_target_pairs={{0,1},{1,0},{2,3},{3,2},{4,5},{5,4},{6,7},{7,6},{8,9},{9,8},{10,11... | collective-permute-start | bytes 3932168 | tf_op jit(solution)/shard_map/ppermute | solution.py:343
  88.7 1.2 %shard_map.106 = (bf16[512,2048]{1,0:T(8,128)(2,1)}, f32[2048,128]{1,0:T(8,128)}) custom-call(s32[1]{0:T(128)} %bitcast.core_ref, bf16[16,2,16,1280]{3,2,1,0:T(8,128)(2,1)S(1)} %all-to-all-done.1.in_ref), custom_call_target="tpu_custom_call" | custom-call | bytes 4194304 | tf_op jit(solution)/shard_map/pallas_call | solution.py:314
  90.0 0.0 copy-done
  90.0 0.7 shard_map.108
  90.7 0.7 collective-permute-done.10.in_ref
  91.4 1.2 %shard_map.107 = (bf16[512,2048]{1,0:T(8,128)(2,1)}, f32[2048,128]{1,0:T(8,128)}) custom-call(s32[1]{0:T(128)S(6)} %sub.10.core_ref, bf16[16,2,16,1280]{3,2,1,0:T(8,128)(2,1)S(1)} %collective-permute-done.10.in_ref, bf16[512,2048]{1,0:T(8,128)(2,1)} %get-tuple-element.45.refs_0_, ...), custom_call_target="tpu_custom_call", output_to_operand_aliasing={{0}: (2, {}), {1}: (3, {})} | custom-call | bytes 4194304 | tf_op jit(solution)/shard_map/pallas_call | solution.py:314
  (1 shorter events, 0.0 us)
Async XLA Ops:
  6.5 5.8 %collective-permute-start.1 = (bf16[16,2,16,1024]{3,2,1,0:T(8,128)(2,1)}, bf16[16,2,16,1024]{3,2,1,0:T(8,128)(2,1)S(1)}, u32[]{:S(2)}, u32[]{:S(2)}) collective-permute-start(bf16[16,2,16,1024]{3,2,1,0:T(8,128)(2,1)} %get-tuple-element.34), channel_id=1, source_target_pairs={{0,1},{1,0},{2,3},{3,2},{4,5},{5,4},{6,7},{7,6},{8,9},{9,8},{10,11... | collective-permute-start | bytes 3145736 | tf_op jit(solution)/shard_map/ppermute | solution.py:343
  11.9 1.6 %collective-permute-start = (bf16[16,2,16,256]{3,2,1,0:T(8,128)(2,1)S(1)}, bf16[16,2,16,256]{3,2,1,0:T(8,128)(2,1)S(1)}, u32[]{:S(2)}, u32[]{:S(2)}) collective-permute-start(bf16[16,2,16,256]{3,2,1,0:T(8,128)(2,1)S(1)} %get-tuple-element.32), channel_id=1, source_target_pairs={{0,1},{1,0},{2,3},{3,2},{4,5},{5,4},{6,7},{7,6},{8,9},{9,8},{10,11... | collective-permute-start | bytes 786440 | tf_op jit(solution)/shard_map/ppermute | solution.py:343
  14.2 6.7 %copy-start.1 = (s32[512,4]{0,1:T(4,128)S(1)}, s32[512,4]{0,1:T(4,128)}, u32[]{:S(2)}) copy-start(s32[512,4]{0,1:T(4,128)} %param.8) | copy-start | bytes 24580
  14.2 27.2 %all-to-all-start = ((bf16[32,16,1280]{2,1,0:T(8,128)(2,1)}), bf16[32,16,1280]{2,1,0:T(8,128)(2,1)S(1)}, u32[]{:S(2)}, u32[]{:S(2)}) async-start(bf16[32,16,1280]{2,1,0:T(8,128)(2,1)} %bitcast.17), calls=%async_computation | async-start | bytes 2621440 | tf_op jit(solution)/shard_map/all_to_all | solution.py:346
  24.8 2.8 %collective-permute-start.5 = (bf16[1040,128]{1,0:T(8,128)(2,1)S(1)}, bf16[1040,128]{1,0:T(8,128)(2,1)S(1)}, u32[]{:S(2)}, u32[]{:S(2)}) collective-permute-start(bf16[1040,128]{1,0:T(8,128)(2,1)S(1)} %get-tuple-element.37), channel_id=1, source_target_pairs={{0,1},{1,0},{2,3},{3,2},{4,5},{5,4},{6,7},{7,6},{8,9},{9,8},{10,11... | collective-permute-start | bytes 798728 | tf_op jit(solution)/shard_map/ppermute | solution.py:343
  41.5 22.0 %all-to-all-start.2 = ((bf16[32,5,16,128]{3,2,1,0:T(8,128)(2,1)}), bf16[32,5,16,128]{3,2,1,0:T(8,128)(2,1)S(1)}, u32[]{:S(2)}, u32[]{:S(2)}) async-start(bf16[32,5,16,128]{3,2,1,0:T(8,128)(2,1)} %shard_map.100), calls=%async_computation.2 | async-start | bytes 1310720 | tf_op jit(solution)/shard_map/all_to_all | solution.py:346
  45.6 12.9 %collective-permute-start.2 = (bf16[16,1280]{1,0:T(8,128)(2,1)S(1)}, bf16[16,1280]{1,0:T(8,128)(2,1)S(1)}, u32[]{:S(2)}, u32[]{:S(2)}) collective-permute-start(bf16[16,1280]{1,0:T(8,128)(2,1)S(1)} %shard_map.98.a_ref), channel_id=1, source_target_pairs={{0,8},{1,9},{2,10},{3,11},{4,12},{5,13},{6,14},{7,15},{8,0},{9,1},... | collective-permute-start | bytes 122888 | tf_op jit(solution)/shard_map/ppermute | solution.py:343
  51.9 6.6 %collective-permute-start.3 = (bf16[16,1280]{1,0:T(8,128)(2,1)S(1)}, bf16[16,1280]{1,0:T(8,128)(2,1)S(1)}, u32[]{:S(2)}, u32[]{:S(2)}) collective-permute-start(bf16[16,1280]{1,0:T(8,128)(2,1)S(1)} %shard_map.98.a_ref), channel_id=1, source_target_pairs={{0,4},{1,5},{2,6},{3,7},{4,0},{5,1},{6,2},{7,3},{8,12},{9,13},{10,... | collective-permute-start | bytes 122888 | tf_op jit(solution)/shard_map/ppermute | solution.py:343
  53.1 6.4 %collective-permute-start.4 = (bf16[16,1280]{1,0:T(8,128)(2,1)S(1)}, bf16[16,1280]{1,0:T(8,128)(2,1)S(1)}, u32[]{:S(2)}, u32[]{:S(2)}) collective-permute-start(bf16[16,1280]{1,0:T(8,128)(2,1)S(1)} %shard_map.98.a_ref), channel_id=1, source_target_pairs={{0,12},{1,13},{2,14},{3,15},{4,8},{5,9},{6,10},{7,11},{8,4},{9,5},... | collective-permute-start | bytes 122888 | tf_op jit(solution)/shard_map/ppermute | solution.py:343
  59.5 3.0 %collective-permute-start.6 = (bf16[16,1280]{1,0:T(8,128)(2,1)S(1)}, bf16[16,1280]{1,0:T(8,128)(2,1)S(1)}, u32[]{:S(2)}, u32[]{:S(2)}) collective-permute-start(bf16[16,1280]{1,0:T(8,128)(2,1)S(1)} %shard_map.102.in_ref), channel_id=1, source_target_pairs={{0,2},{1,3},{2,0},{3,1},{4,6},{5,7},{6,4},{7,5},{8,10},{9,11},{10,... | collective-permute-start | bytes 122888 | tf_op jit(solution)/shard_map/ppermute | solution.py:343
  63.5 19.3 %all-to-all-start.1 = ((bf16[16,2,16,1280]{3,2,1,0:T(8,128)(2,1)}), bf16[16,2,16,1280]{3,2,1,0:T(8,128)(2,1)S(1)}, u32[]{:S(2)}, u32[]{:S(2)}) async-start(bf16[16,2,16,1280]{3,2,1,0:T(8,128)(2,1)} %shard_map.104), calls=%async_computation.1 | async-start | bytes 2621440 | tf_op jit(solution)/shard_map/all_to_all | solution.py:346
  73.4 16.6 %copy-start = (f32[4,64,128]{2,1,0:T(8,128)S(1)}, f32[4,64,128]{2,1,0:T(8,128)}, u32[]{:S(2)}) copy-start(f32[4,64,128]{2,1,0:T(8,128)} %param.13) | copy-start | bytes 393220
  73.4 7.1 %collective-permute-start.7 = (bf16[256,128]{1,0:T(8,128)(2,1)S(1)}, bf16[256,128]{1,0:T(8,128)(2,1)S(1)}, u32[]{:S(2)}, u32[]{:S(2)}) collective-permute-start(bf16[256,128]{1,0:T(8,128)(2,1)S(1)} %get-tuple-element.41), channel_id=1, source_target_pairs={{0,8},{1,9},{2,10},{3,11},{4,12},{5,13},{6,14},{7,15},{8,0},{9,1},... | collective-permute-start | bytes 196616 | tf_op jit(solution)/shard_map/ppermute | solution.py:343
  75.2 5.3 %collective-permute-start.8 = (bf16[256,128]{1,0:T(8,128)(2,1)S(1)}, bf16[256,128]{1,0:T(8,128)(2,1)S(1)}, u32[]{:S(2)}, u32[]{:S(2)}) collective-permute-start(bf16[256,128]{1,0:T(8,128)(2,1)S(1)} %get-tuple-element.42), channel_id=1, source_target_pairs={{0,4},{1,5},{2,6},{3,7},{4,0},{5,1},{6,2},{7,3},{8,12},{9,13},{10,... | collective-permute-start | bytes 196616 | tf_op jit(solution)/shard_map/ppermute | solution.py:343
  76.7 5.6 %collective-permute-start.9 = (bf16[256,128]{1,0:T(8,128)(2,1)S(1)}, bf16[256,128]{1,0:T(8,128)(2,1)S(1)}, u32[]{:S(2)}, u32[]{:S(2)}) collective-permute-start(bf16[256,128]{1,0:T(8,128)(2,1)S(1)} %get-tuple-element.43), channel_id=1, source_target_pairs={{0,12},{1,13},{2,14},{3,15},{4,8},{5,9},{6,10},{7,11},{8,4},{9,5},... | collective-permute-start | bytes 196616 | tf_op jit(solution)/shard_map/ppermute | solution.py:343
  82.8 8.6 %collective-permute-start.10 = (bf16[16,2,16,1280]{3,2,1,0:T(8,128)(2,1)S(1)}, bf16[16,2,16,1280]{3,2,1,0:T(8,128)(2,1)S(1)}, u32[]{:S(2)}, u32[]{:S(2)}) collective-permute-start(bf16[16,2,16,1280]{3,2,1,0:T(8,128)(2,1)S(1)} %all-to-all-done.1.in_ref), channel_id=1, source_target_pairs={{0,1},{1,0},{2,3},{3,2},{4,5},{5,4},{6,7},{7,6},{8,9},{9,8},{10,11... | collective-permute-start | bytes 3932168 | tf_op jit(solution)/shard_map/ppermute | solution.py:343

commit v5 on v4

--- a/solution.py
+++ b/solution.py
@@ -28,10 +28,11 @@
 SLOT_HALF = OWNERS * CAP // 2
 NODE_SLOTS = SLOT_HALF // NODES
 PAIR = 2 * CAP
-SLAB = ZQ + 1
+SLAB = ZP * ZQ + 1
 BF = jnp.bfloat16
 F32 = jnp.float32
 MIB = 1024 * 1024
+COLD_ORDER = ((0, 2, 1, 3), (0, 3, 2, 1))
 VMEM = pl.BlockSpec(memory_space=pltpu.VMEM)
 HBM = pl.BlockSpec(memory_space=pltpu.HBM)
 SMEM = pl.BlockSpec(memory_space=pltpu.SMEM)
@@ -63,8 +64,8 @@
 
 
 def backprop_kernel(
-    core_ref, x_hbm, ids_hbm, y_hbm, wh_hbm, wo_hbm, send_hbm, own_ref, pre_ref, wh_ref, hit_ref,
-    slope_ref, xt_ref, x_ref, ids_ref, y_ref, wo_ref, send_ref, sems, out_sems,
+    core_ref, x_hbm, ids_hbm, y_hbm, wh_hbm, wo_hbm, send_ref, own_ref, pre_ref, wh_ref, hit_ref,
+    slope_ref, xt_ref, x_ref, ids_ref, y_ref, wo_ref, sems,
 ):
     core = core_ref[0]
     step = 256
@@ -77,7 +78,6 @@
         pltpu.make_async_copy(src, dst, sems.at[blocks + i])
         for i, (src, dst) in enumerate(((x_hbm, x_ref), (wo_hbm, wo_ref), (ids_hbm, ids_ref), (y_hbm, y_ref)))
     ]
-    stores = []
     for copy in (*small[1:], small[0], *loads):
         copy.start()
     for copy in small[1:]:
@@ -119,12 +119,6 @@
         for rows, out_ref in ((far_rows, send_ref), (own_rows, own_ref)):
             term = dot(xt_ref[rows, :], pre).astype(BF)
             out_ref[:, part, :, at:at + step] = term.reshape(NODES, CHUNK, step)
-        if at + step == PCOL:
-            copy = pltpu.make_async_copy(send_ref.at[:, part], send_hbm.at[:, part], out_sems.at[part])
-            copy.start()
-            stores.append(copy)
-    for copy in stores:
-        copy.wait()
 
 
 def hot_kernel(core_ref, pre_ref, wh_ref, hit_ref, send_ref, own_ref, grad_ref):
@@ -155,7 +149,8 @@
         before = dot(member.astype(BF), earlier) + carry
         rank = jnp.sum(member * before, axis=0, keepdims=True).astype(jnp.int32)
         carry = carry + jnp.sum(member, axis=1, keepdims=True)
-        core_at, zp_at, zq_at, node_at = owner & 1, (owner >> 1) & 1, (owner >> 2) & 3, owner >> 4
+        turned = ((owner >> 1) + 7) & 7
+        core_at, zp_at, zq_at, node_at = owner & 1, turned & 1, turned >> 1, owner >> 4
         slot = (((core_at * NODES + node_at) * ZP + zp_at) * ZQ + zq_at) * CAP + rank
         slots.append(jnp.where(cold, slot, -1))
         names.append(((offset & (COLD_DEV - 1)) + t * COLD_DEV).astype(F32))
@@ -201,16 +196,32 @@
     )(a, b, *rest)
 
 
-def merge_kernel(core_ref, cold_ref, far_cold_ref, out_ref):
-    first = core_ref[0] == 0
+def cold_split_kernel(place_ref, cold_ref, far_cold_ref, keep_ref, send_ref, rows_ref):
+    pair_at, first = place_ref[3], place_ref[4] == 0
     own, far = cold_ref[...].astype(F32), far_cold_ref[...].astype(F32)
     labels = (own[SLOT_HALF:] + far[SLOT_HALF:]).astype(BF)
     own = own[:SLOT_HALF].reshape(GROUP * ZQ, CAP, E)
     far = far[:SLOT_HALF].reshape(GROUP * ZQ, CAP, E)
     pair = [jnp.where(first, own, far), jnp.where(first, far, own)]
-    out_ref[:, :ZQ] = jnp.concatenate(pair, axis=1).astype(BF).reshape(GROUP, ZQ, PAIR, E)
-    for g in range(GROUP):
-        out_ref[g, ZQ] = labels
+    rows_ref[...] = jnp.concatenate(pair, axis=1).astype(BF).reshape(NODES, ZP, ZQ, PAIR, E)
+    for side, out_ref in ((pair_at, keep_ref), (1 - pair_at, send_ref)):
+        out_ref[:NODES] = rows_ref[:, side]
+        out_ref[NODES] = jnp.broadcast_to(labels[None], (ZQ, PAIR, E))
+
+
+def cold_merge_kernel(place_ref, keep_ref, far_ref, out_ref):
+    pair_at = place_ref[3]
+    lane = lax.broadcasted_iota(jnp.int32, (NODES, E), 1)
+    mine = ((lane >> 5) & 1) == pair_at
+    labels = jnp.zeros((NODES, E), F32)
+    for side, in_ref in ((pair_at, keep_ref), (1 - pair_at, far_ref)):
+        for q in range(ZQ):
+            out_ref[:, side * ZQ + q] = in_ref[:NODES, q]
+        named = jnp.where(mine, in_ref[NODES, 0].astype(F32), 0.0)
+        labels = labels + pltpu.roll(named, ((side - pair_at) * ZQ * CAP) & (E - 1), 1)
+    labels = labels.astype(BF)
+    for n in range(NODES):
+        out_ref[n, SLAB - 1] = labels
 
 
 def group_sum_kernel(in_ref, out_ref):
@@ -272,25 +283,30 @@
 
 
 def cold_dense_kernel(place_ref, in_ref, *out_refs):
-    node, zq, zp = place_ref[0], place_ref[1], place_ref[2]
+    core = place_ref[4]
+    node, quad_at = place_ref[0], place_ref[2]
     mine = lax.broadcasted_iota(jnp.int32, (NODES, E), 0) == node
     labels = []
-    for g in range(GROUP):
-        named = jnp.where(mine, in_ref[g, ZQ].astype(F32), 0.0)
+    for n in range(NODES):
+        named = jnp.where(mine, in_ref[n, SLAB - 1].astype(F32), 0.0)
         labels.append(jnp.sum(named, axis=0, keepdims=True))
     labels = jnp.concatenate(labels, axis=0).astype(BF)
-    entries = GROUP * PAIR
+    entries = NODES * PAIR
     lane = lax.broadcasted_iota(jnp.int32, (E, entries), 0)
     place = lax.broadcasted_iota(jnp.int32, (E, entries), 1)
-    wanted = ((place >> 3) & 1) * NODE_SLOTS + zp * (ZQ * CAP) + (place & 7)
-    keep = lax.broadcasted_iota(jnp.int32, (GROUP, entries), 0) == lax.broadcasted_iota(jnp.int32, (GROUP, entries), 1) >> 4
+    wanted = ((place >> 3) & 1) * NODE_SLOTS + (place & 7)
+    keep = lax.broadcasted_iota(jnp.int32, (NODES, entries), 0) == lax.broadcasted_iota(jnp.int32, (NODES, entries), 1) >> 4
     rows = lax.broadcasted_iota(jnp.int32, (TABLES * COLD_DEV, entries), 0).astype(F32)
     for d, out_ref in enumerate(out_refs):
-        target = zq ^ d
-        moved = dot(labels, jnp.where(lane == wanted + target * CAP, 1.0, 0.0).astype(BF))
-        named = jnp.sum(jnp.where(keep, moved, 0.0), axis=0, keepdims=True)
-        onehot = jnp.where(named == rows, 1.0, 0.0).astype(BF)
-        out_ref[...] = dot(onehot, in_ref[:, target].reshape(entries, E)).astype(BF)
+        d = jnp.where(core == 0, COLD_ORDER[0][d], COLD_ORDER[1][d])
+        total = jnp.zeros((TABLES * COLD_DEV, E), F32)
+        for side in range(ZP):
+            target = side * ZQ + (quad_at ^ d)
+            moved = dot(labels, jnp.where(lane == wanted + target * CAP, 1.0, 0.0).astype(BF))
+            named = jnp.sum(jnp.where(keep, moved, 0.0), axis=0, keepdims=True)
+            onehot = jnp.where(named == rows, 1.0, 0.0).astype(BF)
+            total = total + dot(onehot, in_ref[:, target].reshape(entries, E))
+        out_ref[...] = total.astype(BF)
 
 
 def cold_step_kernel(accum_ref, a_ref, b_ref, c_ref, d_ref, out_ref):
@@ -334,20 +350,31 @@
     node, zq, zp, core = me >> 4, (me >> 2) & 3, (me >> 1) & 1, me & 1
     ids = lookups.T
     core_arg = core.reshape(1)
-    place = jnp.stack([node, zq, zp])
+    turned = ((me >> 1) + 7) & 7
+    place = jnp.stack([node, zq, turned >> 1, turned & 1, core])
 
     def in_hbm(array):
         return pltpu.with_memory_space_constraint(array, pltpu.HBM)
 
-    def flip(array, mask):
-        return lax.ppermute(array, "all", [(i, i ^ mask) for i in range(OWNERS)])
+    def flip(array, mask, other=None):
+        masks = (mask, mask if other is None else other)
+        return lax.ppermute(array, "all", [(i, i ^ masks[i & 1]) for i in range(OWNERS)])
 
     def exchange(array, groups):
         return lax.all_to_all(array, "all", 0, 0, axis_index_groups=groups, tiled=True)
+
+    def turned_flip(array, mask, other=None):
+        masks = (mask, mask if other is None else other)
+
+        def partner(i):
+            return (i & ~14) | (((((((i >> 1) + 7) & 7) ^ masks[i & 1]) + 1) & 7) << 1)
+
+        return lax.ppermute(array, "all", [(i, partner(i)) for i in range(OWNERS)])
 
     with_pair = [
         [n * LOCALS + q * 4 + p * 2 + c for n in range(NODES) for p in range(ZP)] for q in range(ZQ) for c in range(2)
     ]
+    by_node = [[n * LOCALS + low for n in range(NODES)] for low in range(LOCALS)]
     alone = [
         [n * LOCALS + low for n in reversed(range(NODES))] for low in range(LOCALS)
     ]
@@ -356,7 +383,7 @@
     w1_send, w1_own, pre, weights, hits = call(
         backprop_kernel,
         (
-            pltpu.HBM(half_w1, BF),
+            pltpu.VMEM(half_w1, BF),
             pltpu.VMEM(half_w1, BF),
             pltpu.VMEM((TOK, HID), BF),
             pltpu.VMEM((FEAT, HID), BF),
@@ -371,12 +398,10 @@
             pltpu.VMEM((TABLES, TOK), jnp.int32),
             pltpu.VMEM((1, TOK), jnp.int32),
             pltpu.VMEM((HID // E, E), BF),
-            pltpu.VMEM(half_w1, BF),
             pltpu.SemaphoreType.DMA((HID // 256 + 4,)),
-            pltpu.SemaphoreType.DMA((ZP,)),
         ],
         spec=HBM,
-        out_specs=(HBM, VMEM, VMEM, VMEM, VMEM),
+        out_specs=(VMEM,) * 5,
         limit=24,
         flops=3 * 10**9,
         size=8 * MIB,
@@ -403,19 +428,27 @@
         flops=6 * 10**9,
         size=8 * MIB,
     )
+    cold_keep, cold_give = call(
+        cold_split_kernel,
+        (shape(NODES + 1, ZQ, PAIR, E), shape(NODES + 1, ZQ, PAIR, E)),
+        (place, cold_own, flip(cold_send, 1)),
+        scalars=1,
+        scratch=[pltpu.VMEM((NODES, ZP, ZQ, PAIR, E), BF)],
+        size=2 * MIB,
+    )
     slab = call(
-        merge_kernel,
-        shape(GROUP, SLAB, PAIR, E),
-        (core_arg, cold_own, flip(cold_send, 1)),
-        scalars=1,
-        size=3 * MIB,
+        cold_merge_kernel,
+        shape(NODES, SLAB, PAIR, E),
+        (place, cold_keep, turned_flip(cold_give, 1)),
+        scalars=1,
+        size=2 * MIB,
     )
     block = ((core * ZP + zp) * 2 * HALF + node * CHUNK) // CHUNK
     accum = pick(jnp.stack([block, block + HALF // CHUNK]), in_hbm(hot_accum.reshape(TABLES * HOT, E)))
     slab, accum = lax.optimization_barrier((slab, accum))
     part = call(group_sum_kernel, shape(CHUNK, WIDE), (parts,), size=2 * MIB)
-    slab = exchange(slab, with_pair)
-    quad = [part] + [flip(part, 4 * d) for d in (2, 1, 3)]
+    slab = exchange(slab, by_node)
+    quad = [part] + [flip(part, 4 * d, 4 * e) for d, e in zip((2, 1, 3), (3, 2, 1))]
     done = call(step_kernel, pltpu.VMEM((CHUNK, WIDE), BF), (*quad, accum))
     beside = flip(done, 2)
     whole = spread(zp.reshape(1), done)
@@ -429,7 +462,9 @@
         flops=10**9,
         size=2 * MIB,
     )
-    cold = [cold[0]] + [flip(cold[d], 4 * d) for d in (2, 1, 3)]
+    cold = [cold[0]] + [
+        turned_flip(cold[k], 2 * COLD_ORDER[0][k], 2 * COLD_ORDER[1][k]) for k in range(1, ZQ)
+    ]
     half, cold = lax.optimization_barrier((half, cold))
     cold_step = call(
         cold_step_kernel,

time: 93.1 us -> 91.6 us (0.984)
  waiting for transfers between devices: 25 us -> 20.6 us
  starting transfers between devices: 43.3 us -> 45.7 us
    all_to_all x3, waiting for transfers between devices: 13.5 us -> 1.07 us  [exchange(): lax.all_to_all(array, 'all', 0, 0, axis_index_groups=groups, tiled=True)]
    ppermute x11 -> x12, waiting for transfers between devices: 11.5 us -> 19.6 us  [the longest x4 10.3 us: turned_flip(): return lax.ppermute(array, 'all', [(i, partner(i)) for i in range(OWNERS)])]
    all_to_all x3, starting transfers between devices: 18.8 us -> 20.5 us  [exchange(): lax.all_to_all(array, 'all', 0, 0, axis_index_groups=groups, tiled=True)]
    ppermute x11 -> x12, starting transfers between devices: 24.5 us -> 25.2 us  [the longest x8 13.9 us: flip(): lax.ppermute(array, 'all', [(i, i ^ masks[i & 1]) for i in range(OWNERS)])]
    pallas_call x8 -> x9, Pallas kernels: 15.3 us -> 15.7 us  [call(): pl.pallas_call(kernel, out_shape=out_shape, in_specs=[SMEM] * scalars + [...]
  transfers between devices with their start and end apart: 14 -> 15, of which waited for: 9 -> 9; matrix products, arithmetic and copies ran while one was open for 1% -> 1% of each run, Pallas kernels for 16% -> 18%
where the time goes in v5:
time: 91.6 us; the launch traced here: 91.2 us
  starting transfers between devices  45.7 us (50%)
  Pallas kernels  23.3 us (25%)
  waiting for transfers between devices  20.6 us (22%)
    all_to_all x3, starting transfers between devices, exchange(): lax.all_to_all(array, 'all', 0, 0, axis_index_groups=groups, tiled=True)  20.5 us
    pallas_call x9, Pallas kernels, call(): pl.pallas_call(kernel, out_shape=out_shape, in_specs=[SMEM] * scalars + [...  15.7 us
    ppermute x8, starting transfers between devices, flip(): lax.ppermute(array, 'all', [(i, i ^ masks[i & 1]) for i in range(OWNERS)])  13.9 us
    ppermute x4, starting transfers between devices, turned_flip(): return lax.ppermute(array, 'all', [(i, partner(i)) for i in range(OWNERS)])  11.3 us
    ppermute x4, waiting for transfers between devices, turned_flip(): return lax.ppermute(array, 'all', [(i, partner(i)) for i in range(OWNERS)])  10.3 us
    ppermute x8, waiting for transfers between devices, flip(): lax.ppermute(array, 'all', [(i, i ^ masks[i & 1]) for i in range(OWNERS)])  9.22 us
    pallas_call x2, Pallas kernels, finish(): pl.pallas_call(finish_kernel, out_shape=(shape(FEAT, HID), shape(TABLES *...  2.48 us
    pallas_call x2, Pallas kernels, spread(): pl.pallas_call(spread_kernel, out_shape=pltpu.HBM((NODES, ZP, CHUNK, WIDE...  1.92 us
  transfers between devices with their start and end apart: 15, of which 9 were waited for; matrix products, arithmetic and copies ran while one was open for 1% of the time, Pallas kernels for 18%

profile of v5, /device:TPU:1, one launch (start us, length us, event | category | flops | bytes accessed | tf_op | source)
XLA Modules:
  0.0 91.2 jit_solution(6236198489577775415)
XLA Ops:
  0.6 5.1 %shard_map.94 = (bf16[16,2,16,1024]{3,2,1,0:T(8,128)(2,1)S(1)}, bf16[16,2,16,1024]{3,2,1,0:T(8,128)(2,1)S(1)}, bf16[512,2048]{1,0:T(8,128)(2,1)S(1)}, bf16[512,2...) custom-call(s32[1]{0:T(128)} %bitcast.core_ref, bf16[512,512]{1,0:T(8,128)(2,1)} %x_hbm.1, s32[4,512]{1,0:T(4,128)} %bitcast.17, ...), custom_call_target="tpu_custom_call" | custom-call | flops 3000000000 | bytes 8388608 | tf_op jit(solution)/shard_map/pallas_call | solution.py:55
  5.7 3.3 %collective-permute-start.1 = (bf16[16,2,16,1024]{3,2,1,0:T(8,128)(2,1)S(1)}, bf16[16,2,16,1024]{3,2,1,0:T(8,128)(2,1)S(1)}, u32[]{:S(2)}, u32[]{:S(2)}) collective-permute-start(bf16[16,2,16,1024]{3,2,1,0:T(8,128)(2,1)S(1)} %get-tuple-element.36), channel_id=1, source_target_pairs={{0,1},{1,0},{2,3},{3,2},{4,5},{5,4},{6,7},{7,6},{8,9},{9,8},{10,11... | collective-permute-start | bytes 3145736 | tf_op jit(solution)/shard_map/ppermute | solution.py:361
  9.0 2.0 %shard_map.95 = (bf16[16,2,16,256]{3,2,1,0:T(8,128)(2,1)S(1)}, bf16[16,2,16,256]{3,2,1,0:T(8,128)(2,1)S(1)}, bf16[512,512]{1,0:T(8,128)(2,1)S(1)}) custom-call(s32[1]{0:T(128)} %bitcast.core_ref, bf16[512,2048]{1,0:T(8,128)(2,1)S(1)} %get-tuple-element.30.pre_ref, bf16[512,2048]{1,0:T(8,128)(2,1)S(1)} %get-tuple-element.31.wh_ref, ...), custom_call_target="tpu_custom_call" | custom-call | flops 2000000000 | bytes 6291456 | tf_op jit(solution)/shard_map/pallas_call | solution.py:55
  11.0 0.1 collective-permute-start
  11.1 0.2 collective-permute-done.1.b_ref
  11.3 1.1 %shard_map.96.refs_0_ = bf16[16,2,16,1280]{3,2,1,0:T(8,128)(2,1)} custom-call(bf16[16,2,16,1024]{3,2,1,0:T(8,128)(2,1)S(1)} %get-tuple-element.35.a_ref, bf16[16,2,16,1024]{3,2,1,0:T(8,128)(2,1)S(1)} %collective-permute-done.1.b_ref), custom_call_target="tpu_custom_call" | custom-call | bytes 2097152 | tf_op jit(solution)/shard_map/pallas_call | solution.py:187
  12.4 0.2 collective-permute-done.b_ref
  12.7 0.7 shard_map.97
  13.4 0.0 copy-start.1
  13.4 6.7 %all-to-all-start = ((bf16[32,16,1280]{2,1,0:T(8,128)(2,1)}), bf16[32,16,1280]{2,1,0:T(8,128)(2,1)S(1)}, u32[]{:S(2)}, u32[]{:S(2)}) async-start(bf16[32,16,1280]{2,1,0:T(8,128)(2,1)} %bitcast.19), calls=%async_computation | async-start | bytes 2621440 | tf_op jit(solution)/shard_map/all_to_all | solution.py:364
  20.1 0.0 copy-done.1
  20.1 3.9 %shard_map.99 = (bf16[1040,128]{1,0:T(8,128)(2,1)S(1)}, bf16[1040,128]{1,0:T(8,128)(2,1)S(1)}) custom-call(s32[1]{0:T(128)} %bitcast.core_ref, s32[4,512]{1,0:T(4,128)S(1)} %bitcast.18, bf16[512,512]{1,0:T(8,128)(2,1)S(1)} %get-tuple-element.37.grad_ref), custom_call_target="tpu_custom_call" | custom-call | flops 6000000000 | bytes 8388608 | tf_op jit(solution)/shard_map/pallas_call | solution.py:55
  24.0 0.5 collective-permute-start.5
  24.5 0.1 stack.29.place_ref
  24.6 1.1 %collective-permute-done.5.far_cold_ref = bf16[1040,128]{1,0:T(8,128)(2,1)S(1)} collective-permute-done((bf16[1040,128]{1,0:T(8,128)(2,1)S(1)}, bf16[1040,128]{1,0:T(8,128)(2,1)S(1)}, u32[]{:S(2)}, u32[]{:S(2)}) %collective-permute-start.5) | collective-permute-done | bytes 266272 | tf_op jit(solution)/shard_map/ppermute | solution.py:361
  25.7 0.8 shard_map.100
  26.5 5.5 %collective-permute-start.6 = (bf16[17,4,16,128]{3,2,1,0:T(8,128)(2,1)S(1)}, bf16[17,4,16,128]{3,2,1,0:T(8,128)(2,1)S(1)}, u32[]{:S(2)}, u32[]{:S(2)}) collective-permute-start(bf16[17,4,16,128]{3,2,1,0:T(8,128)(2,1)S(1)} %get-tuple-element.41), channel_id=1, source_target_pairs={{0,14},{1,15},{2,4},{3,5},{4,2},{5,3},{6,8},{7,9},{8,6},{9,7},{10,... | collective-permute-start | bytes 835592 | tf_op jit(solution)/shard_map/ppermute | solution.py:372
  32.0 0.7 pad_add_fusion.at_ref
  32.7 1.4 %shard_map.102.accum_ref = f32[16,256]{1,0:T(8,128)S(1)} custom-call(s32[2]{0:T(128)} %pad_add_fusion.at_ref, f32[2048,128]{1,0:T(8,128)} %bitcast.20, f32[2048,128]{1,0:T(8,128)} %bitcast.21), custom_call_target="tpu_custom_call" | custom-call | tf_op jit(solution)/shard_map/pallas_call | solution.py:240
  34.0 4.7 %collective-permute-done.6.far_ref = bf16[17,4,16,128]{3,2,1,0:T(8,128)(2,1)S(1)} collective-permute-done((bf16[17,4,16,128]{3,2,1,0:T(8,128)(2,1)S(1)}, bf16[17,4,16,128]{3,2,1,0:T(8,128)(2,1)S(1)}, u32[]{:S(2)}, u32[]{:S(2)}) %collective-permute-start.6) | collective-permute-done | bytes 278560 | tf_op jit(solution)/shard_map/ppermute | solution.py:372
  38.7 1.4 %shard_map.101 = bf16[16,9,16,128]{3,2,1,0:T(8,128)(2,1)} custom-call(s32[5]{0:T(128)S(1)} %stack.29.place_ref, bf16[17,4,16,128]{3,2,1,0:T(8,128)(2,1)S(1)} %get-tuple-element.40.keep_ref, bf16[17,4,16,128]{3,2,1,0:T(8,128)(2,1)S(1)} %collective-permute-done.6.far_ref), custom_call_target="tpu_custom_call" | custom-call | bytes 2097152 | tf_op jit(solution)/shard_map/pallas_call | solution.py:55
  40.2 1.1 %all-to-all-done.in_ref = bf16[32,16,1280]{2,1,0:T(8,128)(2,1)S(1)} async-done(((bf16[32,16,1280]{2,1,0:T(8,128)(2,1)}), bf16[32,16,1280]{2,1,0:T(8,128)(2,1)S(1)}, u32[]{:S(2)}, u32[]{:S(2)}) %all-to-all-start) | async-done | bytes 1310752 | tf_op jit(solution)/shard_map/all_to_all | solution.py:364
  41.2 5.6 %all-to-all-start.2 = ((bf16[16,9,16,128]{3,2,1,0:T(8,128)(2,1)}), bf16[16,9,16,128]{3,2,1,0:T(8,128)(2,1)S(1)}, u32[]{:S(2)}, u32[]{:S(2)}) async-start(bf16[16,9,16,128]{3,2,1,0:T(8,128)(2,1)} %shard_map.101), calls=%async_computation.2 | async-start | bytes 1179648 | tf_op jit(solution)/shard_map/all_to_all | solution.py:364
  46.8 0.2 shard_map.98.a_ref
  47.0 3.3 %collective-permute-start.2 = (bf16[16,1280]{1,0:T(8,128)(2,1)S(1)}, bf16[16,1280]{1,0:T(8,128)(2,1)S(1)}, u32[]{:S(2)}, u32[]{:S(2)}) collective-permute-start(bf16[16,1280]{1,0:T(8,128)(2,1)S(1)} %shard_map.98.a_ref), channel_id=1, source_target_pairs={{0,8},{1,13},{2,10},{3,15},{4,12},{5,9},{6,14},{7,11},{8,0},{9,5},... | collective-permute-start | bytes 122888 | tf_op jit(solution)/shard_map/ppermute | solution.py:361
  50.4 1.2 %collective-permute-start.3 = (bf16[16,1280]{1,0:T(8,128)(2,1)S(1)}, bf16[16,1280]{1,0:T(8,128)(2,1)S(1)}, u32[]{:S(2)}, u32[]{:S(2)}) collective-permute-start(bf16[16,1280]{1,0:T(8,128)(2,1)S(1)} %shard_map.98.a_ref), channel_id=1, source_target_pairs={{0,4},{1,9},{2,6},{3,11},{4,0},{5,13},{6,2},{7,15},{8,12},{9,1},{1... | collective-permute-start | bytes 122888 | tf_op jit(solution)/shard_map/ppermute | solution.py:361
  51.5 1.2 %collective-permute-start.4 = (bf16[16,1280]{1,0:T(8,128)(2,1)S(1)}, bf16[16,1280]{1,0:T(8,128)(2,1)S(1)}, u32[]{:S(2)}, u32[]{:S(2)}) collective-permute-start(bf16[16,1280]{1,0:T(8,128)(2,1)S(1)} %shard_map.98.a_ref), channel_id=1, source_target_pairs={{0,12},{1,5},{2,14},{3,7},{4,8},{5,1},{6,10},{7,3},{8,4},{9,13},{1... | collective-permute-start | bytes 122888 | tf_op jit(solution)/shard_map/ppermute | solution.py:361
  52.8 0.0 collective-permute-done.2.b_ref
  52.8 5.2 %collective-permute-done.3.c_ref = bf16[16,1280]{1,0:T(8,128)(2,1)S(1)} collective-permute-done((bf16[16,1280]{1,0:T(8,128)(2,1)S(1)}, bf16[16,1280]{1,0:T(8,128)(2,1)S(1)}, u32[]{:S(2)}, u32[]{:S(2)}) %collective-permute-start.3) | collective-permute-done | bytes 40992 | tf_op jit(solution)/shard_map/ppermute | solution.py:361
  57.9 0.0 collective-permute-done.4.d_ref
  58.0 0.1 collective-permute-start.7
  58.1 1.0 %shard_map.104.refs_0_ = bf16[16,2,16,1280]{3,2,1,0:T(8,128)(2,1)} custom-call(s32[1]{0:T(128)} %bitcast.1.part_ref, bf16[16,1280]{1,0:T(8,128)(2,1)S(1)} %shard_map.103.in_ref), custom_call_target="tpu_custom_call" | custom-call | bytes 2097152 | tf_op jit(solution)/shard_map/pallas_call | solution.py:273
  59.0 1.9 %collective-permute-done.7.in_ref = bf16[16,1280]{1,0:T(8,128)(2,1)S(1)} collective-permute-done((bf16[16,1280]{1,0:T(8,128)(2,1)S(1)}, bf16[16,1280]{1,0:T(8,128)(2,1)S(1)}, u32[]{:S(2)}, u32[]{:S(2)}) %collective-permute-start.7) | collective-permute-done | bytes 40992 | tf_op jit(solution)/shard_map/ppermute | solution.py:361
  60.9 1.0 %shard_map.105 = bf16[16,2,16,1280]{3,2,1,0:T(8,128)(2,1)} custom-call(s32[1]{0:T(128)S(6)} %sub.11.part_ref, bf16[16,1280]{1,0:T(8,128)(2,1)S(1)} %collective-permute-done.7.in_ref, bf16[16,2,16,1280]{3,2,1,0:T(8,128)(2,1)} %shard_map.104.refs_0_), custom_call_target="tpu_custom_call", output_to_operand_aliasing={{}: (2, {})} | custom-call | bytes 2097152 | tf_op jit(solution)/shard_map/pallas_call | solution.py:273
  61.9 0.0 all-to-all-done.2.in_ref
  61.9 8.2 %all-to-all-start.1 = ((bf16[16,2,16,1280]{3,2,1,0:T(8,128)(2,1)}), bf16[16,2,16,1280]{3,2,1,0:T(8,128)(2,1)S(1)}, u32[]{:S(2)}, u32[]{:S(2)}) async-start(bf16[16,2,16,1280]{3,2,1,0:T(8,128)(2,1)} %shard_map.105), calls=%async_computation.1 | async-start | bytes 2621440 | tf_op jit(solution)/shard_map/all_to_all | solution.py:364
  70.1 1.6 %shard_map.106 = (bf16[256,128]{1,0:T(8,128)(2,1)S(1)}, bf16[256,128]{1,0:T(8,128)(2,1)S(1)}, bf16[256,128]{1,0:T(8,128)(2,1)S(1)}, bf16[256,128]{1,0:T(8,128)(2,1)S(1)}) custom-call(s32[5]{0:T(128)S(1)} %stack.29.place_ref, bf16[16,9,16,128]{3,2,1,0:T(8,128)(2,1)S(1)} %all-to-all-done.2.in_ref), custom_call_target="tpu_custom_call" | custom-call | flops 1000000000 | bytes 2097152 | tf_op jit(solution)/shard_map/pallas_call | solution.py:55
  71.7 0.0 copy-start
  71.7 1.2 %collective-permute-start.10 = (bf16[256,128]{1,0:T(8,128)(2,1)S(1)}, bf16[256,128]{1,0:T(8,128)(2,1)S(1)}, u32[]{:S(2)}, u32[]{:S(2)}) collective-permute-start(bf16[256,128]{1,0:T(8,128)(2,1)S(1)} %get-tuple-element.47), channel_id=1, source_target_pairs={{0,4},{1,13},{2,14},{3,7},{4,0},{5,9},{6,10},{7,3},{8,12},{9,5},{1... | collective-permute-start | bytes 196616 | tf_op jit(solution)/shard_map/ppermute | solution.py:372
  72.9 2.2 %collective-permute-start.8 = (bf16[256,128]{1,0:T(8,128)(2,1)S(1)}, bf16[256,128]{1,0:T(8,128)(2,1)S(1)}, u32[]{:S(2)}, u32[]{:S(2)}) collective-permute-start(bf16[256,128]{1,0:T(8,128)(2,1)S(1)} %get-tuple-element.45), channel_id=1, source_target_pairs={{0,8},{1,5},{2,10},{3,15},{4,12},{5,1},{6,14},{7,11},{8,0},{9,13},... | collective-permute-start | bytes 196616 | tf_op jit(solution)/shard_map/ppermute | solution.py:372
  75.1 2.4 %collective-permute-start.9 = (bf16[256,128]{1,0:T(8,128)(2,1)S(1)}, bf16[256,128]{1,0:T(8,128)(2,1)S(1)}, u32[]{:S(2)}, u32[]{:S(2)}) collective-permute-start(bf16[256,128]{1,0:T(8,128)(2,1)S(1)} %get-tuple-element.46), channel_id=1, source_target_pairs={{0,12},{1,9},{2,6},{3,11},{4,8},{5,13},{6,2},{7,15},{8,4},{9,1},{1... | collective-permute-start | bytes 196616 | tf_op jit(solution)/shard_map/ppermute | solution.py:372
  77.5 0.0 collective-permute-done.10.d_ref
  77.5 0.0 collective-permute-done.8.b_ref
  77.5 5.7 %collective-permute-done.9.c_ref = bf16[256,128]{1,0:T(8,128)(2,1)S(1)} collective-permute-done((bf16[256,128]{1,0:T(8,128)(2,1)S(1)}, bf16[256,128]{1,0:T(8,128)(2,1)S(1)}, u32[]{:S(2)}, u32[]{:S(2)}) %collective-permute-start.9) | collective-permute-done | bytes 65568 | tf_op jit(solution)/shard_map/ppermute | solution.py:372
  83.1 0.0 all-to-all-done.1.in_ref
  83.1 4.1 %collective-permute-start.11 = (bf16[16,2,16,1280]{3,2,1,0:T(8,128)(2,1)S(1)}, bf16[16,2,16,1280]{3,2,1,0:T(8,128)(2,1)S(1)}, u32[]{:S(2)}, u32[]{:S(2)}) collective-permute-start(bf16[16,2,16,1280]{3,2,1,0:T(8,128)(2,1)S(1)} %all-to-all-done.1.in_ref), channel_id=1, source_target_pairs={{0,1},{1,0},{2,3},{3,2},{4,5},{5,4},{6,7},{7,6},{8,9},{9,8},{10,11... | collective-permute-start | bytes 3932168 | tf_op jit(solution)/shard_map/ppermute | solution.py:361
  87.2 1.2 %shard_map.107 = (bf16[512,2048]{1,0:T(8,128)(2,1)}, f32[2048,128]{1,0:T(8,128)}) custom-call(s32[1]{0:T(128)} %bitcast.core_ref, bf16[16,2,16,1280]{3,2,1,0:T(8,128)(2,1)S(1)} %all-to-all-done.1.in_ref), custom_call_target="tpu_custom_call" | custom-call | bytes 4194304 | tf_op jit(solution)/shard_map/pallas_call | solution.py:330
  88.5 0.0 copy-done
  88.5 0.7 shard_map.109
  89.2 0.7 collective-permute-done.11.in_ref
  89.9 1.2 %shard_map.108 = (bf16[512,2048]{1,0:T(8,128)(2,1)}, f32[2048,128]{1,0:T(8,128)}) custom-call(s32[1]{0:T(128)S(6)} %sub.10.core_ref, bf16[16,2,16,1280]{3,2,1,0:T(8,128)(2,1)S(1)} %collective-permute-done.11.in_ref, bf16[512,2048]{1,0:T(8,128)(2,1)} %get-tuple-element.49.refs_0_, ...), custom_call_target="tpu_custom_call", output_to_operand_aliasing={{0}: (2, {}), {1}: (3, {})} | custom-call | bytes 4194304 | tf_op jit(solution)/shard_map/pallas_call | solution.py:330
  (1 shorter events, 0.0 us)
Async XLA Ops:
  5.7 5.6 %collective-permute-start.1 = (bf16[16,2,16,1024]{3,2,1,0:T(8,128)(2,1)S(1)}, bf16[16,2,16,1024]{3,2,1,0:T(8,128)(2,1)S(1)}, u32[]{:S(2)}, u32[]{:S(2)}) collective-permute-start(bf16[16,2,16,1024]{3,2,1,0:T(8,128)(2,1)S(1)} %get-tuple-element.36), channel_id=1, source_target_pairs={{0,1},{1,0},{2,3},{3,2},{4,5},{5,4},{6,7},{7,6},{8,9},{9,8},{10,11... | collective-permute-start | bytes 3145736 | tf_op jit(solution)/shard_map/ppermute | solution.py:361
  11.0 1.6 %collective-permute-start = (bf16[16,2,16,256]{3,2,1,0:T(8,128)(2,1)S(1)}, bf16[16,2,16,256]{3,2,1,0:T(8,128)(2,1)S(1)}, u32[]{:S(2)}, u32[]{:S(2)}) collective-permute-start(bf16[16,2,16,256]{3,2,1,0:T(8,128)(2,1)S(1)} %get-tuple-element.34), channel_id=1, source_target_pairs={{0,1},{1,0},{2,3},{3,2},{4,5},{5,4},{6,7},{7,6},{8,9},{9,8},{10,11... | collective-permute-start | bytes 786440 | tf_op jit(solution)/shard_map/ppermute | solution.py:361
  13.4 6.7 %copy-start.1 = (s32[512,4]{0,1:T(4,128)S(1)}, s32[512,4]{0,1:T(4,128)}, u32[]{:S(2)}) copy-start(s32[512,4]{0,1:T(4,128)} %param.8) | copy-start | bytes 24580
  13.4 27.8 %all-to-all-start = ((bf16[32,16,1280]{2,1,0:T(8,128)(2,1)}), bf16[32,16,1280]{2,1,0:T(8,128)(2,1)S(1)}, u32[]{:S(2)}, u32[]{:S(2)}) async-start(bf16[32,16,1280]{2,1,0:T(8,128)(2,1)} %bitcast.19), calls=%async_computation | async-start | bytes 2621440 | tf_op jit(solution)/shard_map/all_to_all | solution.py:364
  24.0 1.7 %collective-permute-start.5 = (bf16[1040,128]{1,0:T(8,128)(2,1)S(1)}, bf16[1040,128]{1,0:T(8,128)(2,1)S(1)}, u32[]{:S(2)}, u32[]{:S(2)}) collective-permute-start(bf16[1040,128]{1,0:T(8,128)(2,1)S(1)} %get-tuple-element.39), channel_id=1, source_target_pairs={{0,1},{1,0},{2,3},{3,2},{4,5},{5,4},{6,7},{7,6},{8,9},{9,8},{10,11... | collective-permute-start | bytes 798728 | tf_op jit(solution)/shard_map/ppermute | solution.py:361
  26.5 12.3 %collective-permute-start.6 = (bf16[17,4,16,128]{3,2,1,0:T(8,128)(2,1)S(1)}, bf16[17,4,16,128]{3,2,1,0:T(8,128)(2,1)S(1)}, u32[]{:S(2)}, u32[]{:S(2)}) collective-permute-start(bf16[17,4,16,128]{3,2,1,0:T(8,128)(2,1)S(1)} %get-tuple-element.41), channel_id=1, source_target_pairs={{0,14},{1,15},{2,4},{3,5},{4,2},{5,3},{6,8},{7,9},{8,6},{9,7},{10,... | collective-permute-start | bytes 835592 | tf_op jit(solution)/shard_map/ppermute | solution.py:372
  41.2 20.7 %all-to-all-start.2 = ((bf16[16,9,16,128]{3,2,1,0:T(8,128)(2,1)}), bf16[16,9,16,128]{3,2,1,0:T(8,128)(2,1)S(1)}, u32[]{:S(2)}, u32[]{:S(2)}) async-start(bf16[16,9,16,128]{3,2,1,0:T(8,128)(2,1)} %shard_map.101), calls=%async_computation.2 | async-start | bytes 1179648 | tf_op jit(solution)/shard_map/all_to_all | solution.py:364
  47.0 5.7 %collective-permute-start.2 = (bf16[16,1280]{1,0:T(8,128)(2,1)S(1)}, bf16[16,1280]{1,0:T(8,128)(2,1)S(1)}, u32[]{:S(2)}, u32[]{:S(2)}) collective-permute-start(bf16[16,1280]{1,0:T(8,128)(2,1)S(1)} %shard_map.98.a_ref), channel_id=1, source_target_pairs={{0,8},{1,13},{2,10},{3,15},{4,12},{5,9},{6,14},{7,11},{8,0},{9,5},... | collective-permute-start | bytes 122888 | tf_op jit(solution)/shard_map/ppermute | solution.py:361
  50.4 7.6 %collective-permute-start.3 = (bf16[16,1280]{1,0:T(8,128)(2,1)S(1)}, bf16[16,1280]{1,0:T(8,128)(2,1)S(1)}, u32[]{:S(2)}, u32[]{:S(2)}) collective-permute-start(bf16[16,1280]{1,0:T(8,128)(2,1)S(1)} %shard_map.98.a_ref), channel_id=1, source_target_pairs={{0,4},{1,9},{2,6},{3,11},{4,0},{5,13},{6,2},{7,15},{8,12},{9,1},{1... | collective-permute-start | bytes 122888 | tf_op jit(solution)/shard_map/ppermute | solution.py:361
  51.5 6.4 %collective-permute-start.4 = (bf16[16,1280]{1,0:T(8,128)(2,1)S(1)}, bf16[16,1280]{1,0:T(8,128)(2,1)S(1)}, u32[]{:S(2)}, u32[]{:S(2)}) collective-permute-start(bf16[16,1280]{1,0:T(8,128)(2,1)S(1)} %shard_map.98.a_ref), channel_id=1, source_target_pairs={{0,12},{1,5},{2,14},{3,7},{4,8},{5,1},{6,10},{7,3},{8,4},{9,13},{1... | collective-permute-start | bytes 122888 | tf_op jit(solution)/shard_map/ppermute | solution.py:361
  58.0 2.9 %collective-permute-start.7 = (bf16[16,1280]{1,0:T(8,128)(2,1)S(1)}, bf16[16,1280]{1,0:T(8,128)(2,1)S(1)}, u32[]{:S(2)}, u32[]{:S(2)}) collective-permute-start(bf16[16,1280]{1,0:T(8,128)(2,1)S(1)} %shard_map.103.in_ref), channel_id=1, source_target_pairs={{0,2},{1,3},{2,0},{3,1},{4,6},{5,7},{6,4},{7,5},{8,10},{9,11},{10,... | collective-permute-start | bytes 122888 | tf_op jit(solution)/shard_map/ppermute | solution.py:361
  61.9 21.2 %all-to-all-start.1 = ((bf16[16,2,16,1280]{3,2,1,0:T(8,128)(2,1)}), bf16[16,2,16,1280]{3,2,1,0:T(8,128)(2,1)S(1)}, u32[]{:S(2)}, u32[]{:S(2)}) async-start(bf16[16,2,16,1280]{3,2,1,0:T(8,128)(2,1)} %shard_map.105), calls=%async_computation.1 | async-start | bytes 2621440 | tf_op jit(solution)/shard_map/all_to_all | solution.py:364
  71.7 16.8 %copy-start = (f32[4,64,128]{2,1,0:T(8,128)S(1)}, f32[4,64,128]{2,1,0:T(8,128)}, u32[]{:S(2)}) copy-start(f32[4,64,128]{2,1,0:T(8,128)} %param.13) | copy-start | bytes 393220
  71.7 5.7 %collective-permute-start.10 = (bf16[256,128]{1,0:T(8,128)(2,1)S(1)}, bf16[256,128]{1,0:T(8,128)(2,1)S(1)}, u32[]{:S(2)}, u32[]{:S(2)}) collective-permute-start(bf16[256,128]{1,0:T(8,128)(2,1)S(1)} %get-tuple-element.47), channel_id=1, source_target_pairs={{0,4},{1,13},{2,14},{3,7},{4,0},{5,9},{6,10},{7,3},{8,12},{9,5},{1... | collective-permute-start | bytes 196616 | tf_op jit(solution)/shard_map/ppermute | solution.py:372
  72.9 4.5 %collective-permute-start.8 = (bf16[256,128]{1,0:T(8,128)(2,1)S(1)}, bf16[256,128]{1,0:T(8,128)(2,1)S(1)}, u32[]{:S(2)}, u32[]{:S(2)}) collective-permute-start(bf16[256,128]{1,0:T(8,128)(2,1)S(1)} %get-tuple-element.45), channel_id=1, source_target_pairs={{0,8},{1,5},{2,10},{3,15},{4,12},{5,1},{6,14},{7,11},{8,0},{9,13},... | collective-permute-start | bytes 196616 | tf_op jit(solution)/shard_map/ppermute | solution.py:372
  75.1 8.0 %collective-permute-start.9 = (bf16[256,128]{1,0:T(8,128)(2,1)S(1)}, bf16[256,128]{1,0:T(8,128)(2,1)S(1)}, u32[]{:S(2)}, u32[]{:S(2)}) collective-permute-start(bf16[256,128]{1,0:T(8,128)(2,1)S(1)} %get-tuple-element.46), channel_id=1, source_target_pairs={{0,12},{1,9},{2,6},{3,11},{4,8},{5,13},{6,2},{7,15},{8,4},{9,1},{1... | collective-permute-start | bytes 196616 | tf_op jit(solution)/shard_map/ppermute | solution.py:372
  83.1 6.8 %collective-permute-start.11 = (bf16[16,2,16,1280]{3,2,1,0:T(8,128)(2,1)S(1)}, bf16[16,2,16,1280]{3,2,1,0:T(8,128)(2,1)S(1)}, u32[]{:S(2)}, u32[]{:S(2)}) collective-permute-start(bf16[16,2,16,1280]{3,2,1,0:T(8,128)(2,1)S(1)} %all-to-all-done.1.in_ref), channel_id=1, source_target_pairs={{0,1},{1,0},{2,3},{3,2},{4,5},{5,4},{6,7},{7,6},{8,9},{9,8},{10,11... | collective-permute-start | bytes 3932168 | tf_op jit(solution)/shard_map/ppermute | solution.py:361

commit v6 on v5

--- a/solution.py
+++ b/solution.py
@@ -178,18 +178,23 @@
     rest = () if held is None else (held,)
 
     def kernel(a_ref, b_ref, *refs):
-        out_hbm, sum_ref, sem = refs[-3:]
-        sum_ref[...] = a_ref[...] + b_ref[...]
-        copy = pltpu.make_async_copy(sum_ref, out_hbm.at[:, :, :, pl.ds(at, width)], sem)
-        copy.start()
-        copy.wait()
+        out_hbm, sum_ref, sems = refs[-3:]
+        step = NODES // 4
+        copies = []
+        for j in range(4):
+            rows = pl.ds(j * step, step)
+            sum_ref[rows] = a_ref[rows] + b_ref[rows]
+            copies.append(pltpu.make_async_copy(sum_ref.at[rows], out_hbm.at[rows, :, :, pl.ds(at, width)], sems.at[j]))
+            copies[-1].start()
+        for copy in copies:
+            copy.wait()
 
     return pl.pallas_call(
         kernel,
         out_shape=pltpu.HBM((NODES, ZP, CHUNK, WIDE), BF),
         in_specs=[VMEM] * 2 + [HBM] * len(rest),
         out_specs=HBM,
-        scratch_shapes=[pltpu.VMEM(a.shape, BF), pltpu.SemaphoreType.DMA],
+        scratch_shapes=[pltpu.VMEM(a.shape, BF), pltpu.SemaphoreType.DMA((4,))],
         input_output_aliases={2: 0} if rest else {},
         compiler_params=pltpu.CompilerParams(vmem_limit_bytes=8 * MIB),
         cost_estimate=pl.CostEstimate(flops=0, bytes_accessed=2 * MIB, transcendentals=0),
@@ -260,9 +265,12 @@
 
 
 def spread_kernel(part_ref, in_ref, *refs):
-    out_hbm, sems = refs[-2:]
-    part = part_ref[0]
-    copies = [pltpu.make_async_copy(in_ref, out_hbm.at[n, part], sems.at[n]) for n in range(NODES)]
+    out_hbm, many_ref, sems = refs[-3:]
+    half = NODES // 2
+    many_ref[...] = jnp.broadcast_to(in_ref[...][None], many_ref.shape)
+    copies = [
+        pltpu.make_async_copy(many_ref, out_hbm.at[pl.ds(k * half, half), part_ref[0]], sems.at[k]) for k in range(2)
+    ]
     for copy in copies:
         copy.start()
     for copy in copies:
@@ -275,7 +283,7 @@
         out_shape=pltpu.HBM((NODES, ZP, CHUNK, WIDE), BF),
         in_specs=[SMEM, VMEM] + [HBM] * len(held),
         out_specs=HBM,
-        scratch_shapes=[pltpu.SemaphoreType.DMA((NODES,))],
+        scratch_shapes=[pltpu.VMEM((NODES // 2, CHUNK, WIDE), BF), pltpu.SemaphoreType.DMA((2,))],
         input_output_aliases={2: 0} if held else {},
         compiler_params=pltpu.CompilerParams(vmem_limit_bytes=4 * MIB),
         cost_estimate=pl.CostEstimate(flops=0, bytes_accessed=2 * MIB, transcendentals=0),
@@ -448,20 +456,21 @@
     slab, accum = lax.optimization_barrier((slab, accum))
     part = call(group_sum_kernel, shape(CHUNK, WIDE), (parts,), size=2 * MIB)
     slab = exchange(slab, by_node)
-    quad = [part] + [flip(part, 4 * d, 4 * e) for d, e in zip((2, 1, 3), (3, 2, 1))]
+    quad = [part] + [flip(part, 4 * d, 4 * e) for d, e in zip((2, 1, 3), (2, 3, 1))]
+    cold = call(
+        cold_dense_kernel,
+        tuple(shape(TABLES * COLD_DEV, E) for _ in range(ZQ)),
+        (place, slab),
+        scalars=1,
+        flops=10**9,
+        size=2 * MIB,
+    )
+    quad, cold = lax.optimization_barrier((quad, cold))
     done = call(step_kernel, pltpu.VMEM((CHUNK, WIDE), BF), (*quad, accum))
     beside = flip(done, 2)
     whole = spread(zp.reshape(1), done)
     whole = spread(1 - zp.reshape(1), beside, (whole,))
     half = exchange(whole, alone)
-    cold = call(
-        cold_dense_kernel,
-        tuple(shape(TABLES * COLD_DEV, E) for _ in range(ZQ)),
-        (place, slab),
-        scalars=1,
-        flops=10**9,
-        size=2 * MIB,
-    )
     cold = [cold[0]] + [
         turned_flip(cold[k], 2 * COLD_ORDER[0][k], 2 * COLD_ORDER[1][k]) for k in range(1, ZQ)
     ]

time: 91.6 us -> 90.9 us (level)
    all_to_all x3, waiting for transfers between devices: 1.07 us -> 6.15 us  [exchange(): lax.all_to_all(array, 'all', 0, 0, axis_index_groups=groups, tiled=True)]
    ppermute x8, waiting for transfers between devices: 9.22 us -> 4.21 us  [flip(): lax.ppermute(array, 'all', [(i, i ^ masks[i & 1]) for i in range(OWNERS)])]
    all_to_all x3, starting transfers between devices: 20.5 us -> 18.4 us  [exchange(): lax.all_to_all(array, 'all', 0, 0, axis_index_groups=groups, tiled=True)]
    ppermute x8, starting transfers between devices: 13.9 us -> 15.7 us  [flip(): lax.ppermute(array, 'all', [(i, i ^ masks[i & 1]) for i in range(OWNERS)])]
  transfers between devices with their start and end apart: 15 -> 15, of which waited for: 9 -> 11; matrix products, arithmetic and copies ran while one was open for 1% -> 1% of each run, Pallas kernels for 18% -> 17%
where the time goes in v6:
time: 90.9 us; the launch traced here: 90.4 us
  starting transfers between devices  45.4 us (50%)
  Pallas kernels  23 us (25%)
  waiting for transfers between devices  20.5 us (23%)
    all_to_all x3, starting transfers between devices, exchange(): lax.all_to_all(array, 'all', 0, 0, axis_index_groups=groups, tiled=True)  18.4 us
    pallas_call x9, Pallas kernels, call(): pl.pallas_call(kernel, out_shape=out_shape, in_specs=[SMEM] * scalars + [...  15.7 us
    ppermute x8, starting transfers between devices, flip(): lax.ppermute(array, 'all', [(i, i ^ masks[i & 1]) for i in range(OWNERS)])  15.7 us
    ppermute x4, starting transfers between devices, turned_flip(): return lax.ppermute(array, 'all', [(i, partner(i)) for i in range(OWNERS)])  11.3 us
    ppermute x4, waiting for transfers between devices, turned_flip(): return lax.ppermute(array, 'all', [(i, partner(i)) for i in range(OWNERS)])  10.1 us
    all_to_all x3, waiting for transfers between devices, exchange(): lax.all_to_all(array, 'all', 0, 0, axis_index_groups=groups, tiled=True)  6.15 us
    ppermute x8, waiting for transfers between devices, flip(): lax.ppermute(array, 'all', [(i, i ^ masks[i & 1]) for i in range(OWNERS)])  4.21 us
    pallas_call x2, Pallas kernels, finish(): pl.pallas_call(finish_kernel, out_shape=(shape(FEAT, HID), shape(TABLES *...  2.48 us
  transfers between devices with their start and end apart: 15, of which 11 were waited for; matrix products, arithmetic and copies ran while one was open for 1% of the time, Pallas kernels for 17%

profile of v6, /device:TPU:1, one launch (start us, length us, event | category | flops | bytes accessed | tf_op | source)
XLA Modules:
  0.0 90.4 jit_solution(12482795636106328341)
XLA Ops:
  0.6 5.1 %shard_map.94 = (bf16[16,2,16,1024]{3,2,1,0:T(8,128)(2,1)S(1)}, bf16[16,2,16,1024]{3,2,1,0:T(8,128)(2,1)S(1)}, bf16[512,2048]{1,0:T(8,128)(2,1)S(1)}, bf16[512,2...) custom-call(s32[1]{0:T(128)} %bitcast.core_ref, bf16[512,512]{1,0:T(8,128)(2,1)} %x_hbm.1, s32[4,512]{1,0:T(4,128)} %bitcast.17, ...), custom_call_target="tpu_custom_call" | custom-call | flops 3000000000 | bytes 8388608 | tf_op jit(solution)/shard_map/pallas_call | solution.py:55
  5.7 3.3 %collective-permute-start.1 = (bf16[16,2,16,1024]{3,2,1,0:T(8,128)(2,1)S(1)}, bf16[16,2,16,1024]{3,2,1,0:T(8,128)(2,1)S(1)}, u32[]{:S(2)}, u32[]{:S(2)}) collective-permute-start(bf16[16,2,16,1024]{3,2,1,0:T(8,128)(2,1)S(1)} %get-tuple-element.44), channel_id=1, source_target_pairs={{0,1},{1,0},{2,3},{3,2},{4,5},{5,4},{6,7},{7,6},{8,9},{9,8},{10,11... | collective-permute-start | bytes 3145736 | tf_op jit(solution)/shard_map/ppermute | solution.py:369
  9.0 2.0 %shard_map.95 = (bf16[16,2,16,256]{3,2,1,0:T(8,128)(2,1)S(1)}, bf16[16,2,16,256]{3,2,1,0:T(8,128)(2,1)S(1)}, bf16[512,512]{1,0:T(8,128)(2,1)S(1)}) custom-call(s32[1]{0:T(128)} %bitcast.core_ref, bf16[512,2048]{1,0:T(8,128)(2,1)S(1)} %get-tuple-element.38.pre_ref, bf16[512,2048]{1,0:T(8,128)(2,1)S(1)} %get-tuple-element.39.wh_ref, ...), custom_call_target="tpu_custom_call" | custom-call | flops 2000000000 | bytes 6291456 | tf_op jit(solution)/shard_map/pallas_call | solution.py:55
  11.0 0.1 collective-permute-start
  11.1 0.2 collective-permute-done.1.b_ref
  11.3 1.0 %shard_map.96.refs_0_ = bf16[16,2,16,1280]{3,2,1,0:T(8,128)(2,1)} custom-call(bf16[16,2,16,1024]{3,2,1,0:T(8,128)(2,1)S(1)} %get-tuple-element.43.a_ref, bf16[16,2,16,1024]{3,2,1,0:T(8,128)(2,1)S(1)} %collective-permute-done.1.b_ref), custom_call_target="tpu_custom_call" | custom-call | bytes 2097152 | tf_op jit(solution)/shard_map/pallas_call | solution.py:192
  12.4 0.3 collective-permute-done.b_ref
  12.7 0.7 shard_map.97
  13.4 0.0 copy-start.1
  13.4 6.7 %all-to-all-start = ((bf16[32,16,1280]{2,1,0:T(8,128)(2,1)}), bf16[32,16,1280]{2,1,0:T(8,128)(2,1)S(1)}, u32[]{:S(2)}, u32[]{:S(2)}) async-start(bf16[32,16,1280]{2,1,0:T(8,128)(2,1)} %bitcast.19), calls=%async_computation | async-start | bytes 2621440 | tf_op jit(solution)/shard_map/all_to_all | solution.py:372
  20.1 0.0 copy-done.1
  20.1 3.9 %shard_map.99 = (bf16[1040,128]{1,0:T(8,128)(2,1)S(1)}, bf16[1040,128]{1,0:T(8,128)(2,1)S(1)}) custom-call(s32[1]{0:T(128)} %bitcast.core_ref, s32[4,512]{1,0:T(4,128)S(1)} %bitcast.18, bf16[512,512]{1,0:T(8,128)(2,1)S(1)} %get-tuple-element.45.grad_ref), custom_call_target="tpu_custom_call" | custom-call | flops 6000000000 | bytes 8388608 | tf_op jit(solution)/shard_map/pallas_call | solution.py:55
  24.0 0.5 collective-permute-start.5
  24.5 0.1 stack.29.place_ref
  24.6 1.1 %collective-permute-done.5.far_cold_ref = bf16[1040,128]{1,0:T(8,128)(2,1)S(1)} collective-permute-done((bf16[1040,128]{1,0:T(8,128)(2,1)S(1)}, bf16[1040,128]{1,0:T(8,128)(2,1)S(1)}, u32[]{:S(2)}, u32[]{:S(2)}) %collective-permute-start.5) | collective-permute-done | bytes 266272 | tf_op jit(solution)/shard_map/ppermute | solution.py:369
  25.7 0.8 shard_map.100
  26.4 5.5 %collective-permute-start.6 = (bf16[17,4,16,128]{3,2,1,0:T(8,128)(2,1)S(1)}, bf16[17,4,16,128]{3,2,1,0:T(8,128)(2,1)S(1)}, u32[]{:S(2)}, u32[]{:S(2)}) collective-permute-start(bf16[17,4,16,128]{3,2,1,0:T(8,128)(2,1)S(1)} %get-tuple-element.49), channel_id=1, source_target_pairs={{0,14},{1,15},{2,4},{3,5},{4,2},{5,3},{6,8},{7,9},{8,6},{9,7},{10,... | collective-permute-start | bytes 835592 | tf_op jit(solution)/shard_map/ppermute | solution.py:380
  32.0 0.7 pad_add_fusion.at_ref
  32.6 1.4 %shard_map.102.accum_ref = f32[16,256]{1,0:T(8,128)S(1)} custom-call(s32[2]{0:T(128)} %pad_add_fusion.at_ref, f32[2048,128]{1,0:T(8,128)} %bitcast.20, f32[2048,128]{1,0:T(8,128)} %bitcast.21), custom_call_target="tpu_custom_call" | custom-call | tf_op jit(solution)/shard_map/pallas_call | solution.py:245
  34.0 4.7 %collective-permute-done.6.far_ref = bf16[17,4,16,128]{3,2,1,0:T(8,128)(2,1)S(1)} collective-permute-done((bf16[17,4,16,128]{3,2,1,0:T(8,128)(2,1)S(1)}, bf16[17,4,16,128]{3,2,1,0:T(8,128)(2,1)S(1)}, u32[]{:S(2)}, u32[]{:S(2)}) %collective-permute-start.6) | collective-permute-done | bytes 278560 | tf_op jit(solution)/shard_map/ppermute | solution.py:380
  38.7 1.4 %shard_map.101 = bf16[16,9,16,128]{3,2,1,0:T(8,128)(2,1)} custom-call(s32[5]{0:T(128)S(1)} %stack.29.place_ref, bf16[17,4,16,128]{3,2,1,0:T(8,128)(2,1)S(1)} %get-tuple-element.48.keep_ref, bf16[17,4,16,128]{3,2,1,0:T(8,128)(2,1)S(1)} %collective-permute-done.6.far_ref), custom_call_target="tpu_custom_call" | custom-call | bytes 2097152 | tf_op jit(solution)/shard_map/pallas_call | solution.py:55
  40.1 1.1 %all-to-all-done.in_ref = bf16[32,16,1280]{2,1,0:T(8,128)(2,1)S(1)} async-done(((bf16[32,16,1280]{2,1,0:T(8,128)(2,1)}), bf16[32,16,1280]{2,1,0:T(8,128)(2,1)S(1)}, u32[]{:S(2)}, u32[]{:S(2)}) %all-to-all-start) | async-done | bytes 1310752 | tf_op jit(solution)/shard_map/all_to_all | solution.py:372
  41.2 5.6 %all-to-all-start.1 = ((bf16[16,9,16,128]{3,2,1,0:T(8,128)(2,1)}), bf16[16,9,16,128]{3,2,1,0:T(8,128)(2,1)S(1)}, u32[]{:S(2)}, u32[]{:S(2)}) async-start(bf16[16,9,16,128]{3,2,1,0:T(8,128)(2,1)} %shard_map.101), calls=%async_computation.1 | async-start | bytes 1179648 | tf_op jit(solution)/shard_map/all_to_all | solution.py:372
  46.8 0.2 shard_map.98.a_ref
  47.0 4.3 %collective-permute-start.2 = (bf16[16,1280]{1,0:T(8,128)(2,1)S(1)}, bf16[16,1280]{1,0:T(8,128)(2,1)S(1)}, u32[]{:S(2)}, u32[]{:S(2)}) collective-permute-start(bf16[16,1280]{1,0:T(8,128)(2,1)S(1)} %shard_map.98.a_ref), channel_id=1, source_target_pairs={{0,8},{1,9},{2,10},{3,11},{4,12},{5,13},{6,14},{7,15},{8,0},{9,1},... | collective-permute-start | bytes 122888 | tf_op jit(solution)/shard_map/ppermute | solution.py:369
  51.3 0.3 collective-permute-start.3
  51.5 1.2 %collective-permute-start.4 = (bf16[16,1280]{1,0:T(8,128)(2,1)S(1)}, bf16[16,1280]{1,0:T(8,128)(2,1)S(1)}, u32[]{:S(2)}, u32[]{:S(2)}) collective-permute-start(bf16[16,1280]{1,0:T(8,128)(2,1)S(1)} %shard_map.98.a_ref), channel_id=1, source_target_pairs={{0,12},{1,5},{2,14},{3,7},{4,8},{5,1},{6,10},{7,3},{8,4},{9,13},{1... | collective-permute-start | bytes 122888 | tf_op jit(solution)/shard_map/ppermute | solution.py:369
  52.8 5.1 %all-to-all-done.1.in_ref = bf16[16,9,16,128]{3,2,1,0:T(8,128)(2,1)S(1)} async-done(((bf16[16,9,16,128]{3,2,1,0:T(8,128)(2,1)}), bf16[16,9,16,128]{3,2,1,0:T(8,128)(2,1)S(1)}, u32[]{:S(2)}, u32[]{:S(2)}) %all-to-all-start.1) | async-done | bytes 589856 | tf_op jit(solution)/shard_map/all_to_all | solution.py:372
  57.8 1.6 %shard_map.103 = (bf16[256,128]{1,0:T(8,128)(2,1)S(1)}, bf16[256,128]{1,0:T(8,128)(2,1)S(1)}, bf16[256,128]{1,0:T(8,128)(2,1)S(1)}, bf16[256,128]{1,0:T(8,128)(2,1)S(1)}) custom-call(s32[5]{0:T(128)S(1)} %stack.29.place_ref, bf16[16,9,16,128]{3,2,1,0:T(8,128)(2,1)S(1)} %all-to-all-done.1.in_ref), custom_call_target="tpu_custom_call" | custom-call | flops 1000000000 | bytes 2097152 | tf_op jit(solution)/shard_map/pallas_call | solution.py:55
  59.4 0.0 collective-permute-done.2.b_ref
  59.4 0.0 collective-permute-done.3.c_ref
  59.4 0.0 collective-permute-done.4.d_ref
  59.5 0.1 collective-permute-start.7
  59.6 0.9 shard_map.105.refs_0_
  60.5 2.0 %collective-permute-done.7.in_ref = bf16[16,1280]{1,0:T(8,128)(2,1)S(1)} collective-permute-done((bf16[16,1280]{1,0:T(8,128)(2,1)S(1)}, bf16[16,1280]{1,0:T(8,128)(2,1)S(1)}, u32[]{:S(2)}, u32[]{:S(2)}) %collective-permute-start.7) | collective-permute-done | bytes 40992 | tf_op jit(solution)/shard_map/ppermute | solution.py:369
  62.4 0.9 shard_map.106
  63.3 6.2 %all-to-all-start.2 = ((bf16[16,2,16,1280]{3,2,1,0:T(8,128)(2,1)}), bf16[16,2,16,1280]{3,2,1,0:T(8,128)(2,1)S(1)}, u32[]{:S(2)}, u32[]{:S(2)}) async-start(bf16[16,2,16,1280]{3,2,1,0:T(8,128)(2,1)} %shard_map.106), calls=%async_computation.2 | async-start | bytes 2621440 | tf_op jit(solution)/shard_map/all_to_all | solution.py:372
  69.5 0.0 copy-start
  69.5 2.5 %collective-permute-start.10 = (bf16[256,128]{1,0:T(8,128)(2,1)S(1)}, bf16[256,128]{1,0:T(8,128)(2,1)S(1)}, u32[]{:S(2)}, u32[]{:S(2)}) collective-permute-start(bf16[256,128]{1,0:T(8,128)(2,1)S(1)} %get-tuple-element.63), channel_id=1, source_target_pairs={{0,4},{1,13},{2,14},{3,7},{4,0},{5,9},{6,10},{7,3},{8,12},{9,5},{1... | collective-permute-start | bytes 196616 | tf_op jit(solution)/shard_map/ppermute | solution.py:380
  72.0 1.2 %collective-permute-start.8 = (bf16[256,128]{1,0:T(8,128)(2,1)S(1)}, bf16[256,128]{1,0:T(8,128)(2,1)S(1)}, u32[]{:S(2)}, u32[]{:S(2)}) collective-permute-start(bf16[256,128]{1,0:T(8,128)(2,1)S(1)} %get-tuple-element.61), channel_id=1, source_target_pairs={{0,8},{1,5},{2,10},{3,15},{4,12},{5,1},{6,14},{7,11},{8,0},{9,13},... | collective-permute-start | bytes 196616 | tf_op jit(solution)/shard_map/ppermute | solution.py:380
  73.2 2.0 %collective-permute-start.9 = (bf16[256,128]{1,0:T(8,128)(2,1)S(1)}, bf16[256,128]{1,0:T(8,128)(2,1)S(1)}, u32[]{:S(2)}, u32[]{:S(2)}) collective-permute-start(bf16[256,128]{1,0:T(8,128)(2,1)S(1)} %get-tuple-element.62), channel_id=1, source_target_pairs={{0,12},{1,9},{2,6},{3,11},{4,8},{5,13},{6,2},{7,15},{8,4},{9,1},{1... | collective-permute-start | bytes 196616 | tf_op jit(solution)/shard_map/ppermute | solution.py:380
  75.2 0.3 collective-permute-done.10.d_ref
  75.5 0.5 collective-permute-done.8.b_ref
  76.0 4.7 %collective-permute-done.9.c_ref = bf16[256,128]{1,0:T(8,128)(2,1)S(1)} collective-permute-done((bf16[256,128]{1,0:T(8,128)(2,1)S(1)}, bf16[256,128]{1,0:T(8,128)(2,1)S(1)}, u32[]{:S(2)}, u32[]{:S(2)}) %collective-permute-start.9) | collective-permute-done | bytes 65568 | tf_op jit(solution)/shard_map/ppermute | solution.py:380
  80.7 0.0 all-to-all-done.2.in_ref
  80.7 5.9 %collective-permute-start.11 = (bf16[16,2,16,1280]{3,2,1,0:T(8,128)(2,1)S(1)}, bf16[16,2,16,1280]{3,2,1,0:T(8,128)(2,1)S(1)}, u32[]{:S(2)}, u32[]{:S(2)}) collective-permute-start(bf16[16,2,16,1280]{3,2,1,0:T(8,128)(2,1)S(1)} %all-to-all-done.2.in_ref), channel_id=1, source_target_pairs={{0,1},{1,0},{2,3},{3,2},{4,5},{5,4},{6,7},{7,6},{8,9},{9,8},{10,11... | collective-permute-start | bytes 3932168 | tf_op jit(solution)/shard_map/ppermute | solution.py:369
  86.5 1.2 %shard_map.107 = (bf16[512,2048]{1,0:T(8,128)(2,1)}, f32[2048,128]{1,0:T(8,128)}) custom-call(s32[1]{0:T(128)} %bitcast.core_ref, bf16[16,2,16,1280]{3,2,1,0:T(8,128)(2,1)S(1)} %all-to-all-done.2.in_ref), custom_call_target="tpu_custom_call" | custom-call | bytes 4194304 | tf_op jit(solution)/shard_map/pallas_call | solution.py:338
  87.8 0.0 copy-done
  87.8 0.7 shard_map.109
  88.5 0.7 collective-permute-done.11.in_ref
  89.2 1.2 %shard_map.108 = (bf16[512,2048]{1,0:T(8,128)(2,1)}, f32[2048,128]{1,0:T(8,128)}) custom-call(s32[1]{0:T(128)S(6)} %sub.10.core_ref, bf16[16,2,16,1280]{3,2,1,0:T(8,128)(2,1)S(1)} %collective-permute-done.11.in_ref, bf16[512,2048]{1,0:T(8,128)(2,1)} %get-tuple-element.65.refs_0_, ...), custom_call_target="tpu_custom_call", output_to_operand_aliasing={{0}: (2, {}), {1}: (3, {})} | custom-call | bytes 4194304 | tf_op jit(solution)/shard_map/pallas_call | solution.py:338
  (1 shorter events, 0.0 us)
Async XLA Ops:
  5.7 5.6 %collective-permute-start.1 = (bf16[16,2,16,1024]{3,2,1,0:T(8,128)(2,1)S(1)}, bf16[16,2,16,1024]{3,2,1,0:T(8,128)(2,1)S(1)}, u32[]{:S(2)}, u32[]{:S(2)}) collective-permute-start(bf16[16,2,16,1024]{3,2,1,0:T(8,128)(2,1)S(1)} %get-tuple-element.44), channel_id=1, source_target_pairs={{0,1},{1,0},{2,3},{3,2},{4,5},{5,4},{6,7},{7,6},{8,9},{9,8},{10,11... | collective-permute-start | bytes 3145736 | tf_op jit(solution)/shard_map/ppermute | solution.py:369
  11.0 1.6 %collective-permute-start = (bf16[16,2,16,256]{3,2,1,0:T(8,128)(2,1)S(1)}, bf16[16,2,16,256]{3,2,1,0:T(8,128)(2,1)S(1)}, u32[]{:S(2)}, u32[]{:S(2)}) collective-permute-start(bf16[16,2,16,256]{3,2,1,0:T(8,128)(2,1)S(1)} %get-tuple-element.42), channel_id=1, source_target_pairs={{0,1},{1,0},{2,3},{3,2},{4,5},{5,4},{6,7},{7,6},{8,9},{9,8},{10,11... | collective-permute-start | bytes 786440 | tf_op jit(solution)/shard_map/ppermute | solution.py:369
  13.4 6.7 %copy-start.1 = (s32[512,4]{0,1:T(4,128)S(1)}, s32[512,4]{0,1:T(4,128)}, u32[]{:S(2)}) copy-start(s32[512,4]{0,1:T(4,128)} %param.8) | copy-start | bytes 24580
  13.4 27.8 %all-to-all-start = ((bf16[32,16,1280]{2,1,0:T(8,128)(2,1)}), bf16[32,16,1280]{2,1,0:T(8,128)(2,1)S(1)}, u32[]{:S(2)}, u32[]{:S(2)}) async-start(bf16[32,16,1280]{2,1,0:T(8,128)(2,1)} %bitcast.19), calls=%async_computation | async-start | bytes 2621440 | tf_op jit(solution)/shard_map/all_to_all | solution.py:372
  24.0 1.7 %collective-permute-start.5 = (bf16[1040,128]{1,0:T(8,128)(2,1)S(1)}, bf16[1040,128]{1,0:T(8,128)(2,1)S(1)}, u32[]{:S(2)}, u32[]{:S(2)}) collective-permute-start(bf16[1040,128]{1,0:T(8,128)(2,1)S(1)} %get-tuple-element.47), channel_id=1, source_target_pairs={{0,1},{1,0},{2,3},{3,2},{4,5},{5,4},{6,7},{7,6},{8,9},{9,8},{10,11... | collective-permute-start | bytes 798728 | tf_op jit(solution)/shard_map/ppermute | solution.py:369
  26.4 12.3 %collective-permute-start.6 = (bf16[17,4,16,128]{3,2,1,0:T(8,128)(2,1)S(1)}, bf16[17,4,16,128]{3,2,1,0:T(8,128)(2,1)S(1)}, u32[]{:S(2)}, u32[]{:S(2)}) collective-permute-start(bf16[17,4,16,128]{3,2,1,0:T(8,128)(2,1)S(1)} %get-tuple-element.49), channel_id=1, source_target_pairs={{0,14},{1,15},{2,4},{3,5},{4,2},{5,3},{6,8},{7,9},{8,6},{9,7},{10,... | collective-permute-start | bytes 835592 | tf_op jit(solution)/shard_map/ppermute | solution.py:380
  41.2 16.6 %all-to-all-start.1 = ((bf16[16,9,16,128]{3,2,1,0:T(8,128)(2,1)}), bf16[16,9,16,128]{3,2,1,0:T(8,128)(2,1)S(1)}, u32[]{:S(2)}, u32[]{:S(2)}) async-start(bf16[16,9,16,128]{3,2,1,0:T(8,128)(2,1)} %shard_map.101), calls=%async_computation.1 | async-start | bytes 1179648 | tf_op jit(solution)/shard_map/all_to_all | solution.py:372
  47.0 12.4 %collective-permute-start.2 = (bf16[16,1280]{1,0:T(8,128)(2,1)S(1)}, bf16[16,1280]{1,0:T(8,128)(2,1)S(1)}, u32[]{:S(2)}, u32[]{:S(2)}) collective-permute-start(bf16[16,1280]{1,0:T(8,128)(2,1)S(1)} %shard_map.98.a_ref), channel_id=1, source_target_pairs={{0,8},{1,9},{2,10},{3,11},{4,12},{5,13},{6,14},{7,15},{8,0},{9,1},... | collective-permute-start | bytes 122888 | tf_op jit(solution)/shard_map/ppermute | solution.py:369
  51.3 8.2 %collective-permute-start.3 = (bf16[16,1280]{1,0:T(8,128)(2,1)S(1)}, bf16[16,1280]{1,0:T(8,128)(2,1)S(1)}, u32[]{:S(2)}, u32[]{:S(2)}) collective-permute-start(bf16[16,1280]{1,0:T(8,128)(2,1)S(1)} %shard_map.98.a_ref), channel_id=1, source_target_pairs={{0,4},{1,13},{2,6},{3,15},{4,0},{5,9},{6,2},{7,11},{8,12},{9,5},{1... | collective-permute-start | bytes 122888 | tf_op jit(solution)/shard_map/ppermute | solution.py:369
  51.5 7.9 %collective-permute-start.4 = (bf16[16,1280]{1,0:T(8,128)(2,1)S(1)}, bf16[16,1280]{1,0:T(8,128)(2,1)S(1)}, u32[]{:S(2)}, u32[]{:S(2)}) collective-permute-start(bf16[16,1280]{1,0:T(8,128)(2,1)S(1)} %shard_map.98.a_ref), channel_id=1, source_target_pairs={{0,12},{1,5},{2,14},{3,7},{4,8},{5,1},{6,10},{7,3},{8,4},{9,13},{1... | collective-permute-start | bytes 122888 | tf_op jit(solution)/shard_map/ppermute | solution.py:369
  59.5 2.9 %collective-permute-start.7 = (bf16[16,1280]{1,0:T(8,128)(2,1)S(1)}, bf16[16,1280]{1,0:T(8,128)(2,1)S(1)}, u32[]{:S(2)}, u32[]{:S(2)}) collective-permute-start(bf16[16,1280]{1,0:T(8,128)(2,1)S(1)} %shard_map.104.in_ref), channel_id=1, source_target_pairs={{0,2},{1,3},{2,0},{3,1},{4,6},{5,7},{6,4},{7,5},{8,10},{9,11},{10,... | collective-permute-start | bytes 122888 | tf_op jit(solution)/shard_map/ppermute | solution.py:369
  63.3 17.4 %all-to-all-start.2 = ((bf16[16,2,16,1280]{3,2,1,0:T(8,128)(2,1)}), bf16[16,2,16,1280]{3,2,1,0:T(8,128)(2,1)S(1)}, u32[]{:S(2)}, u32[]{:S(2)}) async-start(bf16[16,2,16,1280]{3,2,1,0:T(8,128)(2,1)} %shard_map.106), calls=%async_computation.2 | async-start | bytes 2621440 | tf_op jit(solution)/shard_map/all_to_all | solution.py:372
  69.5 18.3 %copy-start = (f32[4,64,128]{2,1,0:T(8,128)S(1)}, f32[4,64,128]{2,1,0:T(8,128)}, u32[]{:S(2)}) copy-start(f32[4,64,128]{2,1,0:T(8,128)} %param.13) | copy-start | bytes 393220
  69.5 6.0 %collective-permute-start.10 = (bf16[256,128]{1,0:T(8,128)(2,1)S(1)}, bf16[256,128]{1,0:T(8,128)(2,1)S(1)}, u32[]{:S(2)}, u32[]{:S(2)}) collective-permute-start(bf16[256,128]{1,0:T(8,128)(2,1)S(1)} %get-tuple-element.63), channel_id=1, source_target_pairs={{0,4},{1,13},{2,14},{3,7},{4,0},{5,9},{6,10},{7,3},{8,12},{9,5},{1... | collective-permute-start | bytes 196616 | tf_op jit(solution)/shard_map/ppermute | solution.py:380
  72.0 4.0 %collective-permute-start.8 = (bf16[256,128]{1,0:T(8,128)(2,1)S(1)}, bf16[256,128]{1,0:T(8,128)(2,1)S(1)}, u32[]{:S(2)}, u32[]{:S(2)}) collective-permute-start(bf16[256,128]{1,0:T(8,128)(2,1)S(1)} %get-tuple-element.61), channel_id=1, source_target_pairs={{0,8},{1,5},{2,10},{3,15},{4,12},{5,1},{6,14},{7,11},{8,0},{9,13},... | collective-permute-start | bytes 196616 | tf_op jit(solution)/shard_map/ppermute | solution.py:380
  73.2 7.5 %collective-permute-start.9 = (bf16[256,128]{1,0:T(8,128)(2,1)S(1)}, bf16[256,128]{1,0:T(8,128)(2,1)S(1)}, u32[]{:S(2)}, u32[]{:S(2)}) collective-permute-start(bf16[256,128]{1,0:T(8,128)(2,1)S(1)} %get-tuple-element.62), channel_id=1, source_target_pairs={{0,12},{1,9},{2,6},{3,11},{4,8},{5,13},{6,2},{7,15},{8,4},{9,1},{1... | collective-permute-start | bytes 196616 | tf_op jit(solution)/shard_map/ppermute | solution.py:380
  80.7 8.5 %collective-permute-start.11 = (bf16[16,2,16,1280]{3,2,1,0:T(8,128)(2,1)S(1)}, bf16[16,2,16,1280]{3,2,1,0:T(8,128)(2,1)S(1)}, u32[]{:S(2)}, u32[]{:S(2)}) collective-permute-start(bf16[16,2,16,1280]{3,2,1,0:T(8,128)(2,1)S(1)} %all-to-all-done.2.in_ref), channel_id=1, source_target_pairs={{0,1},{1,0},{2,3},{3,2},{4,5},{5,4},{6,7},{7,6},{8,9},{9,8},{10,11... | collective-permute-start | bytes 3932168 | tf_op jit(solution)/shard_map/ppermute | solution.py:369

commit v7 on v6

--- a/solution.py
+++ b/solution.py
@@ -327,7 +327,7 @@
     for n in range(NODES):
         rows = slice(n * CHUNK, (n + 1) * CHUNK)
         for part in range(ZP):
-            piece = in_ref[NODES - 1 - n, part]
+            piece = in_ref[n, part]
             w1_ref[rows, part * PCOL:(part + 1) * PCOL] = piece[:, :PCOL]
             for b in range(2):
                 at = (2 * part + b) * HALF + n * CHUNK
@@ -380,7 +380,7 @@
         return lax.ppermute(array, "all", [(i, partner(i)) for i in range(OWNERS)])
 
     with_pair = [
-        [n * LOCALS + q * 4 + p * 2 + c for n in range(NODES) for p in range(ZP)] for q in range(ZQ) for c in range(2)
+        [n * LOCALS + q * 4 + p * 2 + c for n in reversed(range(NODES)) for p in reversed(range(ZP))] for q in range(ZQ) for c in range(2)
     ]
     by_node = [[n * LOCALS + low for n in range(NODES)] for low in range(LOCALS)]
     alone = [
@@ -451,7 +451,7 @@
         scalars=1,
         size=2 * MIB,
     )
-    block = ((core * ZP + zp) * 2 * HALF + node * CHUNK) // CHUNK
+    block = ((core * ZP + 1 - zp) * 2 * HALF + (NODES - 1 - node) * CHUNK) // CHUNK
     accum = pick(jnp.stack([block, block + HALF // CHUNK]), in_hbm(hot_accum.reshape(TABLES * HOT, E)))
     slab, accum = lax.optimization_barrier((slab, accum))
     part = call(group_sum_kernel, shape(CHUNK, WIDE), (parts,), size=2 * MIB)
@@ -468,8 +468,8 @@
     quad, cold = lax.optimization_barrier((quad, cold))
     done = call(step_kernel, pltpu.VMEM((CHUNK, WIDE), BF), (*quad, accum))
     beside = flip(done, 2)
-    whole = spread(zp.reshape(1), done)
-    whole = spread(1 - zp.reshape(1), beside, (whole,))
+    whole = spread(1 - zp.reshape(1), done)
+    whole = spread(zp.reshape(1), beside, (whole,))
     half = exchange(whole, alone)
     cold = [cold[0]] + [
         turned_flip(cold[k], 2 * COLD_ORDER[0][k], 2 * COLD_ORDER[1][k]) for k in range(1, ZQ)

time: 90.9 us -> 89.4 us (0.983)
  waiting for transfers between devices: 20.5 us -> 18.6 us
    ppermute x4, starting transfers between devices: 11.3 us -> 10.3 us  [turned_flip(): return lax.ppermute(array, 'all', [(i, partner(i)) for i in range(OWNERS)])]
    ppermute x4, waiting for transfers between devices: 10.1 us -> 9.18 us  [turned_flip(): return lax.ppermute(array, 'all', [(i, partner(i)) for i in range(OWNERS)])]
  transfers between devices with their start and end apart: 15 -> 15, of which waited for: 11 -> 10; matrix products, arithmetic and copies ran while one was open for 1% -> 1% of each run, Pallas kernels for 17% -> 17%
where the time goes in v7:
time: 89.4 us; the launch traced here: 88.9 us
  starting transfers between devices  45.8 us (51%)
  Pallas kernels  23 us (26%)
  waiting for transfers between devices  18.6 us (21%)
    all_to_all x3, starting transfers between devices, exchange(): lax.all_to_all(array, 'all', 0, 0, axis_index_groups=groups, tiled=True)  19.1 us
    ppermute x8, starting transfers between devices, flip(): lax.ppermute(array, 'all', [(i, i ^ masks[i & 1]) for i in range(OWNERS)])  16.4 us
    pallas_call x9, Pallas kernels, call(): pl.pallas_call(kernel, out_shape=out_shape, in_specs=[SMEM] * scalars + [...  15.7 us
    ppermute x4, starting transfers between devices, turned_flip(): return lax.ppermute(array, 'all', [(i, partner(i)) for i in range(OWNERS)])  10.3 us
    ppermute x4, waiting for transfers between devices, turned_flip(): return lax.ppermute(array, 'all', [(i, partner(i)) for i in range(OWNERS)])  9.18 us
    all_to_all x3, waiting for transfers between devices, exchange(): lax.all_to_all(array, 'all', 0, 0, axis_index_groups=groups, tiled=True)  5.78 us
    ppermute x8, waiting for transfers between devices, flip(): lax.ppermute(array, 'all', [(i, i ^ masks[i & 1]) for i in range(OWNERS)])  3.63 us
    pallas_call x2, Pallas kernels, finish(): pl.pallas_call(finish_kernel, out_shape=(shape(FEAT, HID), shape(TABLES *...  2.48 us
  transfers between devices with their start and end apart: 15, of which 10 were waited for; matrix products, arithmetic and copies ran while one was open for 1% of the time, Pallas kernels for 17%

profile of v7, /device:TPU:1, one launch (start us, length us, event | category | flops | bytes accessed | tf_op | source)
XLA Modules:
  0.0 88.9 jit_solution(12633764167938014858)
XLA Ops:
  0.6 5.1 %shard_map.94 = (bf16[16,2,16,1024]{3,2,1,0:T(8,128)(2,1)S(1)}, bf16[16,2,16,1024]{3,2,1,0:T(8,128)(2,1)S(1)}, bf16[512,2048]{1,0:T(8,128)(2,1)S(1)}, bf16[512,2...) custom-call(s32[1]{0:T(128)} %bitcast.core_ref, bf16[512,512]{1,0:T(8,128)(2,1)} %x_hbm.1, s32[4,512]{1,0:T(4,128)} %bitcast.17, ...), custom_call_target="tpu_custom_call" | custom-call | flops 3000000000 | bytes 8388608 | tf_op jit(solution)/shard_map/pallas_call | solution.py:55
  5.7 3.3 %collective-permute-start.1 = (bf16[16,2,16,1024]{3,2,1,0:T(8,128)(2,1)S(1)}, bf16[16,2,16,1024]{3,2,1,0:T(8,128)(2,1)S(1)}, u32[]{:S(2)}, u32[]{:S(2)}) collective-permute-start(bf16[16,2,16,1024]{3,2,1,0:T(8,128)(2,1)S(1)} %get-tuple-element.44), channel_id=1, source_target_pairs={{0,1},{1,0},{2,3},{3,2},{4,5},{5,4},{6,7},{7,6},{8,9},{9,8},{10,11... | collective-permute-start | bytes 3145736 | tf_op jit(solution)/shard_map/ppermute | solution.py:369
  9.0 2.0 %shard_map.95 = (bf16[16,2,16,256]{3,2,1,0:T(8,128)(2,1)S(1)}, bf16[16,2,16,256]{3,2,1,0:T(8,128)(2,1)S(1)}, bf16[512,512]{1,0:T(8,128)(2,1)S(1)}) custom-call(s32[1]{0:T(128)} %bitcast.core_ref, bf16[512,2048]{1,0:T(8,128)(2,1)S(1)} %get-tuple-element.38.pre_ref, bf16[512,2048]{1,0:T(8,128)(2,1)S(1)} %get-tuple-element.39.wh_ref, ...), custom_call_target="tpu_custom_call" | custom-call | flops 2000000000 | bytes 6291456 | tf_op jit(solution)/shard_map/pallas_call | solution.py:55
  11.0 0.1 collective-permute-start
  11.1 0.2 collective-permute-done.1.b_ref
  11.3 1.0 %shard_map.96.refs_0_ = bf16[16,2,16,1280]{3,2,1,0:T(8,128)(2,1)} custom-call(bf16[16,2,16,1024]{3,2,1,0:T(8,128)(2,1)S(1)} %get-tuple-element.43.a_ref, bf16[16,2,16,1024]{3,2,1,0:T(8,128)(2,1)S(1)} %collective-permute-done.1.b_ref), custom_call_target="tpu_custom_call" | custom-call | bytes 2097152 | tf_op jit(solution)/shard_map/pallas_call | solution.py:192
  12.4 0.3 collective-permute-done.b_ref
  12.7 0.7 shard_map.97
  13.4 0.0 copy-start.1
  13.4 8.4 %all-to-all-start = ((bf16[32,16,1280]{2,1,0:T(8,128)(2,1)}), bf16[32,16,1280]{2,1,0:T(8,128)(2,1)S(1)}, u32[]{:S(2)}, u32[]{:S(2)}) async-start(bf16[32,16,1280]{2,1,0:T(8,128)(2,1)} %bitcast.19), calls=%async_computation | async-start | bytes 2621440 | tf_op jit(solution)/shard_map/all_to_all | solution.py:372
  21.8 0.0 copy-done.1
  21.8 3.9 %shard_map.99 = (bf16[1040,128]{1,0:T(8,128)(2,1)S(1)}, bf16[1040,128]{1,0:T(8,128)(2,1)S(1)}) custom-call(s32[1]{0:T(128)} %bitcast.core_ref, s32[4,512]{1,0:T(4,128)S(1)} %bitcast.18, bf16[512,512]{1,0:T(8,128)(2,1)S(1)} %get-tuple-element.45.grad_ref), custom_call_target="tpu_custom_call" | custom-call | flops 6000000000 | bytes 8388608 | tf_op jit(solution)/shard_map/pallas_call | solution.py:55
  25.7 0.5 collective-permute-start.5
  26.2 0.1 stack.29.place_ref
  26.3 1.1 %collective-permute-done.5.far_cold_ref = bf16[1040,128]{1,0:T(8,128)(2,1)S(1)} collective-permute-done((bf16[1040,128]{1,0:T(8,128)(2,1)S(1)}, bf16[1040,128]{1,0:T(8,128)(2,1)S(1)}, u32[]{:S(2)}, u32[]{:S(2)}) %collective-permute-start.5) | collective-permute-done | bytes 266272 | tf_op jit(solution)/shard_map/ppermute | solution.py:369
  27.4 0.8 shard_map.100
  28.1 4.5 %collective-permute-start.6 = (bf16[17,4,16,128]{3,2,1,0:T(8,128)(2,1)S(1)}, bf16[17,4,16,128]{3,2,1,0:T(8,128)(2,1)S(1)}, u32[]{:S(2)}, u32[]{:S(2)}) collective-permute-start(bf16[17,4,16,128]{3,2,1,0:T(8,128)(2,1)S(1)} %get-tuple-element.49), channel_id=1, source_target_pairs={{0,14},{1,15},{2,4},{3,5},{4,2},{5,3},{6,8},{7,9},{8,6},{9,7},{10,... | collective-permute-start | bytes 835592 | tf_op jit(solution)/shard_map/ppermute | solution.py:380
  32.7 0.7 pad_add_fusion.at_ref
  33.3 1.4 %shard_map.102.accum_ref = f32[16,256]{1,0:T(8,128)S(1)} custom-call(s32[2]{0:T(128)} %pad_add_fusion.at_ref, f32[2048,128]{1,0:T(8,128)} %bitcast.20, f32[2048,128]{1,0:T(8,128)} %bitcast.21), custom_call_target="tpu_custom_call" | custom-call | tf_op jit(solution)/shard_map/pallas_call | solution.py:245
  34.7 4.7 %collective-permute-done.6.far_ref = bf16[17,4,16,128]{3,2,1,0:T(8,128)(2,1)S(1)} collective-permute-done((bf16[17,4,16,128]{3,2,1,0:T(8,128)(2,1)S(1)}, bf16[17,4,16,128]{3,2,1,0:T(8,128)(2,1)S(1)}, u32[]{:S(2)}, u32[]{:S(2)}) %collective-permute-start.6) | collective-permute-done | bytes 278560 | tf_op jit(solution)/shard_map/ppermute | solution.py:380
  39.4 1.4 %shard_map.101 = bf16[16,9,16,128]{3,2,1,0:T(8,128)(2,1)} custom-call(s32[5]{0:T(128)S(1)} %stack.29.place_ref, bf16[17,4,16,128]{3,2,1,0:T(8,128)(2,1)S(1)} %get-tuple-element.48.keep_ref, bf16[17,4,16,128]{3,2,1,0:T(8,128)(2,1)S(1)} %collective-permute-done.6.far_ref), custom_call_target="tpu_custom_call" | custom-call | bytes 2097152 | tf_op jit(solution)/shard_map/pallas_call | solution.py:55
  40.8 0.0 all-to-all-done.in_ref
  40.8 3.8 %all-to-all-start.1 = ((bf16[16,9,16,128]{3,2,1,0:T(8,128)(2,1)}), bf16[16,9,16,128]{3,2,1,0:T(8,128)(2,1)S(1)}, u32[]{:S(2)}, u32[]{:S(2)}) async-start(bf16[16,9,16,128]{3,2,1,0:T(8,128)(2,1)} %shard_map.101), calls=%async_computation.1 | async-start | bytes 1179648 | tf_op jit(solution)/shard_map/all_to_all | solution.py:372
  44.6 0.2 shard_map.98.a_ref
  44.8 4.2 %collective-permute-start.2 = (bf16[16,1280]{1,0:T(8,128)(2,1)S(1)}, bf16[16,1280]{1,0:T(8,128)(2,1)S(1)}, u32[]{:S(2)}, u32[]{:S(2)}) collective-permute-start(bf16[16,1280]{1,0:T(8,128)(2,1)S(1)} %shard_map.98.a_ref), channel_id=1, source_target_pairs={{0,8},{1,9},{2,10},{3,11},{4,12},{5,13},{6,14},{7,15},{8,0},{9,1},... | collective-permute-start | bytes 122888 | tf_op jit(solution)/shard_map/ppermute | solution.py:369
  49.0 0.5 collective-permute-start.3
  49.6 1.0 %collective-permute-start.4 = (bf16[16,1280]{1,0:T(8,128)(2,1)S(1)}, bf16[16,1280]{1,0:T(8,128)(2,1)S(1)}, u32[]{:S(2)}, u32[]{:S(2)}) collective-permute-start(bf16[16,1280]{1,0:T(8,128)(2,1)S(1)} %shard_map.98.a_ref), channel_id=1, source_target_pairs={{0,12},{1,5},{2,14},{3,7},{4,8},{5,1},{6,10},{7,3},{8,4},{9,13},{1... | collective-permute-start | bytes 122888 | tf_op jit(solution)/shard_map/ppermute | solution.py:369
  50.5 5.0 %all-to-all-done.1.in_ref = bf16[16,9,16,128]{3,2,1,0:T(8,128)(2,1)S(1)} async-done(((bf16[16,9,16,128]{3,2,1,0:T(8,128)(2,1)}), bf16[16,9,16,128]{3,2,1,0:T(8,128)(2,1)S(1)}, u32[]{:S(2)}, u32[]{:S(2)}) %all-to-all-start.1) | async-done | bytes 589856 | tf_op jit(solution)/shard_map/all_to_all | solution.py:372
  55.5 1.6 %shard_map.103 = (bf16[256,128]{1,0:T(8,128)(2,1)S(1)}, bf16[256,128]{1,0:T(8,128)(2,1)S(1)}, bf16[256,128]{1,0:T(8,128)(2,1)S(1)}, bf16[256,128]{1,0:T(8,128)(2,1)S(1)}) custom-call(s32[5]{0:T(128)S(1)} %stack.29.place_ref, bf16[16,9,16,128]{3,2,1,0:T(8,128)(2,1)S(1)} %all-to-all-done.1.in_ref), custom_call_target="tpu_custom_call" | custom-call | flops 1000000000 | bytes 2097152 | tf_op jit(solution)/shard_map/pallas_call | solution.py:55
  57.1 0.0 collective-permute-done.2.b_ref
  57.1 0.0 collective-permute-done.3.c_ref
  57.1 0.0 collective-permute-done.4.d_ref
  57.2 0.7 collective-permute-start.7
  57.9 0.9 shard_map.105.refs_0_
  58.8 1.4 %collective-permute-done.7.in_ref = bf16[16,1280]{1,0:T(8,128)(2,1)S(1)} collective-permute-done((bf16[16,1280]{1,0:T(8,128)(2,1)S(1)}, bf16[16,1280]{1,0:T(8,128)(2,1)S(1)}, u32[]{:S(2)}, u32[]{:S(2)}) %collective-permute-start.7) | collective-permute-done | bytes 40992 | tf_op jit(solution)/shard_map/ppermute | solution.py:369
  60.1 0.9 shard_map.106
  61.0 7.0 %all-to-all-start.2 = ((bf16[16,2,16,1280]{3,2,1,0:T(8,128)(2,1)}), bf16[16,2,16,1280]{3,2,1,0:T(8,128)(2,1)S(1)}, u32[]{:S(2)}, u32[]{:S(2)}) async-start(bf16[16,2,16,1280]{3,2,1,0:T(8,128)(2,1)} %shard_map.106), calls=%async_computation.2 | async-start | bytes 2621440 | tf_op jit(solution)/shard_map/all_to_all | solution.py:372
  68.0 0.0 copy-start
  68.0 2.2 %collective-permute-start.10 = (bf16[256,128]{1,0:T(8,128)(2,1)S(1)}, bf16[256,128]{1,0:T(8,128)(2,1)S(1)}, u32[]{:S(2)}, u32[]{:S(2)}) collective-permute-start(bf16[256,128]{1,0:T(8,128)(2,1)S(1)} %get-tuple-element.63), channel_id=1, source_target_pairs={{0,4},{1,13},{2,14},{3,7},{4,0},{5,9},{6,10},{7,3},{8,12},{9,5},{1... | collective-permute-start | bytes 196616 | tf_op jit(solution)/shard_map/ppermute | solution.py:380
  70.2 0.9 collective-permute-start.8
  71.1 2.6 %collective-permute-start.9 = (bf16[256,128]{1,0:T(8,128)(2,1)S(1)}, bf16[256,128]{1,0:T(8,128)(2,1)S(1)}, u32[]{:S(2)}, u32[]{:S(2)}) collective-permute-start(bf16[256,128]{1,0:T(8,128)(2,1)S(1)} %get-tuple-element.62), channel_id=1, source_target_pairs={{0,12},{1,9},{2,6},{3,11},{4,8},{5,13},{6,2},{7,15},{8,4},{9,1},{1... | collective-permute-start | bytes 196616 | tf_op jit(solution)/shard_map/ppermute | solution.py:380
  73.7 0.0 collective-permute-done.10.d_ref
  73.7 0.6 collective-permute-done.8.b_ref
  74.3 3.9 %collective-permute-done.9.c_ref = bf16[256,128]{1,0:T(8,128)(2,1)S(1)} collective-permute-done((bf16[256,128]{1,0:T(8,128)(2,1)S(1)}, bf16[256,128]{1,0:T(8,128)(2,1)S(1)}, u32[]{:S(2)}, u32[]{:S(2)}) %collective-permute-start.9) | collective-permute-done | bytes 65568 | tf_op jit(solution)/shard_map/ppermute | solution.py:380
  78.2 0.8 all-to-all-done.2.in_ref
  79.0 6.0 %collective-permute-start.11 = (bf16[16,2,16,1280]{3,2,1,0:T(8,128)(2,1)S(1)}, bf16[16,2,16,1280]{3,2,1,0:T(8,128)(2,1)S(1)}, u32[]{:S(2)}, u32[]{:S(2)}) collective-permute-start(bf16[16,2,16,1280]{3,2,1,0:T(8,128)(2,1)S(1)} %all-to-all-done.2.in_ref), channel_id=1, source_target_pairs={{0,1},{1,0},{2,3},{3,2},{4,5},{5,4},{6,7},{7,6},{8,9},{9,8},{10,11... | collective-permute-start | bytes 3932168 | tf_op jit(solution)/shard_map/ppermute | solution.py:369
  85.0 1.2 %shard_map.107 = (bf16[512,2048]{1,0:T(8,128)(2,1)}, f32[2048,128]{1,0:T(8,128)}) custom-call(s32[1]{0:T(128)} %bitcast.core_ref, bf16[16,2,16,1280]{3,2,1,0:T(8,128)(2,1)S(1)} %all-to-all-done.2.in_ref), custom_call_target="tpu_custom_call" | custom-call | bytes 4194304 | tf_op jit(solution)/shard_map/pallas_call | solution.py:338
  86.3 0.0 copy-done
  86.3 0.7 shard_map.109
  87.0 0.7 collective-permute-done.11.in_ref
  87.7 1.2 %shard_map.108 = (bf16[512,2048]{1,0:T(8,128)(2,1)}, f32[2048,128]{1,0:T(8,128)}) custom-call(s32[1]{0:T(128)S(6)} %sub.16.core_ref, bf16[16,2,16,1280]{3,2,1,0:T(8,128)(2,1)S(1)} %collective-permute-done.11.in_ref, bf16[512,2048]{1,0:T(8,128)(2,1)} %get-tuple-element.65.refs_0_, ...), custom_call_target="tpu_custom_call", output_to_operand_aliasing={{0}: (2, {}), {1}: (3, {})} | custom-call | bytes 4194304 | tf_op jit(solution)/shard_map/pallas_call | solution.py:338
  (1 shorter events, 0.0 us)
Async XLA Ops:
  5.7 5.6 %collective-permute-start.1 = (bf16[16,2,16,1024]{3,2,1,0:T(8,128)(2,1)S(1)}, bf16[16,2,16,1024]{3,2,1,0:T(8,128)(2,1)S(1)}, u32[]{:S(2)}, u32[]{:S(2)}) collective-permute-start(bf16[16,2,16,1024]{3,2,1,0:T(8,128)(2,1)S(1)} %get-tuple-element.44), channel_id=1, source_target_pairs={{0,1},{1,0},{2,3},{3,2},{4,5},{5,4},{6,7},{7,6},{8,9},{9,8},{10,11... | collective-permute-start | bytes 3145736 | tf_op jit(solution)/shard_map/ppermute | solution.py:369
  11.0 1.6 %collective-permute-start = (bf16[16,2,16,256]{3,2,1,0:T(8,128)(2,1)S(1)}, bf16[16,2,16,256]{3,2,1,0:T(8,128)(2,1)S(1)}, u32[]{:S(2)}, u32[]{:S(2)}) collective-permute-start(bf16[16,2,16,256]{3,2,1,0:T(8,128)(2,1)S(1)} %get-tuple-element.42), channel_id=1, source_target_pairs={{0,1},{1,0},{2,3},{3,2},{4,5},{5,4},{6,7},{7,6},{8,9},{9,8},{10,11... | collective-permute-start | bytes 786440 | tf_op jit(solution)/shard_map/ppermute | solution.py:369
  13.4 8.4 %copy-start.1 = (s32[512,4]{0,1:T(4,128)S(1)}, s32[512,4]{0,1:T(4,128)}, u32[]{:S(2)}) copy-start(s32[512,4]{0,1:T(4,128)} %param.8) | copy-start | bytes 24580
  13.4 27.4 %all-to-all-start = ((bf16[32,16,1280]{2,1,0:T(8,128)(2,1)}), bf16[32,16,1280]{2,1,0:T(8,128)(2,1)S(1)}, u32[]{:S(2)}, u32[]{:S(2)}) async-start(bf16[32,16,1280]{2,1,0:T(8,128)(2,1)} %bitcast.19), calls=%async_computation | async-start | bytes 2621440 | tf_op jit(solution)/shard_map/all_to_all | solution.py:372
  25.7 1.7 %collective-permute-start.5 = (bf16[1040,128]{1,0:T(8,128)(2,1)S(1)}, bf16[1040,128]{1,0:T(8,128)(2,1)S(1)}, u32[]{:S(2)}, u32[]{:S(2)}) collective-permute-start(bf16[1040,128]{1,0:T(8,128)(2,1)S(1)} %get-tuple-element.47), channel_id=1, source_target_pairs={{0,1},{1,0},{2,3},{3,2},{4,5},{5,4},{6,7},{7,6},{8,9},{9,8},{10,11... | collective-permute-start | bytes 798728 | tf_op jit(solution)/shard_map/ppermute | solution.py:369
  28.1 11.3 %collective-permute-start.6 = (bf16[17,4,16,128]{3,2,1,0:T(8,128)(2,1)S(1)}, bf16[17,4,16,128]{3,2,1,0:T(8,128)(2,1)S(1)}, u32[]{:S(2)}, u32[]{:S(2)}) collective-permute-start(bf16[17,4,16,128]{3,2,1,0:T(8,128)(2,1)S(1)} %get-tuple-element.49), channel_id=1, source_target_pairs={{0,14},{1,15},{2,4},{3,5},{4,2},{5,3},{6,8},{7,9},{8,6},{9,7},{10,... | collective-permute-start | bytes 835592 | tf_op jit(solution)/shard_map/ppermute | solution.py:380
  40.8 14.7 %all-to-all-start.1 = ((bf16[16,9,16,128]{3,2,1,0:T(8,128)(2,1)}), bf16[16,9,16,128]{3,2,1,0:T(8,128)(2,1)S(1)}, u32[]{:S(2)}, u32[]{:S(2)}) async-start(bf16[16,9,16,128]{3,2,1,0:T(8,128)(2,1)} %shard_map.101), calls=%async_computation.1 | async-start | bytes 1179648 | tf_op jit(solution)/shard_map/all_to_all | solution.py:372
  44.8 12.3 %collective-permute-start.2 = (bf16[16,1280]{1,0:T(8,128)(2,1)S(1)}, bf16[16,1280]{1,0:T(8,128)(2,1)S(1)}, u32[]{:S(2)}, u32[]{:S(2)}) collective-permute-start(bf16[16,1280]{1,0:T(8,128)(2,1)S(1)} %shard_map.98.a_ref), channel_id=1, source_target_pairs={{0,8},{1,9},{2,10},{3,11},{4,12},{5,13},{6,14},{7,15},{8,0},{9,1},... | collective-permute-start | bytes 122888 | tf_op jit(solution)/shard_map/ppermute | solution.py:369
  49.0 8.1 %collective-permute-start.3 = (bf16[16,1280]{1,0:T(8,128)(2,1)S(1)}, bf16[16,1280]{1,0:T(8,128)(2,1)S(1)}, u32[]{:S(2)}, u32[]{:S(2)}) collective-permute-start(bf16[16,1280]{1,0:T(8,128)(2,1)S(1)} %shard_map.98.a_ref), channel_id=1, source_target_pairs={{0,4},{1,13},{2,6},{3,15},{4,0},{5,9},{6,2},{7,11},{8,12},{9,5},{1... | collective-permute-start | bytes 122888 | tf_op jit(solution)/shard_map/ppermute | solution.py:369
  49.6 7.6 %collective-permute-start.4 = (bf16[16,1280]{1,0:T(8,128)(2,1)S(1)}, bf16[16,1280]{1,0:T(8,128)(2,1)S(1)}, u32[]{:S(2)}, u32[]{:S(2)}) collective-permute-start(bf16[16,1280]{1,0:T(8,128)(2,1)S(1)} %shard_map.98.a_ref), channel_id=1, source_target_pairs={{0,12},{1,5},{2,14},{3,7},{4,8},{5,1},{6,10},{7,3},{8,4},{9,13},{1... | collective-permute-start | bytes 122888 | tf_op jit(solution)/shard_map/ppermute | solution.py:369
  57.2 2.9 %collective-permute-start.7 = (bf16[16,1280]{1,0:T(8,128)(2,1)S(1)}, bf16[16,1280]{1,0:T(8,128)(2,1)S(1)}, u32[]{:S(2)}, u32[]{:S(2)}) collective-permute-start(bf16[16,1280]{1,0:T(8,128)(2,1)S(1)} %shard_map.104.in_ref), channel_id=1, source_target_pairs={{0,2},{1,3},{2,0},{3,1},{4,6},{5,7},{6,4},{7,5},{8,10},{9,11},{10,... | collective-permute-start | bytes 122888 | tf_op jit(solution)/shard_map/ppermute | solution.py:369
  61.0 18.0 %all-to-all-start.2 = ((bf16[16,2,16,1280]{3,2,1,0:T(8,128)(2,1)}), bf16[16,2,16,1280]{3,2,1,0:T(8,128)(2,1)S(1)}, u32[]{:S(2)}, u32[]{:S(2)}) async-start(bf16[16,2,16,1280]{3,2,1,0:T(8,128)(2,1)} %shard_map.106), calls=%async_computation.2 | async-start | bytes 2621440 | tf_op jit(solution)/shard_map/all_to_all | solution.py:372
  68.0 18.3 %copy-start = (f32[4,64,128]{2,1,0:T(8,128)S(1)}, f32[4,64,128]{2,1,0:T(8,128)}, u32[]{:S(2)}) copy-start(f32[4,64,128]{2,1,0:T(8,128)} %param.13) | copy-start | bytes 393220
  68.0 5.7 %collective-permute-start.10 = (bf16[256,128]{1,0:T(8,128)(2,1)S(1)}, bf16[256,128]{1,0:T(8,128)(2,1)S(1)}, u32[]{:S(2)}, u32[]{:S(2)}) collective-permute-start(bf16[256,128]{1,0:T(8,128)(2,1)S(1)} %get-tuple-element.63), channel_id=1, source_target_pairs={{0,4},{1,13},{2,14},{3,7},{4,0},{5,9},{6,10},{7,3},{8,12},{9,5},{1... | collective-permute-start | bytes 196616 | tf_op jit(solution)/shard_map/ppermute | solution.py:380
  70.2 4.1 %collective-permute-start.8 = (bf16[256,128]{1,0:T(8,128)(2,1)S(1)}, bf16[256,128]{1,0:T(8,128)(2,1)S(1)}, u32[]{:S(2)}, u32[]{:S(2)}) collective-permute-start(bf16[256,128]{1,0:T(8,128)(2,1)S(1)} %get-tuple-element.61), channel_id=1, source_target_pairs={{0,8},{1,5},{2,10},{3,15},{4,12},{5,1},{6,14},{7,11},{8,0},{9,13},... | collective-permute-start | bytes 196616 | tf_op jit(solution)/shard_map/ppermute | solution.py:380
  71.1 7.1 %collective-permute-start.9 = (bf16[256,128]{1,0:T(8,128)(2,1)S(1)}, bf16[256,128]{1,0:T(8,128)(2,1)S(1)}, u32[]{:S(2)}, u32[]{:S(2)}) collective-permute-start(bf16[256,128]{1,0:T(8,128)(2,1)S(1)} %get-tuple-element.62), channel_id=1, source_target_pairs={{0,12},{1,9},{2,6},{3,11},{4,8},{5,13},{6,2},{7,15},{8,4},{9,1},{1... | collective-permute-start | bytes 196616 | tf_op jit(solution)/shard_map/ppermute | solution.py:380
  79.0 8.7 %collective-permute-start.11 = (bf16[16,2,16,1280]{3,2,1,0:T(8,128)(2,1)S(1)}, bf16[16,2,16,1280]{3,2,1,0:T(8,128)(2,1)S(1)}, u32[]{:S(2)}, u32[]{:S(2)}) collective-permute-start(bf16[16,2,16,1280]{3,2,1,0:T(8,128)(2,1)S(1)} %all-to-all-done.2.in_ref), channel_id=1, source_target_pairs={{0,1},{1,0},{2,3},{3,2},{4,5},{5,4},{6,7},{7,6},{8,9},{9,8},{10,11... | collective-permute-start | bytes 3932168 | tf_op jit(solution)/shard_map/ppermute | solution.py:369

commit v8 on v7

--- a/solution.py
+++ b/solution.py
@@ -456,7 +456,7 @@
     slab, accum = lax.optimization_barrier((slab, accum))
     part = call(group_sum_kernel, shape(CHUNK, WIDE), (parts,), size=2 * MIB)
     slab = exchange(slab, by_node)
-    quad = [part] + [flip(part, 4 * d, 4 * e) for d, e in zip((2, 1, 3), (2, 3, 1))]
+    quad = [part] + [flip(part, 4 * d, 4 * e) for d, e in zip((2, 1, 3), (3, 2, 1))]
     cold = call(
         cold_dense_kernel,
         tuple(shape(TABLES * COLD_DEV, E) for _ in range(ZQ)),

time: 89.4 us -> 89.8 us (level)
  transfers between devices with their start and end apart: 15 -> 15, of which waited for: 10 -> 11; matrix products, arithmetic and copies ran while one was open for 1% -> 1% of each run, Pallas kernels for 17% -> 17%
where the time goes in v8:
time: 89.8 us; the launch traced here: 89.3 us
  starting transfers between devices  45.9 us (51%)
  Pallas kernels  23 us (26%)
  waiting for transfers between devices  18.9 us (21%)
    all_to_all x3, starting transfers between devices, exchange(): lax.all_to_all(array, 'all', 0, 0, axis_index_groups=groups, tiled=True)  19.4 us
    ppermute x8, starting transfers between devices, flip(): lax.ppermute(array, 'all', [(i, i ^ masks[i & 1]) for i in range(OWNERS)])  16.2 us
    pallas_call x9, Pallas kernels, call(): pl.pallas_call(kernel, out_shape=out_shape, in_specs=[SMEM] * scalars + [...  15.7 us
    ppermute x4, starting transfers between devices, turned_flip(): return lax.ppermute(array, 'all', [(i, partner(i)) for i in range(OWNERS)])  10.3 us
    ppermute x4, waiting for transfers between devices, turned_flip(): return lax.ppermute(array, 'all', [(i, partner(i)) for i in range(OWNERS)])  9.38 us
    all_to_all x3, waiting for transfers between devices, exchange(): lax.all_to_all(array, 'all', 0, 0, axis_index_groups=groups, tiled=True)  6.64 us
    ppermute x8, waiting for transfers between devices, flip(): lax.ppermute(array, 'all', [(i, i ^ masks[i & 1]) for i in range(OWNERS)])  2.85 us
    pallas_call x2, Pallas kernels, finish(): pl.pallas_call(finish_kernel, out_shape=(shape(FEAT, HID), shape(TABLES *...  2.48 us
  transfers between devices with their start and end apart: 15, of which 11 were waited for; matrix products, arithmetic and copies ran while one was open for 1% of the time, Pallas kernels for 17%

profile of v8, /device:TPU:1, one launch (start us, length us, event | category | flops | bytes accessed | tf_op | source)
XLA Modules:
  0.0 89.3 jit_solution(5061923740440368925)
XLA Ops:
  0.6 5.1 %shard_map.94 = (bf16[16,2,16,1024]{3,2,1,0:T(8,128)(2,1)S(1)}, bf16[16,2,16,1024]{3,2,1,0:T(8,128)(2,1)S(1)}, bf16[512,2048]{1,0:T(8,128)(2,1)S(1)}, bf16[512,2...) custom-call(s32[1]{0:T(128)} %bitcast.core_ref, bf16[512,512]{1,0:T(8,128)(2,1)} %x_hbm.1, s32[4,512]{1,0:T(4,128)} %bitcast.17, ...), custom_call_target="tpu_custom_call" | custom-call | flops 3000000000 | bytes 8388608 | tf_op jit(solution)/shard_map/pallas_call | solution.py:55
  5.7 3.3 %collective-permute-start.1 = (bf16[16,2,16,1024]{3,2,1,0:T(8,128)(2,1)S(1)}, bf16[16,2,16,1024]{3,2,1,0:T(8,128)(2,1)S(1)}, u32[]{:S(2)}, u32[]{:S(2)}) collective-permute-start(bf16[16,2,16,1024]{3,2,1,0:T(8,128)(2,1)S(1)} %get-tuple-element.44), channel_id=1, source_target_pairs={{0,1},{1,0},{2,3},{3,2},{4,5},{5,4},{6,7},{7,6},{8,9},{9,8},{10,11... | collective-permute-start | bytes 3145736 | tf_op jit(solution)/shard_map/ppermute | solution.py:369
  9.0 2.0 %shard_map.95 = (bf16[16,2,16,256]{3,2,1,0:T(8,128)(2,1)S(1)}, bf16[16,2,16,256]{3,2,1,0:T(8,128)(2,1)S(1)}, bf16[512,512]{1,0:T(8,128)(2,1)S(1)}) custom-call(s32[1]{0:T(128)} %bitcast.core_ref, bf16[512,2048]{1,0:T(8,128)(2,1)S(1)} %get-tuple-element.38.pre_ref, bf16[512,2048]{1,0:T(8,128)(2,1)S(1)} %get-tuple-element.39.wh_ref, ...), custom_call_target="tpu_custom_call" | custom-call | flops 2000000000 | bytes 6291456 | tf_op jit(solution)/shard_map/pallas_call | solution.py:55
  11.0 0.1 collective-permute-start
  11.1 0.2 collective-permute-done.1.b_ref
  11.3 1.0 %shard_map.96.refs_0_ = bf16[16,2,16,1280]{3,2,1,0:T(8,128)(2,1)} custom-call(bf16[16,2,16,1024]{3,2,1,0:T(8,128)(2,1)S(1)} %get-tuple-element.43.a_ref, bf16[16,2,16,1024]{3,2,1,0:T(8,128)(2,1)S(1)} %collective-permute-done.1.b_ref), custom_call_target="tpu_custom_call" | custom-call | bytes 2097152 | tf_op jit(solution)/shard_map/pallas_call | solution.py:192
  12.4 0.3 collective-permute-done.b_ref
  12.7 0.7 shard_map.97
  13.4 0.0 copy-start.1
  13.4 8.4 %all-to-all-start = ((bf16[32,16,1280]{2,1,0:T(8,128)(2,1)}), bf16[32,16,1280]{2,1,0:T(8,128)(2,1)S(1)}, u32[]{:S(2)}, u32[]{:S(2)}) async-start(bf16[32,16,1280]{2,1,0:T(8,128)(2,1)} %bitcast.19), calls=%async_computation | async-start | bytes 2621440 | tf_op jit(solution)/shard_map/all_to_all | solution.py:372
  21.8 0.0 copy-done.1
  21.8 3.9 %shard_map.99 = (bf16[1040,128]{1,0:T(8,128)(2,1)S(1)}, bf16[1040,128]{1,0:T(8,128)(2,1)S(1)}) custom-call(s32[1]{0:T(128)} %bitcast.core_ref, s32[4,512]{1,0:T(4,128)S(1)} %bitcast.18, bf16[512,512]{1,0:T(8,128)(2,1)S(1)} %get-tuple-element.45.grad_ref), custom_call_target="tpu_custom_call" | custom-call | flops 6000000000 | bytes 8388608 | tf_op jit(solution)/shard_map/pallas_call | solution.py:55
  25.7 0.5 collective-permute-start.5
  26.2 0.1 stack.29.place_ref
  26.3 1.1 %collective-permute-done.5.far_cold_ref = bf16[1040,128]{1,0:T(8,128)(2,1)S(1)} collective-permute-done((bf16[1040,128]{1,0:T(8,128)(2,1)S(1)}, bf16[1040,128]{1,0:T(8,128)(2,1)S(1)}, u32[]{:S(2)}, u32[]{:S(2)}) %collective-permute-start.5) | collective-permute-done | bytes 266272 | tf_op jit(solution)/shard_map/ppermute | solution.py:369
  27.4 0.8 shard_map.100
  28.1 4.5 %collective-permute-start.6 = (bf16[17,4,16,128]{3,2,1,0:T(8,128)(2,1)S(1)}, bf16[17,4,16,128]{3,2,1,0:T(8,128)(2,1)S(1)}, u32[]{:S(2)}, u32[]{:S(2)}) collective-permute-start(bf16[17,4,16,128]{3,2,1,0:T(8,128)(2,1)S(1)} %get-tuple-element.49), channel_id=1, source_target_pairs={{0,14},{1,15},{2,4},{3,5},{4,2},{5,3},{6,8},{7,9},{8,6},{9,7},{10,... | collective-permute-start | bytes 835592 | tf_op jit(solution)/shard_map/ppermute | solution.py:380
  32.7 0.7 pad_add_fusion.at_ref
  33.3 1.4 %shard_map.102.accum_ref = f32[16,256]{1,0:T(8,128)S(1)} custom-call(s32[2]{0:T(128)} %pad_add_fusion.at_ref, f32[2048,128]{1,0:T(8,128)} %bitcast.20, f32[2048,128]{1,0:T(8,128)} %bitcast.21), custom_call_target="tpu_custom_call" | custom-call | tf_op jit(solution)/shard_map/pallas_call | solution.py:245
  34.7 4.7 %collective-permute-done.6.far_ref = bf16[17,4,16,128]{3,2,1,0:T(8,128)(2,1)S(1)} collective-permute-done((bf16[17,4,16,128]{3,2,1,0:T(8,128)(2,1)S(1)}, bf16[17,4,16,128]{3,2,1,0:T(8,128)(2,1)S(1)}, u32[]{:S(2)}, u32[]{:S(2)}) %collective-permute-start.6) | collective-permute-done | bytes 278560 | tf_op jit(solution)/shard_map/ppermute | solution.py:380
  39.4 1.4 %shard_map.101 = bf16[16,9,16,128]{3,2,1,0:T(8,128)(2,1)} custom-call(s32[5]{0:T(128)S(1)} %stack.29.place_ref, bf16[17,4,16,128]{3,2,1,0:T(8,128)(2,1)S(1)} %get-tuple-element.48.keep_ref, bf16[17,4,16,128]{3,2,1,0:T(8,128)(2,1)S(1)} %collective-permute-done.6.far_ref), custom_call_target="tpu_custom_call" | custom-call | bytes 2097152 | tf_op jit(solution)/shard_map/pallas_call | solution.py:55
  40.8 0.0 all-to-all-done.in_ref
  40.8 3.8 %all-to-all-start.1 = ((bf16[16,9,16,128]{3,2,1,0:T(8,128)(2,1)}), bf16[16,9,16,128]{3,2,1,0:T(8,128)(2,1)S(1)}, u32[]{:S(2)}, u32[]{:S(2)}) async-start(bf16[16,9,16,128]{3,2,1,0:T(8,128)(2,1)} %shard_map.101), calls=%async_computation.1 | async-start | bytes 1179648 | tf_op jit(solution)/shard_map/all_to_all | solution.py:372
  44.6 0.2 shard_map.98.a_ref
  44.8 3.3 %collective-permute-start.2 = (bf16[16,1280]{1,0:T(8,128)(2,1)S(1)}, bf16[16,1280]{1,0:T(8,128)(2,1)S(1)}, u32[]{:S(2)}, u32[]{:S(2)}) collective-permute-start(bf16[16,1280]{1,0:T(8,128)(2,1)S(1)} %shard_map.98.a_ref), channel_id=1, source_target_pairs={{0,8},{1,13},{2,10},{3,15},{4,12},{5,9},{6,14},{7,11},{8,0},{9,5},... | collective-permute-start | bytes 122888 | tf_op jit(solution)/shard_map/ppermute | solution.py:369
  48.1 1.5 %collective-permute-start.3 = (bf16[16,1280]{1,0:T(8,128)(2,1)S(1)}, bf16[16,1280]{1,0:T(8,128)(2,1)S(1)}, u32[]{:S(2)}, u32[]{:S(2)}) collective-permute-start(bf16[16,1280]{1,0:T(8,128)(2,1)S(1)} %shard_map.98.a_ref), channel_id=1, source_target_pairs={{0,4},{1,9},{2,6},{3,11},{4,0},{5,13},{6,2},{7,15},{8,12},{9,1},{1... | collective-permute-start | bytes 122888 | tf_op jit(solution)/shard_map/ppermute | solution.py:369
  49.6 1.0 %collective-permute-start.4 = (bf16[16,1280]{1,0:T(8,128)(2,1)S(1)}, bf16[16,1280]{1,0:T(8,128)(2,1)S(1)}, u32[]{:S(2)}, u32[]{:S(2)}) collective-permute-start(bf16[16,1280]{1,0:T(8,128)(2,1)S(1)} %shard_map.98.a_ref), channel_id=1, source_target_pairs={{0,12},{1,5},{2,14},{3,7},{4,8},{5,1},{6,10},{7,3},{8,4},{9,13},{1... | collective-permute-start | bytes 122888 | tf_op jit(solution)/shard_map/ppermute | solution.py:369
  50.5 5.0 %all-to-all-done.1.in_ref = bf16[16,9,16,128]{3,2,1,0:T(8,128)(2,1)S(1)} async-done(((bf16[16,9,16,128]{3,2,1,0:T(8,128)(2,1)}), bf16[16,9,16,128]{3,2,1,0:T(8,128)(2,1)S(1)}, u32[]{:S(2)}, u32[]{:S(2)}) %all-to-all-start.1) | async-done | bytes 589856 | tf_op jit(solution)/shard_map/all_to_all | solution.py:372
  55.5 1.6 %shard_map.103 = (bf16[256,128]{1,0:T(8,128)(2,1)S(1)}, bf16[256,128]{1,0:T(8,128)(2,1)S(1)}, bf16[256,128]{1,0:T(8,128)(2,1)S(1)}, bf16[256,128]{1,0:T(8,128)(2,1)S(1)}) custom-call(s32[5]{0:T(128)S(1)} %stack.29.place_ref, bf16[16,9,16,128]{3,2,1,0:T(8,128)(2,1)S(1)} %all-to-all-done.1.in_ref), custom_call_target="tpu_custom_call" | custom-call | flops 1000000000 | bytes 2097152 | tf_op jit(solution)/shard_map/pallas_call | solution.py:55
  57.1 0.0 collective-permute-done.2.b_ref
  57.1 0.0 collective-permute-done.3.c_ref
  57.1 0.0 collective-permute-done.4.d_ref
  57.2 1.5 %collective-permute-start.7 = (bf16[16,1280]{1,0:T(8,128)(2,1)S(1)}, bf16[16,1280]{1,0:T(8,128)(2,1)S(1)}, u32[]{:S(2)}, u32[]{:S(2)}) collective-permute-start(bf16[16,1280]{1,0:T(8,128)(2,1)S(1)} %shard_map.104.in_ref), channel_id=1, source_target_pairs={{0,2},{1,3},{2,0},{3,1},{4,6},{5,7},{6,4},{7,5},{8,10},{9,11},{10,... | collective-permute-start | bytes 122888 | tf_op jit(solution)/shard_map/ppermute | solution.py:369
  58.7 0.9 shard_map.105.refs_0_
  59.5 0.6 collective-permute-done.7.in_ref
  60.1 0.9 shard_map.106
  61.0 7.3 %all-to-all-start.2 = ((bf16[16,2,16,1280]{3,2,1,0:T(8,128)(2,1)}), bf16[16,2,16,1280]{3,2,1,0:T(8,128)(2,1)S(1)}, u32[]{:S(2)}, u32[]{:S(2)}) async-start(bf16[16,2,16,1280]{3,2,1,0:T(8,128)(2,1)} %shard_map.106), calls=%async_computation.2 | async-start | bytes 2621440 | tf_op jit(solution)/shard_map/all_to_all | solution.py:372
  68.3 0.0 copy-start
  68.3 1.4 %collective-permute-start.10 = (bf16[256,128]{1,0:T(8,128)(2,1)S(1)}, bf16[256,128]{1,0:T(8,128)(2,1)S(1)}, u32[]{:S(2)}, u32[]{:S(2)}) collective-permute-start(bf16[256,128]{1,0:T(8,128)(2,1)S(1)} %get-tuple-element.63), channel_id=1, source_target_pairs={{0,4},{1,13},{2,14},{3,7},{4,0},{5,9},{6,10},{7,3},{8,12},{9,5},{1... | collective-permute-start | bytes 196616 | tf_op jit(solution)/shard_map/ppermute | solution.py:380
  69.7 1.6 %collective-permute-start.8 = (bf16[256,128]{1,0:T(8,128)(2,1)S(1)}, bf16[256,128]{1,0:T(8,128)(2,1)S(1)}, u32[]{:S(2)}, u32[]{:S(2)}) collective-permute-start(bf16[256,128]{1,0:T(8,128)(2,1)S(1)} %get-tuple-element.61), channel_id=1, source_target_pairs={{0,8},{1,5},{2,10},{3,15},{4,12},{5,1},{6,14},{7,11},{8,0},{9,13},... | collective-permute-start | bytes 196616 | tf_op jit(solution)/shard_map/ppermute | solution.py:380
  71.3 2.7 %collective-permute-start.9 = (bf16[256,128]{1,0:T(8,128)(2,1)S(1)}, bf16[256,128]{1,0:T(8,128)(2,1)S(1)}, u32[]{:S(2)}, u32[]{:S(2)}) collective-permute-start(bf16[256,128]{1,0:T(8,128)(2,1)S(1)} %get-tuple-element.62), channel_id=1, source_target_pairs={{0,12},{1,9},{2,6},{3,11},{4,8},{5,13},{6,2},{7,15},{8,4},{9,1},{1... | collective-permute-start | bytes 196616 | tf_op jit(solution)/shard_map/ppermute | solution.py:380
  74.1 0.3 collective-permute-done.10.d_ref
  74.3 0.2 collective-permute-done.8.b_ref
  74.6 4.2 %collective-permute-done.9.c_ref = bf16[256,128]{1,0:T(8,128)(2,1)S(1)} collective-permute-done((bf16[256,128]{1,0:T(8,128)(2,1)S(1)}, bf16[256,128]{1,0:T(8,128)(2,1)S(1)}, u32[]{:S(2)}, u32[]{:S(2)}) %collective-permute-start.9) | collective-permute-done | bytes 65568 | tf_op jit(solution)/shard_map/ppermute | solution.py:380
  78.7 1.6 %all-to-all-done.2.in_ref = bf16[16,2,16,1280]{3,2,1,0:T(8,128)(2,1)S(1)} async-done(((bf16[16,2,16,1280]{3,2,1,0:T(8,128)(2,1)}), bf16[16,2,16,1280]{3,2,1,0:T(8,128)(2,1)S(1)}, u32[]{:S(2)}, u32[]{:S(2)}) %all-to-all-start.2) | async-done | bytes 1310752 | tf_op jit(solution)/shard_map/all_to_all | solution.py:372
  80.4 5.0 %collective-permute-start.11 = (bf16[16,2,16,1280]{3,2,1,0:T(8,128)(2,1)S(1)}, bf16[16,2,16,1280]{3,2,1,0:T(8,128)(2,1)S(1)}, u32[]{:S(2)}, u32[]{:S(2)}) collective-permute-start(bf16[16,2,16,1280]{3,2,1,0:T(8,128)(2,1)S(1)} %all-to-all-done.2.in_ref), channel_id=1, source_target_pairs={{0,1},{1,0},{2,3},{3,2},{4,5},{5,4},{6,7},{7,6},{8,9},{9,8},{10,11... | collective-permute-start | bytes 3932168 | tf_op jit(solution)/shard_map/ppermute | solution.py:369
  85.4 1.2 %shard_map.107 = (bf16[512,2048]{1,0:T(8,128)(2,1)}, f32[2048,128]{1,0:T(8,128)}) custom-call(s32[1]{0:T(128)} %bitcast.core_ref, bf16[16,2,16,1280]{3,2,1,0:T(8,128)(2,1)S(1)} %all-to-all-done.2.in_ref), custom_call_target="tpu_custom_call" | custom-call | bytes 4194304 | tf_op jit(solution)/shard_map/pallas_call | solution.py:338
  86.6 0.0 copy-done
  86.6 0.7 shard_map.109
  87.4 0.7 collective-permute-done.11.in_ref
  88.1 1.2 %shard_map.108 = (bf16[512,2048]{1,0:T(8,128)(2,1)}, f32[2048,128]{1,0:T(8,128)}) custom-call(s32[1]{0:T(128)S(6)} %sub.16.core_ref, bf16[16,2,16,1280]{3,2,1,0:T(8,128)(2,1)S(1)} %collective-permute-done.11.in_ref, bf16[512,2048]{1,0:T(8,128)(2,1)} %get-tuple-element.65.refs_0_, ...), custom_call_target="tpu_custom_call", output_to_operand_aliasing={{0}: (2, {}), {1}: (3, {})} | custom-call | bytes 4194304 | tf_op jit(solution)/shard_map/pallas_call | solution.py:338
  (1 shorter events, 0.0 us)
Async XLA Ops:
  5.7 5.6 %collective-permute-start.1 = (bf16[16,2,16,1024]{3,2,1,0:T(8,128)(2,1)S(1)}, bf16[16,2,16,1024]{3,2,1,0:T(8,128)(2,1)S(1)}, u32[]{:S(2)}, u32[]{:S(2)}) collective-permute-start(bf16[16,2,16,1024]{3,2,1,0:T(8,128)(2,1)S(1)} %get-tuple-element.44), channel_id=1, source_target_pairs={{0,1},{1,0},{2,3},{3,2},{4,5},{5,4},{6,7},{7,6},{8,9},{9,8},{10,11... | collective-permute-start | bytes 3145736 | tf_op jit(solution)/shard_map/ppermute | solution.py:369
  11.0 1.6 %collective-permute-start = (bf16[16,2,16,256]{3,2,1,0:T(8,128)(2,1)S(1)}, bf16[16,2,16,256]{3,2,1,0:T(8,128)(2,1)S(1)}, u32[]{:S(2)}, u32[]{:S(2)}) collective-permute-start(bf16[16,2,16,256]{3,2,1,0:T(8,128)(2,1)S(1)} %get-tuple-element.42), channel_id=1, source_target_pairs={{0,1},{1,0},{2,3},{3,2},{4,5},{5,4},{6,7},{7,6},{8,9},{9,8},{10,11... | collective-permute-start | bytes 786440 | tf_op jit(solution)/shard_map/ppermute | solution.py:369
  13.4 8.4 %copy-start.1 = (s32[512,4]{0,1:T(4,128)S(1)}, s32[512,4]{0,1:T(4,128)}, u32[]{:S(2)}) copy-start(s32[512,4]{0,1:T(4,128)} %param.8) | copy-start | bytes 24580
  13.4 27.4 %all-to-all-start = ((bf16[32,16,1280]{2,1,0:T(8,128)(2,1)}), bf16[32,16,1280]{2,1,0:T(8,128)(2,1)S(1)}, u32[]{:S(2)}, u32[]{:S(2)}) async-start(bf16[32,16,1280]{2,1,0:T(8,128)(2,1)} %bitcast.19), calls=%async_computation | async-start | bytes 2621440 | tf_op jit(solution)/shard_map/all_to_all | solution.py:372
  25.7 1.7 %collective-permute-start.5 = (bf16[1040,128]{1,0:T(8,128)(2,1)S(1)}, bf16[1040,128]{1,0:T(8,128)(2,1)S(1)}, u32[]{:S(2)}, u32[]{:S(2)}) collective-permute-start(bf16[1040,128]{1,0:T(8,128)(2,1)S(1)} %get-tuple-element.47), channel_id=1, source_target_pairs={{0,1},{1,0},{2,3},{3,2},{4,5},{5,4},{6,7},{7,6},{8,9},{9,8},{10,11... | collective-permute-start | bytes 798728 | tf_op jit(solution)/shard_map/ppermute | solution.py:369
  28.1 11.3 %collective-permute-start.6 = (bf16[17,4,16,128]{3,2,1,0:T(8,128)(2,1)S(1)}, bf16[17,4,16,128]{3,2,1,0:T(8,128)(2,1)S(1)}, u32[]{:S(2)}, u32[]{:S(2)}) collective-permute-start(bf16[17,4,16,128]{3,2,1,0:T(8,128)(2,1)S(1)} %get-tuple-element.49), channel_id=1, source_target_pairs={{0,14},{1,15},{2,4},{3,5},{4,2},{5,3},{6,8},{7,9},{8,6},{9,7},{10,... | collective-permute-start | bytes 835592 | tf_op jit(solution)/shard_map/ppermute | solution.py:380
  40.8 14.7 %all-to-all-start.1 = ((bf16[16,9,16,128]{3,2,1,0:T(8,128)(2,1)}), bf16[16,9,16,128]{3,2,1,0:T(8,128)(2,1)S(1)}, u32[]{:S(2)}, u32[]{:S(2)}) async-start(bf16[16,9,16,128]{3,2,1,0:T(8,128)(2,1)} %shard_map.101), calls=%async_computation.1 | async-start | bytes 1179648 | tf_op jit(solution)/shard_map/all_to_all | solution.py:372
  44.8 12.3 %collective-permute-start.2 = (bf16[16,1280]{1,0:T(8,128)(2,1)S(1)}, bf16[16,1280]{1,0:T(8,128)(2,1)S(1)}, u32[]{:S(2)}, u32[]{:S(2)}) collective-permute-start(bf16[16,1280]{1,0:T(8,128)(2,1)S(1)} %shard_map.98.a_ref), channel_id=1, source_target_pairs={{0,8},{1,13},{2,10},{3,15},{4,12},{5,9},{6,14},{7,11},{8,0},{9,5},... | collective-permute-start | bytes 122888 | tf_op jit(solution)/shard_map/ppermute | solution.py:369
  48.1 9.0 %collective-permute-start.3 = (bf16[16,1280]{1,0:T(8,128)(2,1)S(1)}, bf16[16,1280]{1,0:T(8,128)(2,1)S(1)}, u32[]{:S(2)}, u32[]{:S(2)}) collective-permute-start(bf16[16,1280]{1,0:T(8,128)(2,1)S(1)} %shard_map.98.a_ref), channel_id=1, source_target_pairs={{0,4},{1,9},{2,6},{3,11},{4,0},{5,13},{6,2},{7,15},{8,12},{9,1},{1... | collective-permute-start | bytes 122888 | tf_op jit(solution)/shard_map/ppermute | solution.py:369
  49.6 7.6 %collective-permute-start.4 = (bf16[16,1280]{1,0:T(8,128)(2,1)S(1)}, bf16[16,1280]{1,0:T(8,128)(2,1)S(1)}, u32[]{:S(2)}, u32[]{:S(2)}) collective-permute-start(bf16[16,1280]{1,0:T(8,128)(2,1)S(1)} %shard_map.98.a_ref), channel_id=1, source_target_pairs={{0,12},{1,5},{2,14},{3,7},{4,8},{5,1},{6,10},{7,3},{8,4},{9,13},{1... | collective-permute-start | bytes 122888 | tf_op jit(solution)/shard_map/ppermute | solution.py:369
  57.2 2.9 %collective-permute-start.7 = (bf16[16,1280]{1,0:T(8,128)(2,1)S(1)}, bf16[16,1280]{1,0:T(8,128)(2,1)S(1)}, u32[]{:S(2)}, u32[]{:S(2)}) collective-permute-start(bf16[16,1280]{1,0:T(8,128)(2,1)S(1)} %shard_map.104.in_ref), channel_id=1, source_target_pairs={{0,2},{1,3},{2,0},{3,1},{4,6},{5,7},{6,4},{7,5},{8,10},{9,11},{10,... | collective-permute-start | bytes 122888 | tf_op jit(solution)/shard_map/ppermute | solution.py:369
  61.0 19.4 %all-to-all-start.2 = ((bf16[16,2,16,1280]{3,2,1,0:T(8,128)(2,1)}), bf16[16,2,16,1280]{3,2,1,0:T(8,128)(2,1)S(1)}, u32[]{:S(2)}, u32[]{:S(2)}) async-start(bf16[16,2,16,1280]{3,2,1,0:T(8,128)(2,1)} %shard_map.106), calls=%async_computation.2 | async-start | bytes 2621440 | tf_op jit(solution)/shard_map/all_to_all | solution.py:372
  68.3 18.3 %copy-start = (f32[4,64,128]{2,1,0:T(8,128)S(1)}, f32[4,64,128]{2,1,0:T(8,128)}, u32[]{:S(2)}) copy-start(f32[4,64,128]{2,1,0:T(8,128)} %param.13) | copy-start | bytes 393220
  68.3 6.0 %collective-permute-start.10 = (bf16[256,128]{1,0:T(8,128)(2,1)S(1)}, bf16[256,128]{1,0:T(8,128)(2,1)S(1)}, u32[]{:S(2)}, u32[]{:S(2)}) collective-permute-start(bf16[256,128]{1,0:T(8,128)(2,1)S(1)} %get-tuple-element.63), channel_id=1, source_target_pairs={{0,4},{1,13},{2,14},{3,7},{4,0},{5,9},{6,10},{7,3},{8,12},{9,5},{1... | collective-permute-start | bytes 196616 | tf_op jit(solution)/shard_map/ppermute | solution.py:380
  69.7 4.8 %collective-permute-start.8 = (bf16[256,128]{1,0:T(8,128)(2,1)S(1)}, bf16[256,128]{1,0:T(8,128)(2,1)S(1)}, u32[]{:S(2)}, u32[]{:S(2)}) collective-permute-start(bf16[256,128]{1,0:T(8,128)(2,1)S(1)} %get-tuple-element.61), channel_id=1, source_target_pairs={{0,8},{1,5},{2,10},{3,15},{4,12},{5,1},{6,14},{7,11},{8,0},{9,13},... | collective-permute-start | bytes 196616 | tf_op jit(solution)/shard_map/ppermute | solution.py:380
  71.3 7.4 %collective-permute-start.9 = (bf16[256,128]{1,0:T(8,128)(2,1)S(1)}, bf16[256,128]{1,0:T(8,128)(2,1)S(1)}, u32[]{:S(2)}, u32[]{:S(2)}) collective-permute-start(bf16[256,128]{1,0:T(8,128)(2,1)S(1)} %get-tuple-element.62), channel_id=1, source_target_pairs={{0,12},{1,9},{2,6},{3,11},{4,8},{5,13},{6,2},{7,15},{8,4},{9,1},{1... | collective-permute-start | bytes 196616 | tf_op jit(solution)/shard_map/ppermute | solution.py:380
  80.4 7.7 %collective-permute-start.11 = (bf16[16,2,16,1280]{3,2,1,0:T(8,128)(2,1)S(1)}, bf16[16,2,16,1280]{3,2,1,0:T(8,128)(2,1)S(1)}, u32[]{:S(2)}, u32[]{:S(2)}) collective-permute-start(bf16[16,2,16,1280]{3,2,1,0:T(8,128)(2,1)S(1)} %all-to-all-done.2.in_ref), channel_id=1, source_target_pairs={{0,1},{1,0},{2,3},{3,2},{4,5},{5,4},{6,7},{7,6},{8,9},{9,8},{10,11... | collective-permute-start | bytes 3932168 | tf_op jit(solution)/shard_map/ppermute | solution.py:369
